TPU v7x, 32 devices: a whole 2x2x4 slice. The times are simulated.
32 devices in a mesh: dp: 4 (over z), mp: 8 (over y, x, core).
Axes of the slice: x: 2, y: 2, z: 4, core: 2. Of those that a mesh axis runs over, the one named last changes fastest.
Arguments:
- layer_input: bfloat16 [8192, 2048], P(('dp', 'mp')), may hold values from -6 to 6
- cotangent: bfloat16 [8192, 2048], P(('dp', 'mp')), may hold values from -6 to 6
- norm_in: float32 [2048], P(('dp', 'mp')), may hold values from 0.5 to 1.5
- norm_mid: float32 [2048], P(('dp', 'mp')), may hold values from 0.5 to 1.5
- w_rnn_in: float32 [2048, 2560], P('dp', 'mp'), may hold values from -0.125 to 0.125
- w_rnn_gate: float32 [2048, 2560], P('dp', 'mp'), may hold values from -0.125 to 0.125
- w_rnn_out: float32 [2560, 2048], P('mp', 'dp'), may hold values from -0.3125 to 0.3125
- gate_in_blocks: float32 [16, 160, 160], P('mp', 'dp'), may hold values from -0.5 to 0.5
- gate_a_blocks: float32 [16, 160, 160], P('mp', 'dp'), may hold values from -0.5 to 0.5
- channel_params: float32 [8, 2560], P('dp', 'mp')
- w_mlp_gate: float32 [2048, 6144], P('dp', 'mp'), may hold values from -0.125 to 0.125
- w_mlp_up: float32 [2048, 6144], P('dp', 'mp'), may hold values from -0.125 to 0.125
- w_mlp_down: float32 [6144, 2048], P('mp', 'dp'), may hold values from -0.15625 to 0.15625
- lengths: int32 [4, 3], P('dp'), may hold values from 1 to 2046, as said below
Outputs:
- layer_output: bfloat16 [8192, 2048], P(('dp', 'mp'))
- grad_input: float32 [8192, 2048], P(('dp', 'mp'))
- grad_norm_in: float32 [2048], P(('dp', 'mp'))
- grad_norm_mid: float32 [2048], P(('dp', 'mp'))
- grad_rnn_in: float32 [2048, 2560], P('dp', 'mp')
- grad_rnn_gate: float32 [2048, 2560], P('dp', 'mp')
- grad_rnn_out: float32 [2560, 2048], P('mp', 'dp')
- grad_gate_in: float32 [16, 160, 160], P('mp', 'dp')
- grad_gate_a: float32 [16, 160, 160], P('mp', 'dp')
- grad_channel: float32 [8, 2560], P('dp', 'mp')
- grad_mlp_gate: float32 [2048, 6144], P('dp', 'mp')
- grad_mlp_up: float32 [2048, 6144], P('dp', 'mp')
- grad_mlp_down: float32 [6144, 2048], P('mp', 'dp')
Inputs may be any that keep to these rules, and one draw needn't show every extreme that they name: The lengths of each pack sum to at most 2048, exactly that in some pack of every draw; the positions after them are padding.
All inputs are finite; a program needn't handle non-finite values.
Results may differ from a plain program's by a relative error of at most 0.019.
Values may be sent and summed in bfloat16 or wider, within the bound.
A program may use at most 320 MiB of HBM per device.

v0:
```python
import jax
import jax.numpy as jnp
from jax import lax
from jax.sharding import PartitionSpec as P

CONV = 4
BLOCK = 64


EPS = 1e-06
DECAY = 8.0


def product(left, right):
    return jnp.dot(left, right, preferred_element_type=jnp.float32)


def product_nt(left, right):
    return lax.dot_general(
        left, right, (((1,), (1,)), ((), ())), preferred_element_type=jnp.float32
    )


def product_tn(left, right):
    return lax.dot_general(
        left, right, (((0,), (0,)), ((), ())), preferred_element_type=jnp.float32
    )


def exact_einsum(form, left, right):
    return jnp.einsum(
        form, left, right, precision=lax.Precision.HIGHEST, preferred_element_type=jnp.float32
    )


def layout(lens, group_len):
    places = jnp.arange(group_len, dtype=jnp.int32)
    finish = jnp.cumsum(lens)
    bounds = jnp.concatenate([finish - lens, finish[-1:]])
    resets = jnp.any(places[:, None] == bounds[None, :], axis=1)
    begins = jnp.max(jnp.where(bounds[None, :] <= places[:, None], bounds[None, :], 0), axis=1)
    living = places < finish[-1]
    return (places, resets, begins, living)


def shifted(values, offset):
    if offset == 0:
        return values
    return jnp.pad(values[: values.shape[0] - offset], ((offset, 0), (0, 0)))


def lifted(values, offset):
    if offset == 0:
        return values
    return jnp.pad(values[offset:], ((0, offset), (0, 0)))


def block_scan(log_coeffs, inputs, keeps):
    length = inputs.shape[0]
    width = inputs.shape[1]
    span_len = min(BLOCK, length)
    blocks_count = length // span_len
    lower_tri = jnp.arange(span_len)[:, None] >= jnp.arange(span_len)[None, :]

    def advance(carry, block):
        logs, values, kept = block
        totals = jnp.cumsum(logs, axis=0)
        breaks = jnp.cumsum(1 - kept.astype(jnp.int32))
        linked = lower_tri & (breaks[:, None] == breaks[None, :])
        gaps = jnp.where(linked[:, :, None], totals[:, None, :] - totals[None, :, :], -jnp.inf)
        result = exact_einsum("tsw,sw->tw", jnp.exp(gaps), values)
        result = result + jnp.where((breaks == 0)[:, None], jnp.exp(totals), 0.0) * carry
        return (result[-1], result)

    initial = jnp.zeros((width,), jnp.float32)
    final, states = lax.scan(
        advance,
        initial,
        (
            log_coeffs.reshape(blocks_count, span_len, width),
            inputs.reshape(blocks_count, span_len, width),
            keeps.reshape(blocks_count, span_len),
        ),
    )
    return states.reshape(length, width)


def channel_forward(values, channel, blocks_in, blocks_a, places, resets, begins):
    group_len, width = values.shape
    convolved = jnp.zeros_like(values) + channel[CONV]
    for offset in range(CONV):
        valid = (places - offset >= begins)[:, None]
        convolved = convolved + jnp.where(valid, shifted(values, offset) * channel[offset], 0.0)
    blocked = convolved.reshape(group_len, blocks_in.shape[0], blocks_in.shape[1])
    gate_in = jax.nn.sigmoid(
        exact_einsum("gnb,nbc->gnc", blocked, blocks_in).reshape(group_len, width)
        + channel[CONV + 1]
    )
    gate_a = jax.nn.sigmoid(
        exact_einsum("gnb,nbc->gnc", blocked, blocks_a).reshape(group_len, width)
        + channel[CONV + 2]
    )
    softened = jax.nn.softplus(-channel[CONV + 3])
    log_decay = -DECAY * gate_a * softened
    decays = jnp.exp(log_decay)
    root_term = jnp.sqrt(1.0 - decays * decays)
    drives = gate_in * convolved * root_term
    states = block_scan(log_decay, drives, jnp.logical_not(resets))
    return (convolved, blocked, gate_in, gate_a, softened, log_decay, decays, root_term, states)


def channel_backward(d_states, values, channel, blocks_in, blocks_a, places, resets, begins, saved):
    convolved, blocked, gate_in, gate_a, softened, log_decay, decays, root_term, states = saved
    group_len, width = values.shape
    keeps = jnp.logical_not(resets)
    next_logs = jnp.concatenate([log_decay[1:], jnp.zeros((1, width), jnp.float32)], axis=0)
    next_keeps = jnp.concatenate([keeps[1:], jnp.zeros((1,), bool)], axis=0)
    adjoint = jnp.flip(
        block_scan(jnp.flip(next_logs, 0), jnp.flip(d_states, 0), jnp.flip(next_keeps, 0)), 0
    )
    previous = shifted(states, 1) * keeps[:, None].astype(jnp.float32)
    d_decay = adjoint * previous - adjoint * gate_in * convolved * decays / root_term
    d_log = d_decay * decays
    d_gate_a = d_log * (-DECAY * softened)
    d_lambda = DECAY * jax.nn.sigmoid(-channel[CONV + 3]) * jnp.sum(d_log * gate_a, axis=0)
    d_gate_in = adjoint * convolved * root_term
    d_conv = adjoint * gate_in * root_term
    d_logit_in = d_gate_in * gate_in * (1.0 - gate_in)
    d_logit_a = d_gate_a * gate_a * (1.0 - gate_a)
    block_count = blocks_in.shape[0]
    block_width = blocks_in.shape[1]
    blocked_in = d_logit_in.reshape(group_len, block_count, block_width)
    blocked_a = d_logit_a.reshape(group_len, block_count, block_width)
    d_conv = d_conv + exact_einsum("gnc,nbc->gnb", blocked_in, blocks_in).reshape(group_len, width)
    d_conv = d_conv + exact_einsum("gnc,nbc->gnb", blocked_a, blocks_a).reshape(group_len, width)
    grad_blocks_in = exact_einsum("gnb,gnc->nbc", blocked, blocked_in)
    grad_blocks_a = exact_einsum("gnb,gnc->nbc", blocked, blocked_a)
    d_values = jnp.zeros_like(values)
    tap_grads = []
    for offset in range(CONV):
        valid = (places - offset >= begins)[:, None]
        masked = jnp.where(valid, d_conv, 0.0)
        d_values = d_values + lifted(masked, offset) * channel[offset]
        tap_grads.append(jnp.sum(masked * shifted(values, offset), axis=0))
    tail_rows = [
        jnp.sum(d_conv, axis=0),
        jnp.sum(d_logit_in, axis=0),
        jnp.sum(d_logit_a, axis=0),
        d_lambda,
    ]
    grad_channel = jnp.stack(tap_grads + tail_rows, axis=0)
    return (d_values, grad_blocks_in, grad_blocks_a, grad_channel)


def on_device(
    layer_input,
    cotangent,
    norm_in,
    norm_mid,
    w_rnn_in,
    w_rnn_gate,
    w_rnn_out,
    gate_in_blocks,
    gate_a_blocks,
    channel_params,
    w_mlp_gate,
    w_mlp_up,
    w_mlp_down,
    lengths,
):
    half = jnp.bfloat16
    single = jnp.float32
    tokens_here = layer_input.shape[0]
    group_len = tokens_here * lax.axis_size("mp")
    mp_index = lax.axis_index("mp")
    rnn_set = (
        lax.all_gather(w_rnn_in.astype(half), "mp", axis=1, tiled=True),
        lax.all_gather(w_rnn_gate.astype(half), "mp", axis=1, tiled=True),
        lax.all_gather(w_rnn_out.astype(half), "mp", axis=0, tiled=True),
        lax.all_gather(norm_in.astype(half), "mp", axis=0, tiled=True),
        lax.all_gather(norm_mid.astype(half), "mp", axis=0, tiled=True),
    )
    shard_set = (
        lax.all_gather(w_mlp_gate.astype(half), "dp", axis=0, tiled=True),
        lax.all_gather(w_mlp_up.astype(half), "dp", axis=0, tiled=True),
        lax.all_gather(w_mlp_down.astype(half), "dp", axis=1, tiled=True),
        lax.all_gather(gate_in_blocks.astype(half), "dp", axis=1, tiled=True),
        lax.all_gather(gate_a_blocks.astype(half), "dp", axis=1, tiled=True),
        lax.all_gather(channel_params.astype(half), "dp", axis=0, tiled=True),
        lax.all_gather(rnn_set[0], "dp", axis=0, tiled=True),
        lax.all_gather(rnn_set[1], "dp", axis=0, tiled=True),
        lax.all_gather(rnn_set[2], "dp", axis=1, tiled=True),
        lax.all_gather(rnn_set[3], "dp", axis=0, tiled=True),
        lax.all_gather(rnn_set[4], "dp", axis=0, tiled=True),
    )
    gate_cols, up_cols, down_part = (shard_set[0], shard_set[1], shard_set[2])
    blocks_in = shard_set[3].astype(single)
    blocks_a = shard_set[4].astype(single)
    channel = shard_set[5].astype(single)
    in_proj, gate_proj, out_proj = (shard_set[6], shard_set[7], shard_set[8])
    gain_first = shard_set[9].astype(single)
    gain_second = shard_set[10].astype(single)
    places, resets, begins, living = layout(lengths[0], group_len)
    alive_here = lax.dynamic_slice_in_dim(living, mp_index * tokens_here, tokens_here).astype(
        single
    )[:, None]
    inputs = layer_input.astype(single)
    scale_first = lax.rsqrt(jnp.mean(inputs * inputs, axis=-1, keepdims=True) + EPS)
    normed = (inputs * scale_first * gain_first).astype(half)
    branch_pre = product(normed, in_proj).astype(half)
    side_gate, side_back = jax.vjp(jax.nn.gelu, product(normed, gate_proj))
    channels_in = lax.all_to_all(branch_pre, "mp", split_axis=1, concat_axis=0, tiled=True)
    channel_values = channels_in.astype(single)
    saved = channel_forward(channel_values, channel, blocks_in, blocks_a, places, resets, begins)
    returned = lax.all_to_all(saved[8].astype(half), "mp", split_axis=0, concat_axis=1, tiled=True)
    returned_f = returned.astype(single)
    branch_out = (side_gate * returned_f * alive_here).astype(half)
    residual = inputs + product(branch_out, out_proj)
    scale_second = lax.rsqrt(jnp.mean(residual * residual, axis=-1, keepdims=True) + EPS)
    normed_mid = (residual * scale_second * gain_second).astype(half)
    rows_all = lax.all_gather(normed_mid, "mp", axis=0, tiled=True)
    gate_pre = product(rows_all, gate_cols)
    up_pre = product(rows_all, up_cols)
    activated, act_back = jax.vjp(jax.nn.gelu, gate_pre)
    hidden = (activated * up_pre).astype(half)
    mlp_out = lax.psum_scatter(
        product(hidden, down_part).astype(jnp.bfloat16), "mp", scatter_dimension=0, tiled=True
    ).astype(jnp.float32)
    cot_all = lax.all_gather(cotangent, "mp", axis=0, tiled=True)
    d_hidden = product_nt(cot_all, down_part)
    d_gate = act_back(d_hidden * up_pre)[0].astype(half)
    d_up = (d_hidden * activated).astype(half)
    d_normed_mid = lax.psum_scatter(
        product_nt(d_gate, gate_cols) + product_nt(d_up, up_cols),
        "mp",
        scatter_dimension=0,
        tiled=True,
    )
    grad_gate = product_tn(rows_all, d_gate)
    grad_up = product_tn(rows_all, d_up)
    grad_down = product_tn(hidden, cot_all)
    layer_output = (residual + mlp_out).astype(half)
    weighted_second = gain_second * d_normed_mid
    grad_gain_second = jnp.sum(d_normed_mid * residual * scale_second, axis=0)
    cube_second = scale_second * scale_second * scale_second
    d_residual = (
        cotangent.astype(single)
        + scale_second * weighted_second
        - residual * cube_second * jnp.mean(weighted_second * residual, axis=-1, keepdims=True)
    )
    d_resid_low = d_residual.astype(half)
    d_branch_out = product_nt(d_resid_low, out_proj)
    grad_out = product_tn(branch_out, d_resid_low)
    d_side = d_branch_out * returned_f * alive_here
    d_returned = (d_branch_out * side_gate * alive_here).astype(half)
    d_side_pre = side_back(d_side)[0].astype(half)
    d_states = lax.all_to_all(d_returned, "mp", split_axis=1, concat_axis=0, tiled=True)
    d_values, grad_blocks_in, grad_blocks_a, grad_channel = channel_backward(
        d_states.astype(single),
        channel_values,
        channel,
        blocks_in,
        blocks_a,
        places,
        resets,
        begins,
        saved,
    )
    d_branch = lax.all_to_all(d_values.astype(half), "mp", split_axis=0, concat_axis=1, tiled=True)
    d_normed = product_nt(d_branch, in_proj) + product_nt(d_side_pre, gate_proj)
    grad_in = product_tn(normed, d_branch)
    grad_side = product_tn(normed, d_side_pre)
    weighted_first = gain_first * d_normed
    grad_gain_first = jnp.sum(d_normed * inputs * scale_first, axis=0)
    cube_first = scale_first * scale_first * scale_first
    grad_input = (
        d_residual
        + scale_first * weighted_first
        - inputs * cube_first * jnp.mean(weighted_first * inputs, axis=-1, keepdims=True)
    )
    shard_grads = (
        lax.psum_scatter(
            grad_gate.astype(jnp.bfloat16), "dp", scatter_dimension=0, tiled=True
        ).astype(jnp.float32),
        lax.psum_scatter(
            grad_up.astype(jnp.bfloat16), "dp", scatter_dimension=0, tiled=True
        ).astype(jnp.float32),
        lax.psum_scatter(
            grad_down.astype(jnp.bfloat16), "dp", scatter_dimension=1, tiled=True
        ).astype(jnp.float32),
        lax.psum_scatter(
            grad_blocks_in.astype(jnp.bfloat16), "dp", scatter_dimension=1, tiled=True
        ).astype(jnp.float32),
        lax.psum_scatter(
            grad_blocks_a.astype(jnp.bfloat16), "dp", scatter_dimension=1, tiled=True
        ).astype(jnp.float32),
        lax.psum_scatter(
            grad_channel.astype(jnp.bfloat16), "dp", scatter_dimension=0, tiled=True
        ).astype(jnp.float32),
        lax.psum_scatter(
            grad_in.astype(jnp.bfloat16), "dp", scatter_dimension=0, tiled=True
        ).astype(jnp.float32),
        lax.psum_scatter(
            grad_side.astype(jnp.bfloat16), "dp", scatter_dimension=0, tiled=True
        ).astype(jnp.float32),
        lax.psum_scatter(
            grad_out.astype(jnp.bfloat16), "dp", scatter_dimension=1, tiled=True
        ).astype(jnp.float32),
        lax.psum_scatter(
            grad_gain_first.astype(jnp.bfloat16), "dp", scatter_dimension=0, tiled=True
        ).astype(jnp.float32),
        lax.psum_scatter(
            grad_gain_second.astype(jnp.bfloat16), "dp", scatter_dimension=0, tiled=True
        ).astype(jnp.float32),
    )
    rnn_grads = (
        lax.psum_scatter(
            shard_grads[6].astype(jnp.bfloat16), "mp", scatter_dimension=1, tiled=True
        ).astype(jnp.float32),
        lax.psum_scatter(
            shard_grads[7].astype(jnp.bfloat16), "mp", scatter_dimension=1, tiled=True
        ).astype(jnp.float32),
        lax.psum_scatter(
            shard_grads[8].astype(jnp.bfloat16), "mp", scatter_dimension=0, tiled=True
        ).astype(jnp.float32),
        lax.psum_scatter(
            shard_grads[9].astype(jnp.bfloat16), "mp", scatter_dimension=0, tiled=True
        ).astype(jnp.float32),
        lax.psum_scatter(
            shard_grads[10].astype(jnp.bfloat16), "mp", scatter_dimension=0, tiled=True
        ).astype(jnp.float32),
    )
    return (
        layer_output,
        grad_input,
        rnn_grads[3],
        rnn_grads[4],
        rnn_grads[0],
        rnn_grads[1],
        rnn_grads[2],
        shard_grads[3],
        shard_grads[4],
        shard_grads[5],
        shard_grads[0],
        shard_grads[1],
        shard_grads[2],
    )


def solution(mesh):
    return jax.shard_map(
        on_device,
        mesh=mesh,
        in_specs=(
            P(("dp", "mp"), None),
            P(("dp", "mp"), None),
            P(("dp", "mp")),
            P(("dp", "mp")),
            P("dp", "mp"),
            P("dp", "mp"),
            P("mp", "dp"),
            P("mp", "dp", None),
            P("mp", "dp", None),
            P("dp", "mp"),
            P("dp", "mp"),
            P("dp", "mp"),
            P("mp", "dp"),
            P("dp", None),
        ),
        out_specs=(
            P(("dp", "mp"), None),
            P(("dp", "mp"), None),
            P(("dp", "mp")),
            P(("dp", "mp")),
            P("dp", "mp"),
            P("dp", "mp"),
            P("mp", "dp"),
            P("mp", "dp", None),
            P("mp", "dp", None),
            P("dp", "mp"),
            P("dp", "mp"),
            P("dp", "mp"),
            P("mp", "dp"),
        ),
        check_vma=False,
    )
```

profile of v0, /device:TPU:0, one launch (start us, length us, event | category | flops | bytes accessed | tf_op | source)
XLA Modules:
  0.0 2149.9 jit_solution(9971873090308239379)
XLA Ops:
  12.0 31.3 %all-gather.19.cloned.1.call-done = bf16[512,2560]{0,1:T(8,128)(2,1)} async-done(((bf16[512,320]{0,1:T(8,128)(2,1)}), bf16[512,2560]{0,1:T(8,128)(2,1)}) %all-gather.19.cloned.1.call-update) | async-done | bytes 2621456 | tf_op jit(solution)/shard_map/all_gather | solution.py:177
  43.4 32.5 %all-gather.15.cloned.1.call-done = bf16[512,2560]{0,1:T(8,128)(2,1)} async-done(((bf16[512,320]{0,1:T(8,128)(2,1)}), bf16[512,2560]{0,1:T(8,128)(2,1)}) %all-gather.15.cloned.1.call-update) | async-done | bytes 2621456 | tf_op jit(solution)/shard_map/all_gather | solution.py:178
  76.0 32.5 %all-gather.23.cloned.1.call-done = bf16[2560,512]{1,0:T(8,128)(2,1)} async-done(((bf16[320,512]{1,0:T(8,128)(2,1)}), bf16[2560,512]{1,0:T(8,128)(2,1)}) %all-gather.23.cloned.1.call-update) | async-done | bytes 2621456 | tf_op jit(solution)/shard_map/all_gather | solution.py:179
  111.5 13.1 all-reduce.18
  124.6 16.0 all-gather
  141.5 12.1 all-gather.1
  154.4 139.7 %all-gather.21.cloned.1.call-done = bf16[2048,2560]{0,1:T(8,128)(2,1)} async-done(((bf16[512,2560]{0,1:T(8,128)(2,1)}), bf16[2048,2560]{0,1:T(8,128)(2,1)}) %all-gather.21.cloned.1.call-update) | async-done | bytes 10485776 | tf_op jit(solution)/shard_map/all_gather | solution.py:190
  294.1 6.9 convolution_convert_fusion.4
  307.7 18.3 all_gather.61
  325.9 17.4 all_gather.62
  369.7 110.4 %while.26 = (s32[]{:T(128)}, f32[320]{0:T(512)S(1)}, f32[32,64,320]{2,1,0:T(8,128)S(1)}, f32[32,64,320]{2,1,0:T(8,128)}, pred[32,64]{1,0:T(8,128)(4,1)S(1)}, /*i...) while((s32[]{:T(128)}, f32[320]{0:T(512)S(1)}, f32[32,64,320]{2,1,0:T(8,128)S(1)}, ...), condition=%wide.region_7.8_spmd.clone, body=%wide.region_4.7_spmd.clone.sunk | while | flops 6590594 | bytes 1146357 | solution.py:76
  487.8 12.4 all-gather.2
  510.9 10.3 multiply_convert_fusion.3
  521.3 145.3 %all-gather.25.cloned.1.call-done = bf16[2560,2048]{1,0:T(8,128)(2,1)} async-done(((bf16[2560,512]{1,0:T(8,128)(2,1)}), bf16[2560,2048]{1,0:T(8,128)(2,1)}) %all-gather.25.cloned.1.call-update) | async-done | bytes 10485776 | tf_op jit(solution)/shard_map/all_gather | solution.py:192
  679.8 50.7 %all-gather.29.cloned.1.call-done = bf16[2048,768]{1,0:T(8,128)(2,1)} async-done(((bf16[512,768]{1,0:T(8,128)(2,1)}), bf16[2048,768]{1,0:T(8,128)(2,1)}) %all-gather.29.cloned.1.call-update) | async-done | bytes 3145744 | tf_op jit(solution)/shard_map/all_gather | solution.py:184
  730.4 55.5 %all-gather.27.cloned.1.call-done = bf16[2048,2048]{1,0:T(8,128)(2,1)} async-done(((bf16[256,2048]{1,0:T(8,128)(2,1)}), bf16[2048,2048]{1,0:T(8,128)(2,1)}) %all-gather.27.cloned.1.call-update) | async-done | bytes 8388624 | tf_op jit(solution)/shard_map/all_gather | solution.py:221
  786.0 11.7 fusion.57
  797.7 54.0 %all-gather.31.cloned.1.call-done = bf16[2048,768]{1,0:T(8,128)(2,1)} async-done(((bf16[512,768]{1,0:T(8,128)(2,1)}), bf16[2048,768]{1,0:T(8,128)(2,1)}) %all-gather.31.cloned.1.call-update) | async-done | bytes 3145744 | tf_op jit(solution)/shard_map/all_gather | solution.py:185
  851.7 11.7 fusion.58
  863.3 52.5 %all-gather.33.cloned.1.call-done = bf16[768,2048]{1,0:T(8,128)(2,1)} async-done(((bf16[768,512]{1,0:T(8,128)(2,1)}), bf16[768,2048]{1,0:T(8,128)(2,1)}) %all-gather.33.cloned.1.call-update) | async-done | bytes 3145744 | tf_op jit(solution)/shard_map/all_gather | solution.py:186
  915.8 55.0 %all-gather.35.cloned.1.call-done = bf16[2048,2048]{1,0:T(8,128)(2,1)} async-done(((bf16[256,2048]{1,0:T(8,128)(2,1)}), bf16[2048,2048]{1,0:T(8,128)(2,1)}) %all-gather.35.cloned.1.call-update) | async-done | bytes 8388624 | tf_op jit(solution)/shard_map/all_gather | solution.py:229
  970.8 18.5 multiply_convert_fusion
  989.4 13.6 fusion.59
  1003.0 13.6 convolution_add_fusion
  1016.7 11.5 convolution_convert_fusion.3
  1028.7 104.1 %reduce-scatter.20.cloned.1.call-done = f32[256,2048]{1,0:T(8,128)} async-done(((f32[2048,2048]{1,0:T(8,128)}), f32[256,2048]{1,0:T(8,128)}) %reduce-scatter.20.cloned.1.call-update) | async-done | bytes 2097168 | tf_op jit(solution)/shard_map/reduce_scatter | solution.py:233
  1135.5 72.0 %reduce-scatter.18.cloned.1.call-done = bf16[256,2048]{1,0:T(8,128)(2,1)} async-done(((bf16[2048,2048]{1,0:T(8,128)(2,1)}), bf16[256,2048]{1,0:T(8,128)(2,1)}) %reduce-scatter.18.cloned.1.call-update) | async-done | bytes 1048592 | tf_op jit(solution)/shard_map/reduce_scatter | solution.py:226
  1211.5 11.4 fusion.23
  1238.8 17.5 rev.16
  1262.4 8.9 convolution_convert_fusion
  1273.3 17.6 rev.14
  1294.7 110.5 %while.27 = (s32[]{:T(128)}, f32[320]{0:T(512)S(1)}, f32[32,64,320]{2,1,0:T(8,128)S(1)}, f32[32,64,320]{2,1,0:T(8,128)}, pred[32,64]{1,0:T(8,128)(4,1)S(1)}, /*i...) while((s32[]{:T(128)}, f32[320]{0:T(512)S(1)}, f32[32,64,320]{2,1,0:T(8,128)S(1)}, ...), condition=%wide.region_15.16_spmd.clone, body=%wide.region_12.15_spmd.clone.sunk | while | flops 6590594 | bytes 1146357 | solution.py:76
  1407.4 25.6 %rev.17 = f32[2048,320]{0,1:T(8,128)} reverse(f32[2048,320]{0,1:T(8,128)} %copy.102), dimensions={0} | reverse | bytes 5242880 | tf_op jit(solution)/shard_map/jit(_flip)/rev | solution.py:118
  1454.1 22.2 %all_to_all.55 = bf16[8,256,320]{1,2,0:T(8,128)(2,1)S(1)} all-to-all(bf16[8,256,320]{1,2,0:T(8,128)(2,1)S(1)} %bitcast.211), channel_id=1, replica_groups=mesh['dp'=4,'mp'=8] {'mp'}, dimensions={0} | all-to-all | bytes 2621440 | tf_op jit(solution)/shard_map/all_to_all | solution.py:269
  1483.3 11.8 convolution_convert_fusion.7
  1495.2 11.4 convolution_convert_fusion.6
  1506.6 12.2 convolution_convert_fusion.5
  1531.8 57.6 %reduce-scatter.26.cloned.1.call-done = bf16[2560,512]{1,0:T(8,128)(2,1)} async-done(((bf16[2560,2048]{1,0:T(8,128)(2,1)}), bf16[2560,512]{1,0:T(8,128)(2,1)}) %reduce-scatter.26.cloned.1.call-update) | async-done | bytes 2621456 | tf_op jit(solution)/shard_map/reduce_scatter | solution.py:306
  1589.4 181.4 %reduce-scatter.22.cloned.1.call-done = bf16[512,2560]{1,0:T(8,128)(2,1)} async-done(((bf16[2048,2560]{1,0:T(8,128)(2,1)}), bf16[512,2560]{1,0:T(8,128)(2,1)}) %reduce-scatter.22.cloned.1.call-update) | async-done | bytes 2621456 | tf_op jit(solution)/shard_map/reduce_scatter | solution.py:300
  1779.2 55.2 %reduce-scatter.30.cloned.1.call-done = bf16[512,768]{1,0:T(8,128)(2,1)} async-done(((bf16[2048,768]{1,0:T(8,128)(2,1)}), bf16[512,768]{1,0:T(8,128)(2,1)}) %reduce-scatter.30.cloned.1.call-update) | async-done | bytes 786448 | tf_op jit(solution)/shard_map/reduce_scatter | solution.py:282
  1836.8 60.2 %reduce-scatter.32.cloned.1.call-done = bf16[512,768]{1,0:T(8,128)(2,1)} async-done(((bf16[2048,768]{1,0:T(8,128)(2,1)}), bf16[512,768]{1,0:T(8,128)(2,1)}) %reduce-scatter.32.cloned.1.call-update) | async-done | bytes 786448 | tf_op jit(solution)/shard_map/reduce_scatter | solution.py:285
  1899.3 60.3 %reduce-scatter.34.cloned.1.call-done = bf16[768,512]{1,0:T(8,128)(2,1)} async-done(((bf16[768,2048]{1,0:T(8,128)(2,1)}), bf16[768,512]{1,0:T(8,128)(2,1)}) %reduce-scatter.34.cloned.1.call-update) | async-done | bytes 786448 | tf_op jit(solution)/shard_map/reduce_scatter | solution.py:288
  1963.2 35.8 %all-reduce.23.cloned.1.call-done = (bf16[2,160,160]{2,1,0:T(8,128)(2,1)}, bf16[2,160,160]{2,1,0:T(8,128)(2,1)}) async-done(((bf16[2,160,160]{2,1,0:T(8,128)(2,1)}, bf16[2,160,160]{2,1,0:T(8,128)(2,1)}), (bf16[2,160,160]{2,1,0:T(8,128)(2,1)}, bf16[2,160,160]{2,1,0:T(8,128)(2,1)})) %all-reduce.23.cloned.1.call-update) | async-done | bytes 204816
  2006.7 9.5 fusion.39
  2016.2 17.2 all-reduce.19
  2033.5 12.0 all-reduce.17
  2052.3 41.2 %reduce-scatter.28.cloned.1.call-done = bf16[320,512]{1,0:T(8,128)(2,1)} async-done(((bf16[2560,512]{1,0:T(8,128)(2,1)}), bf16[320,512]{1,0:T(8,128)(2,1)}) %reduce-scatter.28.cloned.1.call-update) | async-done | bytes 327696 | tf_op jit(solution)/shard_map/reduce_scatter | solution.py:323
  2095.4 45.5 %reduce-scatter.36.cloned.1.call-done = bf16[320,512]{1,0:T(8,128)(2,1)} async-done(((bf16[2560,512]{1,0:T(8,128)(2,1)}), bf16[320,512]{1,0:T(8,128)(2,1)}) %reduce-scatter.36.cloned.1.call-update) | async-done | bytes 327696
  (1014 shorter events, 401.2 us)
Async XLA Ops:
  7.2 36.1 %all-gather.19.cloned.1.call-start = ((), (), s32[]{:S(2)}) async-start(), calls=%async_computation.17 | async-start | bytes 2949120 | tf_op jit(solution)/shard_map/all_gather | solution.py:177
  9.2 66.8 %all-gather.15.cloned.1.call-start = ((), (), s32[]{:S(2)}) async-start(), calls=%async_computation.15 | async-start | bytes 2949120 | tf_op jit(solution)/shard_map/all_gather | solution.py:178
  11.1 97.5 %all-gather.23.cloned.1.call-start = ((), (), s32[]{:S(2)}) async-start(), calls=%async_computation.19 | async-start | bytes 2949120 | tf_op jit(solution)/shard_map/all_gather | solution.py:179
  11.9 282.2 %all-gather.21.cloned.1.call-start = ((), (), s32[]{:S(2)}) async-start(), calls=%async_computation.18 | async-start | bytes 13107200 | tf_op jit(solution)/shard_map/all_gather | solution.py:190
  43.4 467.6 %all-gather.17.cloned.1.call-start = ((), (), s32[]{:S(2)}) async-start(), calls=%async_computation.16 | async-start | bytes 13107200 | tf_op jit(solution)/shard_map/all_gather | solution.py:191
  75.9 32.7 %copy-start.24 = (f32[512,768]{1,0:T(8,128)S(1)}, f32[512,768]{1,0:T(8,128)}, u32[]{:S(2)}) copy-start(f32[512,768]{1,0:T(8,128)} %param.28) | copy-start | bytes 4718596
  76.0 590.6 %all-gather.25.cloned.1.call-start = ((), (), s32[]{:S(2)}) async-start(), calls=%async_computation.20 | async-start | bytes 13107200 | tf_op jit(solution)/shard_map/all_gather | solution.py:192
  108.6 32.0 %copy-start.15 = (bf16[256,2048]{1,0:T(8,128)(2,1)S(1)}, bf16[256,2048]{1,0:T(8,128)(2,1)}, u32[]{:S(2)}) copy-start(bf16[256,2048]{1,0:T(8,128)(2,1)} %param.18) | copy-start | bytes 3145732
  108.6 32.9 %copy-start.60 = (f32[2,320]{1,0:T(2,128)S(1)}, f32[2,320]{1,0:T(2,128)}, u32[]{:S(2)}) copy-start(f32[2,320]{1,0:T(2,128)} %param.27) | copy-start | bytes 7684
  108.6 45.0 %copy-start.66 = (s32[1,3]{1,0:T(1,128)S(1)}, s32[1,3]{1,0:T(1,128)}, u32[]{:S(2)}) copy-start(s32[1,3]{1,0:T(1,128)} %param.31) | copy-start | bytes 40
  108.6 45.8 %copy-start.32 = (f32[2,40,160]{2,1,0:T(8,128)S(1)}, f32[2,40,160]{2,1,0:T(8,128)}, u32[]{:S(2)}) copy-start(f32[2,40,160]{2,1,0:T(8,128)} %param.25) | copy-start | bytes 153604
  108.6 45.8 %copy-start.33 = (f32[2,40,160]{2,1,0:T(8,128)S(1)}, f32[2,40,160]{2,1,0:T(8,128)}, u32[]{:S(2)}) copy-start(f32[2,40,160]{2,1,0:T(8,128)} %param.26) | copy-start | bytes 153604
  108.6 621.8 %all-gather.29.cloned.1.call-start = ((), (), s32[]{:S(2)}) async-start(), calls=%async_computation.22 | async-start | bytes 3932160 | tf_op jit(solution)/shard_map/all_gather | solution.py:184
  153.6 189.8 %copy-start.34 = (f32[8,320]{1,0:T(8,128)}, f32[8,320]{1,0:T(8,128)S(1)}, u32[]{:S(2)}) copy-start(f32[8,320]{1,0:T(8,128)S(1)} %reshape.355) | copy-start | bytes 30724
  302.5 41.1 %all-to-all-start = ((bf16[256,8,320]{0,2,1:T(8,128)(2,1)}), bf16[256,8,320]{0,2,1:T(8,128)(2,1)S(1)}, u32[]{:S(2)}, u32[]{:S(2)}) async-start(bf16[256,8,320]{0,2,1:T(8,128)(2,1)} %bitcast.11), calls=%async_computation | async-start | bytes 2621440 | tf_op jit(solution)/shard_map/all_to_all | solution.py:212
  307.6 18.4 copy-start.40
  325.9 21.0 copy-start.25
  343.6 23.2 %copy-start.38 = (f32[320]{0:T(512)}, f32[320]{0:T(512)S(1)}, u32[]{:S(2)}) copy-start(f32[320]{0:T(512)S(1)} %get-tuple-element.201) | copy-start | bytes 3844
  484.2 21.7 %all-to-all-start.1 = ((bf16[8,256,320]{1,2,0:T(8,128)(2,1)}), bf16[8,256,320]{1,2,0:T(8,128)(2,1)S(1)}, u32[]{:S(2)}, u32[]{:S(2)}) async-start(bf16[8,256,320]{1,2,0:T(8,128)(2,1)} %copy.96), calls=%async_computation.1 | async-start | bytes 2621440 | tf_op jit(solution)/shard_map/all_to_all | solution.py:215
  487.8 298.2 %all-gather.27.cloned.1.call-start = ((), (), s32[]{:S(2)}) async-start(), calls=%async_computation.21 | async-start | bytes 9437184 | tf_op jit(solution)/shard_map/all_gather | solution.py:221
  673.9 177.7 %all-gather.31.cloned.1.call-start = ((), (), s32[]{:S(2)}) async-start(), calls=%async_computation.23 | async-start | bytes 3932160 | tf_op jit(solution)/shard_map/all_gather | solution.py:185
  676.5 239.3 %all-gather.33.cloned.1.call-start = ((), (), s32[]{:S(2)}) async-start(), calls=%async_computation.24 | async-start | bytes 3932160 | tf_op jit(solution)/shard_map/all_gather | solution.py:186
  679.0 291.8 %all-gather.35.cloned.1.call-start = ((), (), s32[]{:S(2)}) async-start(), calls=%async_computation.26 | async-start | bytes 9437184 | tf_op jit(solution)/shard_map/all_gather | solution.py:229
  679.7 453.0 %reduce-scatter.20.cloned.1.call-start = ((), (), s32[]{:S(2)}) async-start(), calls=%async_computation.27 | async-start | bytes 18874368 | tf_op jit(solution)/shard_map/reduce_scatter | solution.py:233
  970.8 18.5 copy-start.62
  989.3 13.6 copy-start.68
  989.3 13.6 copy-start.63
  1016.6 190.9 %reduce-scatter.18.cloned.1.call-start = ((), (), s32[]{:S(2)}) async-start(), calls=%async_computation.25 | async-start | bytes 9437184 | tf_op jit(solution)/shard_map/reduce_scatter | solution.py:226
  1028.3 499.1 %reduce-scatter.24.cloned.1.call-start = ((), (), s32[]{:S(2)}) async-start(), calls=%async_computation.29 | async-start | bytes 13107200 | tf_op jit(solution)/shard_map/reduce_scatter | solution.py:303
  1211.5 11.4 copy-start.19
  1233.1 38.2 %all-to-all-start.2 = ((bf16[256,8,320]{0,2,1:T(8,128)(2,1)}), bf16[256,8,320]{0,2,1:T(8,128)(2,1)}, u32[]{:S(2)}, u32[]{:S(2)}) async-start(bf16[256,8,320]{0,2,1:T(8,128)(2,1)} %bitcast.210), calls=%async_computation.4 | async-start | bytes 2621440 | tf_op jit(solution)/shard_map/all_to_all | solution.py:257
  1237.4 351.9 %reduce-scatter.26.cloned.1.call-start = ((), (), s32[]{:S(2)}) async-start(), calls=%async_computation.30 | async-start | bytes 13107200 | tf_op jit(solution)/shard_map/reduce_scatter | solution.py:306
  1271.3 499.5 %reduce-scatter.22.cloned.1.call-start = ((), (), s32[]{:S(2)}) async-start(), calls=%async_computation.28 | async-start | bytes 13107200 | tf_op jit(solution)/shard_map/reduce_scatter | solution.py:300
  1407.4 25.6 %copy-start.3 = (f32[2048,320]{0,1:T(8,128)S(1)}, f32[2048,320]{0,1:T(8,128)}, u32[]{:S(2)}) copy-start(f32[2048,320]{0,1:T(8,128)} %copy-done.2) | copy-start | bytes 7864324
  1407.4 25.6 %copy-start.35 = (f32[2048]{0:T(1024)S(1)}, f32[2048]{0:T(1024)}, u32[]{:S(2)}) copy-start(f32[2048]{0:T(1024)} %get-tuple-element.278) | copy-start | bytes 24580
  1407.4 25.6 %copy-start.37 = (f32[320]{0:T(512)S(1)}, f32[320]{0:T(512)}, u32[]{:S(2)}) copy-start(f32[320]{0:T(512)} %copy-done.36) | copy-start | bytes 3844
  1454.0 23.4 %copy-start.17 = (bf16[256,2048]{1,0:T(8,128)(2,1)S(1)}, bf16[256,2048]{1,0:T(8,128)(2,1)}, u32[]{:S(2)}) copy-start(bf16[256,2048]{1,0:T(8,128)(2,1)} %param.18) | copy-start | bytes 3145732
  1483.3 351.1 %reduce-scatter.30.cloned.1.call-start = ((), (), s32[]{:S(2)}) async-start(), calls=%async_computation.32 | async-start | bytes 3932160 | tf_op jit(solution)/shard_map/reduce_scatter | solution.py:282
  1495.1 401.8 %reduce-scatter.32.cloned.1.call-start = ((), (), s32[]{:S(2)}) async-start(), calls=%async_computation.33 | async-start | bytes 3932160 | tf_op jit(solution)/shard_map/reduce_scatter | solution.py:285
  1506.6 453.1 %reduce-scatter.34.cloned.1.call-start = ((), (), s32[]{:S(2)}) async-start(), calls=%async_computation.34 | async-start | bytes 3932160 | tf_op jit(solution)/shard_map/reduce_scatter | solution.py:288
  1518.8 480.2 %all-reduce.23.cloned.1.call-start = ((), (), s32[]{:S(2)}) async-start(), calls=%async_computation.37 | async-start | bytes 655360
  1527.3 522.8 %reduce-scatter.38.cloned.1.call-start = ((), (), s32[]{:S(2)}) async-start(), calls=%async_computation.36 | async-start | bytes 2949120
  1531.8 561.8 %reduce-scatter.28.cloned.1.call-start = ((), (), s32[]{:S(2)}) async-start(), calls=%async_computation.31 | async-start | bytes 2949120 | tf_op jit(solution)/shard_map/reduce_scatter | solution.py:323
  1589.4 551.6 %reduce-scatter.36.cloned.1.call-start = ((), (), s32[]{:S(2)}) async-start(), calls=%async_computation.35 | async-start | bytes 2949120
  1836.8 125.4 %copy-start.10 = (f32[2048,320]{0,1:T(8,128)S(1)}, f32[2048,320]{0,1:T(8,128)}, u32[]{:S(2)}) copy-start(f32[2048,320]{0,1:T(8,128)} %copy-done.8) | copy-start | bytes 7864324
  2006.6 9.5 copy-start.58
  2006.7 40.0 %copy-start.20 = (f32[256,2048]{1,0:T(8,128)S(1)}, f32[256,2048]{1,0:T(8,128)}, u32[]{:S(2)}) copy-start(f32[256,2048]{1,0:T(8,128)} %copy-done.19) | copy-start | bytes 6291460
  2006.7 40.0 %copy-start.59 = (f32[256]{0:T(256)S(1)}, f32[256]{0:T(256)}, u32[]{:S(2)}) copy-start(f32[256]{0:T(256)} %get-tuple-element.280) | copy-start | bytes 3076
  (47 other events, 113.5 us)
Sparse Core Ops, SparseCore 0:
  10.5 32.8 all-gather.18
  45.8 30.1 all-gather.14
  78.4 30.1 all-gather.22
  110.0 184.1 all-gather.20
  295.5 187.3 all-gather.16
  484.3 182.1 all-gather.24
  668.7 61.6 all-gather.28
  732.9 53.0 all-gather.26
  788.1 63.4 all-gather.30
  853.6 62.0 all-gather.32
  917.7 53.0 all-gather.34
  1016.8 115.9 reduce-scatter.19
  1136.2 71.2 reduce-scatter.17
  1229.9 177.9 reduce-scatter.23
  1410.3 179.0 reduce-scatter.25
  1591.7 179.0 reduce-scatter.21
  1773.1 61.2 reduce-scatter.29
  1836.6 60.2 reduce-scatter.31
  1899.4 60.2 reduce-scatter.33
  1962.6 36.3 all-reduce.22
  2002.7 43.4 reduce-scatter.37
  2049.9 43.6 reduce-scatter.27
  2097.2 43.6 reduce-scatter.35
where the time goes:
time: 2160 us; the launch traced here: 2150 us
  waiting for transfers between devices  1370 us (63%)
  other arithmetic  214 us (10%)
  matrix products  201 us (9%)
  local copies, waits for them, and re-layouts  190 us (9%)
  blocking collectives  141 us (7%)
    reduce_scatter x1, waiting for transfers between devices, on_device(): lax.psum_scatter(grad_in.astype(jnp.bfloat16), 'dp', scatter_dimension=0,...  181 us
    all_gather x1, waiting for transfers between devices, on_device(): lax.all_gather(rnn_set[2], 'dp', axis=1, tiled=True)  145 us
    all_gather x1, waiting for transfers between devices, on_device(): lax.all_gather(rnn_set[0], 'dp', axis=0, tiled=True)  140 us
    dot_general x64, other arithmetic, exact_einsum(): jnp.einsum(form, left, right, precision=lax.Precision.HIGHEST, preferred_...  115 us
    reduce_scatter x1, waiting for transfers between devices, on_device(): lax.psum_scatter(product_nt(d_gate, gate_cols) + product_nt(d_up, up_cols...  104 us
    unnamed x26, waiting for transfers between devices  82.3 us
    dot_general x6, matrix products, product_nt(): lax.dot_general(left, right, (((1,), (1,)), ((), ())), preferred_element_...  72.9 us
    reduce_scatter x1, waiting for transfers between devices, on_device(): lax.psum_scatter(product(hidden, down_part).astype(jnp.bfloat16), 'mp', s...  72 us
  transfers between devices with their start and end apart: 26, of which 21 were waited for; matrix products, arithmetic and copies ran while one was open for 25% of the time, Pallas kernels for 0%

commit v1 on v0

v1 whole, which is shorter than its diff:
```python
import functools

import jax
import jax.numpy as jnp
from jax import lax
from jax.experimental import pallas as pl
from jax.experimental.pallas import tpu as pltpu
from jax.sharding import PartitionSpec as P

CONV = 4
EPS = 1e-06
DECAY = 8.0
HALF = jnp.bfloat16
SINGLE = jnp.float32
MESH = pl.DeviceIdType.MESH
VMEM_BYTES = 56 * 1024 * 1024
GELU_C = 0.7978845608028654
GELU_K = 0.044715


def dot_nn(left, right):
    return lax.dot_general(
        left, right, (((1,), (0,)), ((), ())), preferred_element_type=SINGLE
    )


def dot_nt(left, right):
    return lax.dot_general(
        left, right, (((1,), (1,)), ((), ())), preferred_element_type=SINGLE
    )


def dot_tn(left, right):
    return lax.dot_general(
        left, right, (((0,), (0,)), ((), ())), preferred_element_type=SINGLE
    )


def gelu(v):
    return 0.5 * v * (1.0 + jnp.tanh(GELU_C * (v + GELU_K * v * v * v)))


def gelu_both(v):
    square = v * v
    t = jnp.tanh(GELU_C * (v + GELU_K * v * square))
    value = 0.5 * v * (1.0 + t)
    slope = 0.5 * (1.0 + t) + 0.5 * v * (1.0 - t * t) * (GELU_C * (1.0 + 3.0 * GELU_K * square))
    return value, slope


def flip(me, mask, count):
    place = me
    bit = 1
    while bit < count:
        if mask & bit:
            place = place + (1 - 2 * ((me // bit) % 2)) * bit
        bit *= 2
    return place


def gather_plan(count):
    bits = [1 << b for b in range(count.bit_length() - 1)]
    outer = bits[1:]
    orders = (outer + bits[:1], outer[::-1] + bits[:1])
    sends = []
    for half, order in enumerate(orders):
        for stage, bit in enumerate(order):
            for pick in range(1 << stage):
                mask = sum(order[j] for j in range(stage) if pick >> j & 1)
                sends.append((bin(mask).count("1"), half, mask, bit))
    sends.sort(key=lambda s: s[0])
    return bits, [s[1:] for s in sends]


def start_barrier(masks, count):
    me = lax.axis_index("mp")
    barrier = pltpu.get_barrier_semaphore()
    for mask in masks:
        pl.semaphore_signal(
            barrier, inc=1, device_id={"mp": flip(me, mask, count)}, device_id_type=MESH
        )
    pl.semaphore_wait(barrier, len(masks))


def gather_kernel(count, x_ref, o_ref, own_sem, send, recv):
    me = lax.axis_index("mp")
    rows = x_ref.shape[0]
    bits, plan = gather_plan(count)
    own = pltpu.make_async_copy(x_ref, o_ref.at[me], own_sem)
    own.start()
    start_barrier(bits, count)
    copies = {}
    landed = set()
    for half, mask, bit in plan:
        span = pl.ds(half * (rows // 2), rows // 2)
        slot = flip(me, mask, count)
        if mask and (half, mask) not in landed:
            copies[(half, mask)].wait_recv()
            landed.add((half, mask))
        source = o_ref.at[slot, span] if mask else x_ref.at[span]
        copy = pltpu.make_async_remote_copy(
            src_ref=source,
            dst_ref=o_ref.at[slot, span],
            send_sem=send.at[half, mask | bit],
            recv_sem=recv.at[half, mask | bit],
            device_id={"mp": flip(me, bit, count)},
            device_id_type=MESH,
        )
        copy.start()
        copies[(half, mask | bit)] = copy
    for key, copy in copies.items():
        if key not in landed:
            copy.wait_recv()
    for copy in copies.values():
        copy.wait_send()
    own.wait()


def gather_rows(x, collective_id):
    count = lax.axis_size("mp")
    if count != 8:
        return lax.all_gather(x, "mp", axis=0, tiled=False)
    rows, width = x.shape
    return pl.pallas_call(
        functools.partial(gather_kernel, count),
        out_shape=jax.ShapeDtypeStruct((count, rows, width), x.dtype),
        in_specs=[pl.BlockSpec(memory_space=pl.ANY)],
        out_specs=pl.BlockSpec(memory_space=pl.ANY),
        scratch_shapes=[
            pltpu.SemaphoreType.DMA,
            pltpu.SemaphoreType.DMA((2, count)),
            pltpu.SemaphoreType.DMA((2, count)),
        ],
        compiler_params=pltpu.CompilerParams(
            collective_id=collective_id, has_side_effects=True, vmem_limit_bytes=VMEM_BYTES
        ),
        cost_estimate=pl.CostEstimate(
            flops=0, bytes_accessed=2 * count * rows * width * 2 * 4, transcendentals=0
        ),
        name="gather_rows",
    )(x)


def scatter_kernel(products, tile, *refs):
    count = 8
    pairs = len(products)
    lefts, rights = refs[:pairs], refs[pairs : 2 * pairs]
    out_ref = refs[2 * pairs]
    acc, core_out, core_in, link_out, link_in = refs[2 * pairs + 1 : 2 * pairs + 6]
    core_send, core_recv, link_send, link_recv = refs[2 * pairs + 6 :]
    rows, width = out_ref.shape
    me = lax.axis_index("mp")
    start_barrier((1, 2, 4), count)

    def partial(slot, store):
        first = pl.multiple_of(slot * rows, rows)

        def step(t, carry):
            columns = pl.ds(pl.multiple_of(t * tile, tile), tile)
            total = None
            for left, right, product in zip(lefts, rights, products):
                term = product(left[pl.ds(first, rows), :], right, t, columns)
                total = term if total is None else total + term
            store(columns, total)
            return carry

        lax.fori_loop(0, width // tile, step, 0)

    def into_core(c):
        def store(columns, total):
            core_out[c, :, columns] = total.astype(HALF)

        return store

    def into_acc(c):
        def store(columns, total):
            acc[c, :, columns] = total

        return store

    core_copies = {}
    link_copies = {}
    middle = rows // 2

    def core_half(c):
        partial(flip(me, 2 * c + 1, count), into_core(c))
        copy = pltpu.make_async_remote_copy(
            src_ref=core_out.at[c],
            dst_ref=core_in.at[c],
            send_sem=core_send.at[c],
            recv_sem=core_recv.at[c],
            device_id={"mp": flip(me, 1, count)},
            device_id_type=MESH,
        )
        copy.start()
        core_copies[c] = copy

    def core_sum(c):
        core_copies[c].wait_recv()

        def step(t, carry):
            columns = pl.ds(pl.multiple_of(t * tile, tile), tile)
            acc[c, :, columns] = acc[c, :, columns] + core_in[c, :, columns].astype(SINGLE)
            return carry

        lax.fori_loop(0, width // tile, step, 0)

    def link(index, c, half, axis):
        span = pl.ds(half * middle, middle)

        def step(t, carry):
            columns = pl.ds(pl.multiple_of(t * tile, tile), tile)
            link_out[index, :, columns] = acc[c, span, columns].astype(HALF)
            return carry

        lax.fori_loop(0, width // tile, step, 0)
        copy = pltpu.make_async_remote_copy(
            src_ref=link_out.at[index],
            dst_ref=link_in.at[index],
            send_sem=link_send.at[index],
            recv_sem=link_recv.at[index],
            device_id={"mp": flip(me, 2 * axis, count)},
            device_id_type=MESH,
        )
        copy.start()
        link_copies[index] = copy

    def link_sum(index, c, half):
        link_copies[index].wait_recv()
        span = pl.ds(half * middle, middle)

        def step(t, carry):
            columns = pl.ds(pl.multiple_of(t * tile, tile), tile)
            acc[c, span, columns] = acc[c, span, columns] + link_in[index, :, columns].astype(
                SINGLE
            )
            return carry

        lax.fori_loop(0, width // tile, step, 0)

    core_half(3)
    partial(flip(me, 6, count), into_acc(3))
    core_half(1)
    core_sum(3)
    link(0, 3, 0, 2)
    link(1, 3, 1, 1)
    partial(flip(me, 2, count), into_acc(1))
    core_half(2)
    core_sum(1)
    link(2, 1, 1, 1)
    partial(flip(me, 4, count), into_acc(2))
    core_half(0)
    core_sum(2)
    link(3, 2, 0, 2)
    partial(me, into_acc(0))
    core_sum(0)
    link_sum(0, 1, 0)
    link(4, 1, 0, 1)
    link_sum(1, 2, 1)
    link(5, 2, 1, 2)
    link_sum(2, 0, 1)
    link_sum(3, 0, 0)
    link_sum(4, 0, 0)
    link_sum(5, 0, 1)
    out_ref[...] = acc[0]
    for copy in core_copies.values():
        copy.wait_send()
    for copy in link_copies.values():
        copy.wait_send()


def scatter_products(lefts, rights, products, fallback, width, tile, collective_id, flops):
    count = lax.axis_size("mp")
    tokens = lefts[0].shape[0]
    rows = tokens // count
    if count != 8:
        return lax.psum_scatter(
            fallback().astype(HALF), "mp", scatter_dimension=0, tiled=True
        ).astype(SINGLE)
    return pl.pallas_call(
        functools.partial(scatter_kernel, products, tile),
        out_shape=jax.ShapeDtypeStruct((rows, width), SINGLE),
        in_specs=[pl.BlockSpec(memory_space=pltpu.VMEM)] * (len(lefts) + len(rights)),
        out_specs=pl.BlockSpec(memory_space=pltpu.VMEM),
        scratch_shapes=[
            pltpu.VMEM((4, rows, width), SINGLE),
            pltpu.VMEM((4, rows, width), HALF),
            pltpu.VMEM((4, rows, width), HALF),
            pltpu.VMEM((6, rows // 2, width), HALF),
            pltpu.VMEM((6, rows // 2, width), HALF),
            pltpu.SemaphoreType.DMA((4,)),
            pltpu.SemaphoreType.DMA((4,)),
            pltpu.SemaphoreType.DMA((6,)),
            pltpu.SemaphoreType.DMA((6,)),
        ],
        compiler_params=pltpu.CompilerParams(
            collective_id=collective_id, has_side_effects=True, vmem_limit_bytes=VMEM_BYTES
        ),
        cost_estimate=pl.CostEstimate(
            flops=flops, bytes_accessed=tokens * width * 2 * 8, transcendentals=0
        ),
        name="scatter_products",
    )(*lefts, *rights)


def positions(lens_ref, first, shape):
    place = lax.broadcasted_iota(jnp.int32, shape, 0) + first
    begin = jnp.zeros(shape, jnp.int32)
    total = 0
    for j in range(lens_ref.shape[1]):
        total = total + lens_ref[0, j]
        begin = jnp.where(place >= total, total, begin)
    return place - begin, place < total


def split_dot(dot, left, right):
    high = left.astype(HALF)
    low = (left - high.astype(SINGLE)).astype(HALF)
    return dot(high, right) + dot(low, right)


def lane_tiles(width):
    return [(t, t * 128, min(128, width - t * 128)) for t in range(-(-width // 128))]


def put_tiles(ref, value):
    for t, first, lanes in lane_tiles(value.shape[1]):
        ref[t, :, :lanes] = value[:, first : first + lanes]


def scan_start(tiles, lanes):
    return [(jnp.zeros((lanes, 128), SINGLE), jnp.ones((lanes, 128), SINGLE)) for _ in tiles]


def sigmoid(v):
    return 1.0 / (1.0 + jnp.exp(-v))


def forward_kernel(
    lens_ref,
    x_ref,
    gain_ref,
    pack_ref,
    bin_ref,
    ba_ref,
    chan_ref,
    n1_ref,
    bx_ref,
    by_ref,
    conv_ref,
    gi_ref,
    ra_ref,
    h_ref,
    ob_ref,
    taps,
    coef,
    drive,
    carry,
):
    step = pl.program_id(0)
    rows, width = bx_ref.shape
    depth = pack_ref.shape[2]
    lanes = 8
    span = rows // lanes

    @pl.when(step == 0)
    def _():
        taps[...] = jnp.zeros_like(taps)
        carry[...] = jnp.zeros_like(carry)
        coef[...] = jnp.zeros_like(coef)
        drive[...] = jnp.zeros_like(drive)

    x = x_ref[0].astype(SINGLE)
    scale = lax.rsqrt(jnp.mean(x * x, axis=-1, keepdims=True) + EPS)
    normed = (x * scale * gain_ref[...]).astype(HALF)
    n1_ref[...] = normed
    total = None
    for d in range(pack_ref.shape[0]):
        term = dot_nt(normed[:, d * depth : (d + 1) * depth], pack_ref[d, : 2 * width, :])
        total = term if total is None else total + term
    bx = total[:, :width].astype(HALF)
    by = total[:, width:]
    bx_ref[...] = bx
    by_ref[...] = by
    pos, live = positions(lens_ref, step * rows, (rows, width))
    taps[0:8, :] = taps[rows : rows + 8, :]
    taps[8 : rows + 8, :] = bx.astype(SINGLE)
    conv = jnp.zeros((rows, width), SINGLE) + chan_ref[CONV : CONV + 1, :]
    for k in range(CONV):
        moved = taps[8 - k : 8 - k + rows, :]
        conv = conv + jnp.where(pos >= k, moved * chan_ref[k : k + 1, :], 0.0)
    conv_ref[...] = conv
    high = conv.astype(HALF)
    low = (conv - high.astype(SINGLE)).astype(HALF)
    gate_in = sigmoid(
        dot_nn(high, bin_ref[...]) + dot_nn(low, bin_ref[...]) + chan_ref[CONV + 1 : CONV + 2, :]
    )
    gate_a = sigmoid(
        dot_nn(high, ba_ref[...]) + dot_nn(low, ba_ref[...]) + chan_ref[CONV + 2 : CONV + 3, :]
    )
    gi_ref[...] = gate_in
    ra_ref[...] = gate_a
    decay = jnp.exp(-DECAY * gate_a * chan_ref[CONV + 4 : CONV + 5, :])
    root = jnp.sqrt(1.0 - decay * decay)
    put_tiles(coef, jnp.where(pos == 0, 0.0, decay))
    put_tiles(drive, gate_in * conv * root)
    tiles = lane_tiles(width)

    def scan(i, state):
        at = pl.ds(i, lanes, stride=span)
        result = []
        for (t, _, _), (h, prod) in zip(tiles, state):
            a = coef[t, at, :]
            h = a * h + drive[t, at, :]
            prod = prod * a
            drive[t, at, :] = h
            coef[t, at, :] = prod
            result.append((h, prod))
        return result

    state = lax.fori_loop(0, span, scan, scan_start(tiles, lanes), unroll=4)
    for (t, first, used), (h, prod) in zip(tiles, state):
        running = carry[t, 0:1, :]
        for s in range(lanes):
            at = slice(s * span, (s + 1) * span)
            value = drive[t, at, :] + coef[t, at, :] * running
            h_ref[at, first : first + used] = value[:, :used]
            running = h[s : s + 1, :] + prod[s : s + 1, :] * running
        carry[t, 0:1, :] = running
    mixed = h_ref[...].astype(HALF).astype(SINGLE)
    ob_ref[...] = jnp.where(live, gelu(by) * mixed, 0.0).astype(HALF)


def forward_channels(lens, x_all, gain, pack, blocks_in, blocks_a, chan):
    count, rows, model = x_all.shape
    width = chan.shape[1]
    tokens = count * rows
    whole = lambda shape: pl.BlockSpec(shape, lambda i: (0,) * len(shape))
    part = pl.BlockSpec((rows, width), lambda i: (i, 0))
    full = lambda kind: jax.ShapeDtypeStruct((tokens, width), kind)
    return pl.pallas_call(
        forward_kernel,
        grid=(count,),
        out_shape=(
            jax.ShapeDtypeStruct((tokens, model), HALF),
            full(HALF),
            full(SINGLE),
            full(SINGLE),
            full(SINGLE),
            full(SINGLE),
            full(SINGLE),
            full(HALF),
        ),
        in_specs=[
            pl.BlockSpec(memory_space=pltpu.SMEM),
            pl.BlockSpec((1, rows, model), lambda i: (i, 0, 0)),
            whole(gain.shape),
            whole(pack.shape),
            whole(blocks_in.shape),
            whole(blocks_a.shape),
            whole(chan.shape),
        ],
        out_specs=(pl.BlockSpec((rows, model), lambda i: (i, 0)),) + (part,) * 7,
        scratch_shapes=[
            pltpu.VMEM((rows + 8, width), SINGLE),
            pltpu.VMEM((len(lane_tiles(width)), rows, 128), SINGLE),
            pltpu.VMEM((len(lane_tiles(width)), rows, 128), SINGLE),
            pltpu.VMEM((len(lane_tiles(width)), 8, 128), SINGLE),
        ],
        compiler_params=pltpu.CompilerParams(vmem_limit_bytes=VMEM_BYTES),
        cost_estimate=pl.CostEstimate(
            flops=2 * tokens * model * 2 * width,
            bytes_accessed=tokens * (model * 4 + width * 24),
            transcendentals=8 * tokens * width,
        ),
        name="forward_channels",
    )(lens, x_all, gain, pack, blocks_in, blocks_a, chan)


def backward_kernel(
    lens_ref,
    dt_ref,
    pack_ref,
    bin_ref,
    ba_ref,
    chan_ref,
    bx_ref,
    by_ref,
    conv_ref,
    gi_ref,
    ra_ref,
    h_ref,
    hprev_ref,
    dbx_ref,
    dby_ref,
    gin_ref,
    ga_ref,
    gchan_ref,
    lift,
    coef,
    drive,
    carry,
):
    step = pl.program_id(0)
    chunk = pl.num_programs(0) - 1 - step
    rows, width = bx_ref.shape
    depth = pack_ref.shape[2]
    lanes = 8
    span = rows // lanes

    @pl.when(step == 0)
    def _():
        lift[...] = jnp.zeros_like(lift)
        carry[...] = jnp.zeros_like(carry)
        coef[...] = jnp.zeros_like(coef)
        drive[...] = jnp.zeros_like(drive)
        gin_ref[...] = jnp.zeros_like(gin_ref)
        ga_ref[...] = jnp.zeros_like(ga_ref)
        gchan_ref[...] = jnp.zeros_like(gchan_ref)

    d_out = None
    for d in range(pack_ref.shape[0]):
        term = dot_nt(
            dt_ref[0, :, d * depth : (d + 1) * depth], pack_ref[d, 2 * width : 3 * width, :]
        )
        d_out = term if d_out is None else d_out + term
    pos, live = positions(lens_ref, chunk * rows, (rows, width))
    by = by_ref[...]
    h = h_ref[...]
    side, slope = gelu_both(by)
    d_out = jnp.where(live, d_out, 0.0)
    dby_ref[...] = (d_out * h.astype(HALF).astype(SINGLE) * slope).astype(HALF)
    gate_a = ra_ref[...]
    soft = chan_ref[CONV + 4 : CONV + 5, :]
    decay = jnp.exp(-DECAY * gate_a * soft)
    put_tiles(coef, jnp.where(pos == 0, 0.0, decay))
    put_tiles(drive, (d_out * side).astype(HALF).astype(SINGLE))
    tiles = lane_tiles(width)

    def scan(j, state):
        at = pl.ds(span - 1 - j, lanes, stride=span)
        result = []
        for (t, _, _), (after, prod) in zip(tiles, state):
            a = coef[t, at, :]
            lam = drive[t, at, :] + after
            drive[t, at, :] = lam
            coef[t, at, :] = prod
            result.append((a * lam, prod * a))
        return result

    state = lax.fori_loop(0, span, scan, scan_start(tiles, lanes), unroll=4)
    for (t, first, used), (after, prod) in zip(tiles, state):
        running = carry[t, 0:1, :]
        for s in reversed(range(lanes)):
            at = slice(s * span, (s + 1) * span)
            value = drive[t, at, :] + coef[t, at, :] * running
            lift[at, first : first + used] = value[:, :used]
            running = after[s : s + 1, :] + prod[s : s + 1, :] * running
        carry[t, 0:1, :] = running
    lam = lift[0:rows, :]
    last = jnp.where(chunk > 0, hprev_ref[7:8, :], 0.0)
    before = jnp.concatenate([last, h[: rows - 1, :]], axis=0)
    before = jnp.where(pos == 0, 0.0, before)
    conv = conv_ref[...]
    gate_in = gi_ref[...]
    root = jnp.sqrt(1.0 - decay * decay)
    d_decay = lam * before - lam * gate_in * conv * decay / root
    d_log = d_decay * decay
    d_a = d_log * (-DECAY * soft)
    d_in = lam * conv * root
    d_logit_in = d_in * gate_in * (1.0 - gate_in)
    d_logit_a = d_a * gate_a * (1.0 - gate_a)
    d_conv = (
        lam * gate_in * root
        + split_dot(dot_nt, d_logit_in, bin_ref[...])
        + split_dot(dot_nt, d_logit_a, ba_ref[...])
    )
    low = conv.astype(HALF)
    gin_ref[...] += dot_tn(low, d_logit_in.astype(HALF))
    ga_ref[...] += dot_tn(low, d_logit_a.astype(HALF))
    lift[0:rows, :] = d_conv
    bx = bx_ref[...].astype(SINGLE)
    d_bx = jnp.zeros((rows, width), SINGLE)
    for k in range(CONV):
        if k:
            ahead, _ = positions(lens_ref, chunk * rows + k, (rows, width))
            moved = jnp.where(ahead >= k, lift[k : k + rows, :], 0.0)
        else:
            moved = d_conv
        d_bx = d_bx + moved * chan_ref[k : k + 1, :]
        gchan_ref[k : k + 1, :] += jnp.sum(moved * bx, axis=0, keepdims=True)
    dbx_ref[...] = d_bx.astype(HALF)
    lift[rows : rows + 8, :] = d_conv[0:8, :]
    sums = (d_conv, d_logit_in, d_logit_a, d_log * gate_a)
    for j, value in enumerate(sums):
        gchan_ref[CONV + j : CONV + j + 1, :] += jnp.sum(value, axis=0, keepdims=True)


def backward_channels(lens, dt_all, pack, blocks_in, blocks_a, chan, saved):
    bx, by, conv, gate_in, gate_a, h = saved
    count, rows, model = dt_all.shape
    width = chan.shape[1]
    tokens = count * rows
    last = count - 1
    whole = lambda shape: pl.BlockSpec(shape, lambda i: (0,) * len(shape))
    part = pl.BlockSpec((rows, width), lambda i: (last - i, 0))
    before = pl.BlockSpec(
        (8, width), lambda i: (jnp.maximum((last - i) * (rows // 8) - 1, 0), 0)
    )
    full = lambda kind: jax.ShapeDtypeStruct((tokens, width), kind)
    square = jax.ShapeDtypeStruct((width, width), SINGLE)
    return pl.pallas_call(
        backward_kernel,
        grid=(count,),
        out_shape=(full(HALF), full(HALF), square, square, jax.ShapeDtypeStruct((8, width), SINGLE)),
        in_specs=[
            pl.BlockSpec(memory_space=pltpu.SMEM),
            pl.BlockSpec((1, rows, model), lambda i: (last - i, 0, 0)),
            whole(pack.shape),
            whole(blocks_in.shape),
            whole(blocks_a.shape),
            whole(chan.shape),
            part,
            part,
            part,
            part,
            part,
            part,
            before,
        ],
        out_specs=(part, part, whole((width, width)), whole((width, width)), whole((8, width))),
        scratch_shapes=[
            pltpu.VMEM((rows + 8, width), SINGLE),
            pltpu.VMEM((len(lane_tiles(width)), rows, 128), SINGLE),
            pltpu.VMEM((len(lane_tiles(width)), rows, 128), SINGLE),
            pltpu.VMEM((len(lane_tiles(width)), 8, 128), SINGLE),
        ],
        compiler_params=pltpu.CompilerParams(vmem_limit_bytes=VMEM_BYTES),
        cost_estimate=pl.CostEstimate(
            flops=2 * tokens * model * width,
            bytes_accessed=tokens * (model * 2 + width * 28),
            transcendentals=8 * tokens * width,
        ),
        name="backward_channels",
    )(lens, dt_all, pack, blocks_in, blocks_a, chan, bx, by, conv, gate_in, gate_a, h, h)


def diagonal(blocks):
    count, size, _ = blocks.shape
    spread = blocks[:, :, None, :] * jnp.eye(count, dtype=blocks.dtype)[:, None, :, None]
    return spread.reshape(count * size, count * size)


def on_device(
    layer_input,
    cotangent,
    norm_in,
    norm_mid,
    w_rnn_in,
    w_rnn_gate,
    w_rnn_out,
    gate_in_blocks,
    gate_a_blocks,
    channel_params,
    w_mlp_gate,
    w_mlp_up,
    w_mlp_down,
    lengths,
):
    parts = lax.axis_size("dp")
    rows, model = layer_input.shape
    depth, width = w_rnn_in.shape
    heads, bite, block = gate_in_blocks.shape
    tokens = rows * lax.axis_size("mp")

    flat = jnp.concatenate(
        [
            gate_in_blocks.astype(HALF).reshape(-1),
            gate_a_blocks.astype(HALF).reshape(-1),
            channel_params.astype(HALF).reshape(-1),
        ]
    )
    used = flat.shape[0]
    small_rows = -(-used // (16 * depth)) * 16
    flat = jnp.pad(flat, (0, small_rows * depth - used)).reshape(small_rows, depth)
    mine = jnp.concatenate(
        [
            w_rnn_in.astype(HALF).T,
            w_rnn_gate.astype(HALF).T,
            w_rnn_out.astype(HALF),
            flat,
        ],
        axis=0,
    )
    pack = lax.all_gather(mine, "dp", axis=0, tiled=False)
    down = lax.all_gather(w_mlp_down.astype(HALF), "dp", axis=1, tiled=True)
    gate_w = lax.all_gather(w_mlp_gate.astype(HALF), "dp", axis=0, tiled=True)
    up_w = lax.all_gather(w_mlp_up.astype(HALF), "dp", axis=0, tiled=True)
    gains = lax.all_gather(
        jnp.stack([norm_in, norm_mid]).astype(HALF), ("dp", "mp"), axis=1, tiled=True
    ).astype(SINGLE)
    gain_first, gain_second = gains[0:1], gains[1:2]

    small = pack[:, 3 * width :, :].reshape(parts, -1)
    size = heads * bite * block
    whole_block = lambda v: diagonal(
        v.reshape(parts, heads, bite, block).transpose(1, 0, 2, 3).reshape(heads, block, block)
    )
    blocks_in = whole_block(small[:, :size])
    blocks_a = whole_block(small[:, size : 2 * size])
    channel = small[:, 2 * size : used].reshape(2 * CONV, width).astype(SINGLE)
    soft = jax.nn.softplus(-channel[2 * CONV - 1 :])
    chan = jnp.concatenate([channel, soft, jnp.zeros((7, width), SINGLE)], axis=0)

    x_all = gather_rows(layer_input, 0)
    c_all = gather_rows(cotangent, 1).reshape(tokens, model)
    n1, bx, by, conv, gate_in, gate_a, h, ob = forward_channels(
        lengths, x_all, gain_first, pack, blocks_in, blocks_a, chan
    )
    inputs = layer_input.astype(SINGLE)
    out = scatter_products(
        [ob],
        [pack],
        [lambda l, r, t, cols: dot_nn(l, r[t, 2 * width : 3 * width, :])],
        lambda: jnp.einsum(
            "tc,dcm->tdm", ob, pack[:, 2 * width : 3 * width], preferred_element_type=SINGLE
        ).reshape(tokens, model),
        model,
        depth,
        2,
        2 * tokens * width * model,
    )
    residual = inputs + out
    scale_second = lax.rsqrt(jnp.mean(residual * residual, axis=-1, keepdims=True) + EPS)
    normed_mid = (residual * scale_second * gain_second).astype(HALF)
    n2 = gather_rows(normed_mid, 3).reshape(tokens, model)

    gate_pre = dot_nn(n2, gate_w)
    d_hidden = dot_nt(c_all, down)
    act, slope = gelu_both(gate_pre)
    d_up = (d_hidden * act).astype(HALF)
    up_pre = dot_nn(n2, up_w)
    hidden = (act * up_pre).astype(HALF)
    d_gate = (d_hidden * up_pre * slope).astype(HALF)
    tile = 512
    by_rows = lambda l, r, t, cols: dot_nt(l, r[cols, :])
    d_normed_mid = scatter_products(
        [d_gate, d_up],
        [gate_w, up_w],
        [by_rows, by_rows],
        lambda: dot_nt(d_gate, gate_w) + dot_nt(d_up, up_w),
        model,
        tile,
        4,
        4 * tokens * model * up_w.shape[1],
    )
    grad_up = dot_tn(n2, d_up)
    grad_gate = dot_tn(n2, d_gate)
    grad_down = dot_tn(hidden, c_all)
    mlp_out = scatter_products(
        [hidden],
        [down],
        [lambda l, r, t, cols: dot_nn(l, r[:, cols])],
        lambda: dot_nn(hidden, down),
        model,
        tile,
        5,
        2 * tokens * model * up_w.shape[1],
    )
    layer_output = (residual + mlp_out).astype(HALF)

    weighted_second = gain_second * d_normed_mid
    grad_gain_second = jnp.sum(d_normed_mid * residual * scale_second, axis=0)
    cube_second = scale_second * scale_second * scale_second
    d_residual = (
        cotangent.astype(SINGLE)
        + scale_second * weighted_second
        - residual * cube_second * jnp.mean(weighted_second * residual, axis=-1, keepdims=True)
    )
    dt_all = gather_rows(d_residual.astype(HALF), 6)

    d_bx, d_by, gin, ga, gchan = backward_channels(
        lengths, dt_all, pack, blocks_in, blocks_a, chan, (bx, by, conv, gate_in, gate_a, h)
    )
    d_normed = scatter_products(
        [d_bx, d_by],
        [pack, pack],
        [
            lambda l, r, t, cols: dot_nn(l, r[t, :width, :]),
            lambda l, r, t, cols: dot_nn(l, r[t, width : 2 * width, :]),
        ],
        lambda: jnp.einsum(
            "tc,dcm->tdm",
            jnp.concatenate([d_bx, d_by], axis=1),
            pack[:, : 2 * width],
            preferred_element_type=SINGLE,
        ).reshape(tokens, model),
        model,
        depth,
        7,
        4 * tokens * width * model,
    )
    dt_flat = dt_all.reshape(tokens, model)
    grad_out = dot_tn(ob, dt_flat)
    grad_in = dot_tn(d_bx, n1)
    grad_side = dot_tn(d_by, n1)

    scale_first = lax.rsqrt(jnp.mean(inputs * inputs, axis=-1, keepdims=True) + EPS)
    weighted_first = gain_first * d_normed
    grad_gain_first = jnp.sum(d_normed * inputs * scale_first, axis=0)
    cube_first = scale_first * scale_first * scale_first
    grad_input = (
        d_residual
        + scale_first * weighted_first
        - inputs * cube_first * jnp.mean(weighted_first * inputs, axis=-1, keepdims=True)
    )

    def over_dp(value, dimension):
        return lax.psum_scatter(
            value.astype(HALF), "dp", scatter_dimension=dimension, tiled=True
        )

    own = lambda full: jnp.stack(
        [full[j * block : (j + 1) * block, j * block : (j + 1) * block] for j in range(heads)]
    )
    decay_row = DECAY * jax.nn.sigmoid(-channel[2 * CONV - 1 :]) * gchan[2 * CONV - 1 :]
    grad_channel = jnp.concatenate([gchan[: 2 * CONV - 1], decay_row], axis=0)
    split = lambda v: v.reshape(heads, parts, bite, block).transpose(1, 0, 2, 3).reshape(parts, -1)
    small_grads = jnp.concatenate(
        [split(own(gin)), split(own(ga)), grad_channel.reshape(parts, -1)], axis=1
    )
    small_grads = jnp.pad(small_grads, ((0, 0), (0, small_rows * depth - used)))
    small_grads = small_grads.reshape(parts, small_rows, depth)
    by_part = lambda v: v.reshape(width, parts, depth).transpose(1, 0, 2)
    rnn_grads = jnp.concatenate(
        [by_part(grad_in), by_part(grad_side), by_part(grad_out), small_grads], axis=1
    )
    grad_up = over_dp(grad_up, 0).astype(SINGLE)
    grad_gate = over_dp(grad_gate, 0).astype(SINGLE)
    grad_down = over_dp(grad_down, 1).astype(SINGLE)
    rnn_grads = over_dp(rnn_grads, 0)[0].astype(SINGLE)
    flat_grads = rnn_grads[3 * width :].reshape(-1)
    gain_grads = lax.psum_scatter(
        jnp.stack([grad_gain_first, grad_gain_second]).astype(HALF),
        ("dp", "mp"),
        scatter_dimension=1,
        tiled=True,
    ).astype(SINGLE)
    return (
        layer_output,
        grad_input,
        gain_grads[0],
        gain_grads[1],
        rnn_grads[:width].T,
        rnn_grads[width : 2 * width].T,
        rnn_grads[2 * width : 3 * width],
        flat_grads[:size].reshape(heads, bite, block),
        flat_grads[size : 2 * size].reshape(heads, bite, block),
        flat_grads[2 * size : used].reshape(channel_params.shape),
        grad_gate,
        grad_up,
        grad_down,
    )


def solution(mesh):
    rows = P(("dp", "mp"), None)
    return jax.shard_map(
        on_device,
        mesh=mesh,
        in_specs=(
            rows,
            rows,
            P(("dp", "mp")),
            P(("dp", "mp")),
            P("dp", "mp"),
            P("dp", "mp"),
            P("mp", "dp"),
            P("mp", "dp", None),
            P("mp", "dp", None),
            P("dp", "mp"),
            P("dp", "mp"),
            P("dp", "mp"),
            P("mp", "dp"),
            P("dp", None),
        ),
        out_specs=(
            rows,
            rows,
            P(("dp", "mp")),
            P(("dp", "mp")),
            P("dp", "mp"),
            P("dp", "mp"),
            P("mp", "dp"),
            P("mp", "dp", None),
            P("mp", "dp", None),
            P("dp", "mp"),
            P("dp", "mp"),
            P("dp", "mp"),
            P("mp", "dp"),
        ),
        check_vma=False,
    )
```

time: 2160 us -> 957 us (0.44)
  waiting for transfers between devices: 1370 us -> 307 us
  Pallas kernels: 0 us -> 423 us
  other arithmetic: 214 us -> 37.8 us
  local copies, waits for them, and re-layouts: 190 us -> 29.6 us
  matrix products: 201 us -> 96.6 us
  blocking collectives: 141 us -> 43.6 us
    all_gather x11 -> x4, waiting for transfers between devices: 649 us -> 0.03 us  [the longest x1 0.02 us: on_device(): gate_w = lax.all_gather(w_mlp_gate.astype(HALF), 'dp', axis=0, tiled=True)]
    pallas_call x0 -> x10, Pallas kernels: none -> 423 us  [the longest x4 191 us: scatter_products(): pl.pallas_call(functools.partial(scatter_kernel, products, tile), out_sha...]
    reduce_scatter x9 -> x4, waiting for transfers between devices: 632 us -> 255 us  [over_dp(): lax.psum_scatter(value.astype(HALF), 'dp', scatter_dimension=dimension, t...]
    dot_general x64 -> x0, other arithmetic: 115 us -> none  [exact_einsum(): jnp.einsum(form, left, right, precision=lax.Precision.HIGHEST, preferred_...]
    dot_general x24 -> x9, matrix products: 201 us -> 96.6 us  [the longest x6 54.3 us: dot_tn(): lax.dot_general(left, right, (((0,), (0,)), ((), ())), preferred_element_...]
    rev x6 -> x0, local copies, waits for them, and re-layouts: 67.9 us -> none  [the longest x1 25.6 us: channel_backward(): jnp.flip(block_scan(jnp.flip(next_logs, 0), jnp.flip(d_states, 0), jnp.fl...]
    squeeze x64 -> x1, local copies, waits for them, and re-layouts: 61.5 us -> 0.53 us  [on_device(): gain_grads[1]]
    unnamed x3 -> x0, blocking collectives: 42.2 us -> none
  transfers between devices with their start and end apart: 26 -> 9, of which waited for: 21 -> 5; matrix products, arithmetic and copies ran while one was open for 25% -> 13% of each run, Pallas kernels for 0% -> 21%
where the time goes in v1:
time: 957 us; the launch traced here: 953 us
  Pallas kernels  423 us (44%)
  waiting for transfers between devices  307 us (32%)
  matrix products  96.6 us (10%)
  blocking collectives  43.6 us (5%)
  other arithmetic  37.8 us (4%)
  local copies, waits for them, and re-layouts  29.6 us (3%)
  between operations  14.7 us (2%)
    reduce_scatter x4, waiting for transfers between devices, over_dp(): lax.psum_scatter(value.astype(HALF), 'dp', scatter_dimension=dimension, t...  255 us
    pallas_call x4, Pallas kernels, scatter_products(): pl.pallas_call(functools.partial(scatter_kernel, products, tile), out_sha...  191 us
    pallas_call x4, Pallas kernels, gather_rows(): pl.pallas_call(functools.partial(gather_kernel, count), out_shape=jax.Sha...  162 us
    dot_general x6, matrix products, dot_tn(): lax.dot_general(left, right, (((0,), (0,)), ((), ())), preferred_element_...  54.3 us
    unnamed x10, waiting for transfers between devices  52.6 us
    all_gather x1, blocking collectives, on_device(): lax.all_gather(jnp.stack([norm_in, norm_mid]).astype(HALF), ('dp', 'mp'),...  43.6 us
    pallas_call x1, Pallas kernels, forward_channels(): pl.pallas_call(forward_kernel, grid=(count,), out_shape=(jax.ShapeDtypeSt...  35.6 us
    pallas_call x1, Pallas kernels, backward_channels(): pl.pallas_call(backward_kernel, grid=(count,), out_shape=(full(HALF), ful...  34.4 us
  transfers between devices with their start and end apart: 9, of which 5 were waited for; matrix products, arithmetic and copies ran while one was open for 13% of the time, Pallas kernels for 21%

profile of v1, /device:TPU:0, one launch (start us, length us, event | category | flops | bytes accessed | tf_op | source)
XLA Modules:
  0.0 952.5 jit_solution(10062539242781149279)
XLA Ops:
  7.2 1.2 convert_element_type.106
  11.4 1.4 convert_bitcast_fusion
  12.7 1.0 pad_maximum_fusion.1
  13.9 1.0 convert_element_type.114
  16.5 1.0 convert_element_type.117
  17.6 43.6 %all-gather.1 = bf16[32,64,2]{1,2,0:T(2,128)(2,1)S(1)} all-gather(bf16[1,64,2]{1,2,0:T(2,128)(2,1)S(1)} %maximum_bitcast_fusion.2), channel_id=1, replica_groups=mesh['dp'=4,'mp'=8] {'dp','mp'}, dimensions={0}, use_global_device_ids=true | all-gather | bytes 8448 | tf_op jit(solution)/shard_map/all_gather | solution.py:699
  62.0 39.9 %gather_rows.4.x_ref = bf16[8,256,2048]{2,1,0:T(8,128)(2,1)} custom-call(bf16[256,2048]{1,0:T(8,128)(2,1)} %x_ref.2), custom_call_target="tpu_custom_call" | custom-call | bytes 67108864 | tf_op jit(solution)/shard_map/gather_rows/pallas_call | solution.py:124
  101.9 41.9 %gather_rows.6 = bf16[8,256,2048]{2,1,0:T(8,128)(2,1)} custom-call(bf16[256,2048]{1,0:T(8,128)(2,1)} %x_ref.3), custom_call_target="tpu_custom_call" | custom-call | bytes 67108864 | tf_op jit(solution)/shard_map/gather_rows/pallas_call | solution.py:124
  143.9 1.0 slice_bitcast_fusion.3
  148.9 35.6 %forward_channels.1 = (bf16[2048,2048]{1,0:T(8,128)(2,1)}, bf16[2048,320]{1,0:T(8,128)(2,1)}, f32[2048,320]{1,0:T(8,128)}, f32[2048,320]{1,0:T(8,128)}, f32[2048...) custom-call(s32[1,3]{1,0:T(1,128)} %lens_ref.3, ...), custom_call_target="tpu_custom_call" | custom-call | flops 5368709120 | bytes 32505856 | tf_op jit(solution)/shard_map/forward_channels/pallas_call | solution.py:441
  184.5 45.5 %scatter_products.4 = f32[256,2048]{1,0:T(8,128)} custom-call(bf16[2048,320]{1,0:T(8,128)(2,1)} %get-tuple-element.26.refs_0_, bf16[4,1024,512]{2,1,0:T(8,128)(2,1)} %bitcast.124), custom_call_target="tpu_custom_call" | custom-call | flops 2684354560 | bytes 67108864 | tf_op jit(solution)/shard_map/scatter_products/pallas_call | solution.py:280
  230.0 2.1 multiply_reduce_fusion.2
  232.1 1.2 multiply_convert_fusion.3.x_ref
  233.3 40.0 %gather_rows.5 = bf16[8,256,2048]{2,1,0:T(8,128)(2,1)} custom-call(bf16[256,2048]{1,0:T(8,128)(2,1)} %multiply_convert_fusion.3.x_ref), custom_call_target="tpu_custom_call" | custom-call | bytes 67108864 | tf_op jit(solution)/shard_map/gather_rows/pallas_call | solution.py:124
  273.4 11.7 %fusion.26 = f32[2048,768]{1,0:T(8,128)} fusion(bf16[2048,2048]{1,0:T(8,128)(2,1)} %bitcast.115, bf16[2048,768]{1,0:T(8,128)(2,1)} %all-gather.7.cloned.1.call-done.refs_2_), kind=kOutput, calls=%fused_computation.84 | convolution fusion | flops 6442450944 | bytes 17825792 | tf_op jit(solution)/shard_map/dot_general | solution.py:22
  285.1 11.7 %fusion.27 = f32[2048,768]{1,0:T(8,128)} fusion(bf16[2048,2048]{1,0:T(8,128)(2,1)} %bitcast.116, bf16[2048,768]{1,0:T(8,128)(2,1)} %all-gather.9.cloned.1.call-done.refs_3_), kind=kOutput, calls=%fused_computation.85 | convolution fusion | flops 6442450944 | bytes 17825792 | tf_op jit(solution)/shard_map/dot_general | solution.py:22
  296.8 18.9 %multiply_convert_fusion = (bf16[2048,768]{1,0:T(8,128)(2,1)}, bf16[2048,768]{1,0:T(8,128)(2,1)}, bf16[2048,768]{1,0:T(8,128)(2,1)}) fusion(f32[2048,768]{1,0:T(8,128)} %fusion.26, f32[2048,768]{1,0:T(8,128)} %fusion.27, bf16[2048,2048]{1,0:T(8,128)(2,1)} %bitcast.113, bf16[768,2048]{1,0:T(8,128)(2,1)} %all-gather.11.cloned.1.call-done.refs_1_), kind=kOutput, calls=%fused_computation | convolution fusion | flops 6480199680 | bytes 33554432 | tf_op jit(solution)/shard_map/dot_general | solution.py:28
  315.7 50.8 %scatter_products.6 = f32[256,2048]{1,0:T(8,128)} custom-call(bf16[2048,768]{1,0:T(8,128)(2,1)} %get-tuple-element.48.refs_0_, bf16[2048,768]{1,0:T(8,128)(2,1)} %get-tuple-element.47.refs_1_, bf16[2048,768]{1,0:T(8,128)(2,1)} %all-gather.7.cloned.1.call-done.refs_2_, bf16[2048,768]{1,0:T(8,128)(2,1)} %all-gather.9.cloned.1.call-done.refs_3_), custom_call_target="tpu_custom_call" | custom-call | flops 12884901888 | bytes 67108864 | tf_op jit(solution)/shard_map/scatter_products/pallas_call | solution.py:280
  366.5 2.1 multiply_reduce_fusion
  368.7 46.2 %scatter_products.5 = f32[256,2048]{1,0:T(8,128)} custom-call(bf16[2048,768]{1,0:T(8,128)(2,1)} %get-tuple-element.49.refs_0_, bf16[768,2048]{1,0:T(8,128)(2,1)} %all-gather.11.cloned.1.call-done.refs_1_), custom_call_target="tpu_custom_call" | custom-call | flops 6442450944 | bytes 67108864 | tf_op jit(solution)/shard_map/scatter_products/pallas_call | solution.py:280
  414.9 4.3 fusion.20
  419.2 39.8 %gather_rows.7.dt_ref = bf16[8,256,2048]{2,1,0:T(8,128)(2,1)} custom-call(bf16[256,2048]{1,0:T(8,128)(2,1)} %get-tuple-element.43.x_ref), custom_call_target="tpu_custom_call" | custom-call | bytes 67108864 | tf_op jit(solution)/shard_map/gather_rows/pallas_call | solution.py:124
  459.1 34.4 %backward_channels.1 = (bf16[2048,320]{1,0:T(8,128)(2,1)}, bf16[2048,320]{1,0:T(8,128)(2,1)}, f32[320,320]{1,0:T(8,128)}, f32[320,320]{1,0:T(8,128)}, f32[8,320]{1,0:T(8,128)}) custom-call(s32[1,3]{1,0:T(1,128)} %lens_ref.3, bf16[8,256,2048]{2,1,0:T(8,128)(2,1)} %gather_rows.7.dt_ref, bf16[4,1024,512]{2,1,0:T(8,128)(2,1)} %bitcast.125, ...), custom_call_target="tpu_custom_call" | custom-call | flops 2684354560 | bytes 26738688 | tf_op jit(solution)/shard_map/backward_channels/pallas_call | solution.py:612
  493.6 48.5 %scatter_products.7 = f32[256,2048]{1,0:T(8,128)} custom-call(bf16[2048,320]{1,0:T(8,128)(2,1)} %get-tuple-element.33.refs_0_, bf16[2048,320]{1,0:T(8,128)(2,1)} %get-tuple-element.34.refs_1_, bf16[4,1024,512]{2,1,0:T(8,128)(2,1)} %bitcast.126, bf16[4,1024,512]{2,1,0:T(8,128)(2,1)} %bitcast.127), custom_call_target="tpu_custom_call" | custom-call | flops 5368709120 | bytes 67108864 | tf_op jit(solution)/shard_map/scatter_products/pallas_call | solution.py:280
  542.1 2.1 fusion.5
  544.3 1.1 copy.69
  545.4 11.4 %convolution_convert_fusion.1 = bf16[2048,768]{1,0:T(8,128)(2,1)} fusion(bf16[2048,2048]{1,0:T(8,128)(2,1)} %bitcast.117, bf16[2048,768]{1,0:T(8,128)(2,1)} %get-tuple-element.47.refs_1_), kind=kOutput, calls=%fused_computation.12 | convolution fusion | flops 6444023808 | bytes 14680064 | tf_op jit(solution)/shard_map/dot_general | solution.py:34
  556.9 11.6 %convolution_convert_fusion.2 = bf16[2048,768]{1,0:T(8,128)(2,1)} fusion(bf16[2048,2048]{1,0:T(8,128)(2,1)} %bitcast.118, bf16[2048,768]{1,0:T(8,128)(2,1)} %get-tuple-element.48.refs_0_), kind=kOutput, calls=%fused_computation.13 | convolution fusion | flops 6444023808 | bytes 14680064 | tf_op jit(solution)/shard_map/dot_general | solution.py:34
  568.5 1.3 copy-done.15
  569.9 6.5 convolution_convert_fusion.4
  576.5 10.4 %convolution_convert_fusion = bf16[768,2048]{1,0:T(8,128)(2,1)} fusion(bf16[2048,768]{1,0:T(8,128)(2,1)S(1)} %copy-done.16, bf16[2048,2048]{1,0:T(8,128)(2,1)} %bitcast.114), kind=kOutput, calls=%fused_computation.11 | convolution fusion | flops 6444023808 | bytes 14680064 | tf_op jit(solution)/shard_map/dot_general | solution.py:34
  586.9 6.8 convolution_convert_fusion.3
  593.8 1.2 copy.80
  595.0 12.6 %copy.64 = bf16[2048,2048]{1,0:T(8,128)(2,1)} copy(bf16[2048,2048]{0,1:T(8,128)(2,1)} %bitcast.112) | data formatting | bytes 16777216 | tf_op jit(solution)/shard_map/dot_general | solution.py:34
  609.5 7.6 fusion.7
  617.1 2.1 pad_maximum_fusion
  619.3 1.6 copy-done.1
  620.8 3.5 fusion.2
  624.3 52.4 %reduce-scatter.16.cloned.1.call-done = bf16[64,2]{1,0:T(8,128)(2,1)} async-done(((bf16[2048,2]{1,0:T(8,128)(2,1)}), bf16[64,2]{1,0:T(8,128)(2,1)}) %reduce-scatter.16.cloned.1.call-update) | async-done | bytes 272
  678.1 57.1 %reduce-scatter.12.cloned.1.call-done = bf16[512,768]{1,0:T(8,128)(2,1)} async-done(((bf16[2048,768]{1,0:T(8,128)(2,1)}), bf16[512,768]{1,0:T(8,128)(2,1)}) %reduce-scatter.12.cloned.1.call-update) | async-done | bytes 786448 | tf_op jit(solution)/shard_map/reduce_scatter | solution.py:819
  735.2 2.4 convert_element_type.128
  737.6 60.3 %reduce-scatter.10.cloned.1.call-done = bf16[512,768]{1,0:T(8,128)(2,1)} async-done(((bf16[2048,768]{1,0:T(8,128)(2,1)}), bf16[512,768]{1,0:T(8,128)(2,1)}) %reduce-scatter.10.cloned.1.call-update) | async-done | bytes 786448 | tf_op jit(solution)/shard_map/reduce_scatter | solution.py:819
  797.9 2.4 convert_element_type.126
  800.3 60.3 %reduce-scatter.14.cloned.1.call-done = bf16[768,512]{1,0:T(8,128)(2,1)} async-done(((bf16[768,2048]{1,0:T(8,128)(2,1)}), bf16[768,512]{1,0:T(8,128)(2,1)}) %reduce-scatter.14.cloned.1.call-update) | async-done | bytes 786448 | tf_op jit(solution)/shard_map/reduce_scatter | solution.py:819
  860.6 2.5 convert_element_type.130
  863.1 76.7 %reduce-scatter.8.cloned.1.call-done = bf16[1,1024,512]{2,1,0:T(8,128)(2,1)} async-done(((bf16[4,1024,512]{2,1,0:T(8,128)(2,1)}), bf16[1,1024,512]{2,1,0:T(8,128)(2,1)}) %reduce-scatter.8.cloned.1.call-update) | async-done | bytes 1048592 | tf_op jit(solution)/shard_map/reduce_scatter | solution.py:819
  939.9 1.5 convert_element_type.124
  941.4 1.3 slice_bitcast_fusion
  (116 shorter events, 16.0 us)
Async XLA Ops:
  7.2 6.7 copy-start.5
  7.2 136.7 %all-gather.13.cloned.1.call-start = ((), (), s32[]{:S(2)}) async-start(), calls=%async_computation.12 | async-start | bytes 5242880 | tf_op jit(solution)/shard_map/all_gather | solution.py:695
  12.7 2.2 copy-start.6
  13.8 259.5 %all-gather.7.cloned.1.call-start = ((), (), s32[]{:S(2)}) async-start(), calls=%async_computation.5 | async-start | bytes 3932160 | tf_op jit(solution)/shard_map/all_gather | solution.py:697
  14.8 1.7 copy-start.7
  14.9 2.7 copy-start.13
  14.9 2.7 copy-start.14
  14.9 270.2 %all-gather.9.cloned.1.call-start = ((), (), s32[]{:S(2)}) async-start(), calls=%async_computation.6 | async-start | bytes 3932160 | tf_op jit(solution)/shard_map/all_gather | solution.py:698
  15.9 280.9 %all-gather.11.cloned.1.call-start = ((), (), s32[]{:S(2)}) async-start(), calls=%async_computation.7 | async-start | bytes 3932160 | tf_op jit(solution)/shard_map/all_gather | solution.py:696
  17.5 659.2 %reduce-scatter.16.cloned.1.call-start = ((), (), s32[]{:S(2)}) async-start(), calls=%async_computation.13 | async-start | bytes 540672
  145.2 39.2 %copy-start.11 = (f32[8,320]{1,0:T(8,128)}, f32[8,320]{1,0:T(8,128)S(1)}, u32[]{:S(2)}) copy-start(f32[8,320]{1,0:T(8,128)S(1)} %reshape.199) | copy-start | bytes 30724
  184.5 45.5 %copy-start = (bf16[256,2048]{1,0:T(8,128)(2,1)S(1)}, bf16[256,2048]{1,0:T(8,128)(2,1)}, u32[]{:S(2)}) copy-start(bf16[256,2048]{1,0:T(8,128)(2,1)} %x_ref.2) | copy-start | bytes 3145732
  368.7 46.2 %copy-start.2 = (f32[256,2048]{1,0:T(8,128)S(1)}, f32[256,2048]{1,0:T(8,128)}, u32[]{:S(2)}) copy-start(f32[256,2048]{1,0:T(8,128)} %scatter_products.6) | copy-start | bytes 6291460
  368.7 46.2 %copy-start.4 = (bf16[256,2048]{1,0:T(8,128)(2,1)S(1)}, bf16[256,2048]{1,0:T(8,128)(2,1)}, u32[]{:S(2)}) copy-start(bf16[256,2048]{1,0:T(8,128)(2,1)} %x_ref.3) | copy-start | bytes 3145732
  493.5 48.5 %copy-start.10 = (f32[1,2048]{1,0:T(1,128)S(1)}, f32[1,2048]{1,0:T(1,128)}, u32[]{:S(2)}) copy-start(f32[1,2048]{1,0:T(1,128)} %get-tuple-element.64.gain_ref) | copy-start | bytes 24580
  545.4 189.9 %reduce-scatter.12.cloned.1.call-start = ((), (), s32[]{:S(2)}) async-start(), calls=%async_computation.10 | async-start | bytes 3932160 | tf_op jit(solution)/shard_map/reduce_scatter | solution.py:819
  556.8 241.1 %reduce-scatter.10.cloned.1.call-start = ((), (), s32[]{:S(2)}) async-start(), calls=%async_computation.9 | async-start | bytes 3932160 | tf_op jit(solution)/shard_map/reduce_scatter | solution.py:819
  568.4 1.4 copy-start.15
  568.5 292.2 %reduce-scatter.14.cloned.1.call-start = ((), (), s32[]{:S(2)}) async-start(), calls=%async_computation.11 | async-start | bytes 3932160 | tf_op jit(solution)/shard_map/reduce_scatter | solution.py:819
  569.9 6.6 copy-start.16
  586.9 353.0 %reduce-scatter.8.cloned.1.call-start = ((), (), s32[]{:S(2)}) async-start(), calls=%async_computation.8 | async-start | bytes 5242880 | tf_op jit(solution)/shard_map/reduce_scatter | solution.py:819
  595.0 12.7 %copy-start.9 = (f32[320,320]{1,0:T(8,128)S(1)}, f32[320,320]{1,0:T(8,128)}, u32[]{:S(2)}) copy-start(f32[320,320]{1,0:T(8,128)} %get-tuple-element.36) | copy-start | bytes 1228804
  595.0 13.1 %copy-start.8 = (f32[320,320]{1,0:T(8,128)S(1)}, f32[320,320]{1,0:T(8,128)}, u32[]{:S(2)}) copy-start(f32[320,320]{1,0:T(8,128)} %get-tuple-element.37) | copy-start | bytes 1228804
  607.6 0.8 copy-start.12
  609.5 7.6 copy-start.3
  619.2 1.6 copy-start.1
Sparse Core Ops, SparseCore 0:
  13.9 83.4 all-gather.12
  99.6 61.9 all-gather.6
  163.8 62.1 all-gather.8
  227.4 62.1 all-gather.10
  545.5 131.2 reduce-scatter.15
  679.0 56.1 reduce-scatter.11
  737.6 60.2 reduce-scatter.9
  800.3 60.2 reduce-scatter.13
  863.0 76.7 reduce-scatter.7

commit v2 on v1

--- a/solution.py
+++ b/solution.py
@@ -56,6 +56,111 @@
             place = place + (1 - 2 * ((me // bit) % 2)) * bit
         bit *= 2
     return place
+
+
+def all_bits():
+    inner, outer = lax.axis_size("mp"), lax.axis_size("dp")
+    bits = [(1 << b, "mp", 1 << b) for b in range(inner.bit_length() - 1)]
+    return bits + [(inner << b, "dp", 1 << b) for b in range(outer.bit_length() - 1)]
+
+
+def across(axis, bit):
+    return {axis: flip(lax.axis_index(axis), bit, 2 * bit)}
+
+
+def greet(bits):
+    barrier = pltpu.get_barrier_semaphore()
+    for _, axis, bit in bits:
+        pl.semaphore_signal(barrier, inc=1, device_id=across(axis, bit), device_id_type=MESH)
+    pl.semaphore_wait(barrier, len(bits))
+
+
+def share_kernel(x_ref, o_ref, send, recv):
+    bits = all_bits()
+    place = lax.axis_index("dp") * lax.axis_size("mp") + lax.axis_index("mp")
+    o_ref[place] = x_ref[...]
+    greet(bits)
+    copies = []
+    for j, (size, axis, bit) in enumerate(bits):
+        window = o_ref.at[pl.ds(place // size * size, size)]
+        copy = pltpu.make_async_remote_copy(
+            src_ref=window,
+            dst_ref=window,
+            send_sem=send.at[j],
+            recv_sem=recv.at[j],
+            device_id=across(axis, bit),
+            device_id_type=MESH,
+        )
+        copy.start()
+        copy.wait_recv()
+        copies.append(copy)
+    for copy in copies:
+        copy.wait_send()
+
+
+def share(x, collective_id):
+    bits = all_bits()
+    return pl.pallas_call(
+        share_kernel,
+        out_shape=jax.ShapeDtypeStruct((1 << len(bits),) + x.shape, x.dtype),
+        in_specs=[pl.BlockSpec(memory_space=pltpu.VMEM)],
+        out_specs=pl.BlockSpec(memory_space=pltpu.VMEM),
+        scratch_shapes=[
+            pltpu.SemaphoreType.DMA((len(bits),)),
+            pltpu.SemaphoreType.DMA((len(bits),)),
+        ],
+        compiler_params=pltpu.CompilerParams(
+            collective_id=collective_id, has_side_effects=True
+        ),
+        name="share",
+    )(x)
+
+
+def total_kernel(x_ref, o_ref, kept, landed, send, recv):
+    bits = all_bits()
+    place = lax.axis_index("dp") * lax.axis_size("mp") + lax.axis_index("mp")
+    kept[...] = x_ref[...]
+    greet(bits)
+    copies = []
+    for j, (size, axis, bit) in reversed(list(enumerate(bits))):
+        first = place // size * size
+        other = first + (1 - 2 * ((place // size) % 2)) * size
+        copy = pltpu.make_async_remote_copy(
+            src_ref=kept.at[pl.ds(other, size)],
+            dst_ref=landed.at[pl.ds(size, size)],
+            send_sem=send.at[j],
+            recv_sem=recv.at[j],
+            device_id=across(axis, bit),
+            device_id_type=MESH,
+        )
+        copy.start()
+        copy.wait_recv()
+        mine = pl.ds(first, size)
+        kept[mine] = kept[mine] + landed[size : 2 * size]
+        copies.append(copy)
+    o_ref[...] = kept[place]
+    for copy in copies:
+        copy.wait_send()
+
+
+def total(x, collective_id):
+    bits = all_bits()
+    return pl.pallas_call(
+        total_kernel,
+        out_shape=jax.ShapeDtypeStruct(x.shape[1:], x.dtype),
+        in_specs=[pl.BlockSpec(memory_space=pltpu.VMEM)],
+        out_specs=pl.BlockSpec(memory_space=pltpu.VMEM),
+        scratch_shapes=[
+            pltpu.VMEM(x.shape, x.dtype),
+            pltpu.VMEM(x.shape, x.dtype),
+            pltpu.SemaphoreType.DMA((len(bits),)),
+            pltpu.SemaphoreType.DMA((len(bits),)),
+        ],
+        compiler_params=pltpu.CompilerParams(
+            collective_id=collective_id, has_side_effects=True
+        ),
+        name="total",
+    )(x)
 
 
 def gather_plan(count):
@@ -491,11 +596,15 @@
     ra_ref,
     h_ref,
     hprev_ref,
+    ob_ref,
+    n1_ref,
     dbx_ref,
     dby_ref,
     gin_ref,
     ga_ref,
     gchan_ref,
+    grads_ref,
+    grads,
     lift,
     coef,
     drive,
@@ -517,6 +626,7 @@
         gin_ref[...] = jnp.zeros_like(gin_ref)
         ga_ref[...] = jnp.zeros_like(ga_ref)
         gchan_ref[...] = jnp.zeros_like(gchan_ref)
+        grads[...] = jnp.zeros_like(grads)
 
     d_out = None
     for d in range(pack_ref.shape[0]):
@@ -594,10 +704,20 @@
     sums = (d_conv, d_logit_in, d_logit_a, d_log * gate_a)
     for j, value in enumerate(sums):
         gchan_ref[CONV + j : CONV + j + 1, :] += jnp.sum(value, axis=0, keepdims=True)
+    lefts = (dbx_ref[...], dby_ref[...], ob_ref[...])
+    for d in range(grads.shape[0]):
+        columns = slice(d * depth, (d + 1) * depth)
+        rights = (n1_ref[:, columns], n1_ref[:, columns], dt_ref[0, :, columns])
+        for j, (left, right) in enumerate(zip(lefts, rights)):
+            grads[d, j * width : (j + 1) * width, :] += dot_tn(left, right)
+
+    @pl.when(chunk == 0)
+    def _():
+        grads_ref[...] = grads[...].astype(HALF)
 
 
 def backward_channels(lens, dt_all, pack, blocks_in, blocks_a, chan, saved):
-    bx, by, conv, gate_in, gate_a, h = saved
+    bx, by, conv, gate_in, gate_a, h, ob, n1 = saved
     count, rows, model = dt_all.shape
     width = chan.shape[1]
     tokens = count * rows
@@ -609,10 +729,18 @@
     )
     full = lambda kind: jax.ShapeDtypeStruct((tokens, width), kind)
     square = jax.ShapeDtypeStruct((width, width), SINGLE)
+    grads = (pack.shape[0], 3 * width, pack.shape[2])
     return pl.pallas_call(
         backward_kernel,
         grid=(count,),
-        out_shape=(full(HALF), full(HALF), square, square, jax.ShapeDtypeStruct((8, width), SINGLE)),
+        out_shape=(
+            full(HALF),
+            full(HALF),
+            square,
+            square,
+            jax.ShapeDtypeStruct((8, width), SINGLE),
+            jax.ShapeDtypeStruct(grads, HALF),
+        ),
         in_specs=[
             pl.BlockSpec(memory_space=pltpu.SMEM),
             pl.BlockSpec((1, rows, model), lambda i: (last - i, 0, 0)),
@@ -627,9 +755,19 @@
             part,
             part,
             before,
+            part,
+            pl.BlockSpec((rows, model), lambda i: (last - i, 0)),
         ],
-        out_specs=(part, part, whole((width, width)), whole((width, width)), whole((8, width))),
+        out_specs=(
+            part,
+            part,
+            whole((width, width)),
+            whole((width, width)),
+            whole((8, width)),
+            whole(grads),
+        ),
         scratch_shapes=[
+            pltpu.VMEM(grads, SINGLE),
             pltpu.VMEM((rows + 8, width), SINGLE),
             pltpu.VMEM((len(lane_tiles(width)), rows, 128), SINGLE),
             pltpu.VMEM((len(lane_tiles(width)), rows, 128), SINGLE),
@@ -642,7 +780,7 @@
             transcendentals=8 * tokens * width,
         ),
         name="backward_channels",
-    )(lens, dt_all, pack, blocks_in, blocks_a, chan, bx, by, conv, gate_in, gate_a, h, h)
+    )(lens, dt_all, pack, blocks_in, blocks_a, chan, bx, by, conv, gate_in, gate_a, h, h, ob, n1)
 
 
 def diagonal(blocks):
@@ -696,10 +834,11 @@
     down = lax.all_gather(w_mlp_down.astype(HALF), "dp", axis=1, tiled=True)
     gate_w = lax.all_gather(w_mlp_gate.astype(HALF), "dp", axis=0, tiled=True)
     up_w = lax.all_gather(w_mlp_up.astype(HALF), "dp", axis=0, tiled=True)
-    gains = lax.all_gather(
-        jnp.stack([norm_in, norm_mid]).astype(HALF), ("dp", "mp"), axis=1, tiled=True
-    ).astype(SINGLE)
-    gain_first, gain_second = gains[0:1], gains[1:2]
+    bite_gain = norm_in.shape[0]
+    gains = jnp.stack([norm_in, norm_mid]).astype(HALF).astype(SINGLE)
+    gains = share(jnp.pad(gains, ((0, 6), (0, 128 - bite_gain))), 8)
+    gain_first = gains[:, 0, :bite_gain].reshape(1, model)
+    gain_second = gains[:, 1, :bite_gain].reshape(1, model)
 
     small = pack[:, 3 * width :, :].reshape(parts, -1)
     size = heads * bite * block
@@ -735,13 +874,22 @@
     normed_mid = (residual * scale_second * gain_second).astype(HALF)
     n2 = gather_rows(normed_mid, 3).reshape(tokens, model)
 
+    def over_dp(value, dimension):
+        return lax.psum_scatter(
+            value.astype(HALF), "dp", scatter_dimension=dimension, tiled=True
+        )
+
+    d_hidden = dot_nt(c_all, down)
     gate_pre = dot_nn(n2, gate_w)
-    d_hidden = dot_nt(c_all, down)
     act, slope = gelu_both(gate_pre)
     d_up = (d_hidden * act).astype(HALF)
+    grad_up = over_dp(dot_tn(n2, d_up), 0)
     up_pre = dot_nn(n2, up_w)
     hidden = (act * up_pre).astype(HALF)
     d_gate = (d_hidden * up_pre * slope).astype(HALF)
+    grad_gate = dot_tn(n2, d_gate).astype(HALF)
+    d_gate, grad_gate = lax.optimization_barrier((d_gate, grad_gate))
+    grad_gate = over_dp(grad_gate, 0)
     tile = 512
     by_rows = lambda l, r, t, cols: dot_nt(l, r[cols, :])
     d_normed_mid = scatter_products(
@@ -754,20 +902,10 @@
         4,
         4 * tokens * model * up_w.shape[1],
     )
-    grad_up = dot_tn(n2, d_up)
-    grad_gate = dot_tn(n2, d_gate)
-    grad_down = dot_tn(hidden, c_all)
-    mlp_out = scatter_products(
-        [hidden],
-        [down],
-        [lambda l, r, t, cols: dot_nn(l, r[:, cols])],
-        lambda: dot_nn(hidden, down),
-        model,
-        tile,
-        5,
-        2 * tokens * model * up_w.shape[1],
-    )
-    layer_output = (residual + mlp_out).astype(HALF)
+    hidden, d_normed_mid = lax.optimization_barrier((hidden, d_normed_mid))
+    grad_down = dot_tn(c_all, hidden).astype(HALF)
+    d_normed_mid, grad_down = lax.optimization_barrier((d_normed_mid, grad_down))
+    grad_down = over_dp(grad_down, 0)
 
     weighted_second = gain_second * d_normed_mid
     grad_gain_second = jnp.sum(d_normed_mid * residual * scale_second, axis=0)
@@ -777,11 +915,15 @@
         + scale_second * weighted_second
         - residual * cube_second * jnp.mean(weighted_second * residual, axis=-1, keepdims=True)
     )
-    dt_all = gather_rows(d_residual.astype(HALF), 6)
-
-    d_bx, d_by, gin, ga, gchan = backward_channels(
-        lengths, dt_all, pack, blocks_in, blocks_a, chan, (bx, by, conv, gate_in, gate_a, h)
-    )
+    d_resid_low, grad_up = lax.optimization_barrier((d_residual.astype(HALF), grad_up))
+    dt_all = gather_rows(d_resid_low, 6)
+    dt_all, grad_gate = lax.optimization_barrier((dt_all, grad_gate))
+
+    saved = (bx, by, conv, gate_in, gate_a, h, ob, n1)
+    d_bx, d_by, gin, ga, gchan, rnn_grads = backward_channels(
+        lengths, dt_all, pack, blocks_in, blocks_a, chan, saved
+    )
+    d_bx, grad_down = lax.optimization_barrier((d_bx, grad_down))
     d_normed = scatter_products(
         [d_bx, d_by],
         [pack, pack],
@@ -800,10 +942,20 @@
         7,
         4 * tokens * width * model,
     )
-    dt_flat = dt_all.reshape(tokens, model)
-    grad_out = dot_tn(ob, dt_flat)
-    grad_in = dot_tn(d_bx, n1)
-    grad_side = dot_tn(d_by, n1)
+    rnn_grads = over_dp(rnn_grads, 0)
+    hidden, d_normed = lax.optimization_barrier((hidden, d_normed))
+    mlp_out = scatter_products(
+        [hidden],
+        [down],
+        [lambda l, r, t, cols: dot_nn(l, r[:, cols])],
+        lambda: dot_nn(hidden, down),
+        model,
+        tile,
+        5,
+        2 * tokens * model * up_w.shape[1],
+    )
+    mlp_out, rnn_grads = lax.optimization_barrier((mlp_out, rnn_grads))
+    layer_output = (residual + mlp_out).astype(HALF)
 
     scale_first = lax.rsqrt(jnp.mean(inputs * inputs, axis=-1, keepdims=True) + EPS)
     weighted_first = gain_first * d_normed
@@ -815,11 +967,6 @@
         - inputs * cube_first * jnp.mean(weighted_first * inputs, axis=-1, keepdims=True)
     )
 
-    def over_dp(value, dimension):
-        return lax.psum_scatter(
-            value.astype(HALF), "dp", scatter_dimension=dimension, tiled=True
-        )
-
     own = lambda full: jnp.stack(
         [full[j * block : (j + 1) * block, j * block : (j + 1) * block] for j in range(heads)]
     )
@@ -831,35 +978,25 @@
     )
     small_grads = jnp.pad(small_grads, ((0, 0), (0, small_rows * depth - used)))
     small_grads = small_grads.reshape(parts, small_rows, depth)
-    by_part = lambda v: v.reshape(width, parts, depth).transpose(1, 0, 2)
-    rnn_grads = jnp.concatenate(
-        [by_part(grad_in), by_part(grad_side), by_part(grad_out), small_grads], axis=1
-    )
-    grad_up = over_dp(grad_up, 0).astype(SINGLE)
-    grad_gate = over_dp(grad_gate, 0).astype(SINGLE)
-    grad_down = over_dp(grad_down, 1).astype(SINGLE)
-    rnn_grads = over_dp(rnn_grads, 0)[0].astype(SINGLE)
-    flat_grads = rnn_grads[3 * width :].reshape(-1)
-    gain_grads = lax.psum_scatter(
-        jnp.stack([grad_gain_first, grad_gain_second]).astype(HALF),
-        ("dp", "mp"),
-        scatter_dimension=1,
-        tiled=True,
-    ).astype(SINGLE)
+    rnn_grads = rnn_grads[0].astype(SINGLE)
+    flat_grads = over_dp(small_grads, 0).astype(SINGLE).reshape(-1)
+    gain_grads = jnp.stack([grad_gain_first, grad_gain_second]).reshape(2, -1, bite_gain)
+    gain_grads = jnp.pad(gain_grads.transpose(1, 0, 2), ((0, 0), (0, 6), (0, 128 - bite_gain)))
+    gain_grads = total(gain_grads, 9)
     return (
         layer_output,
         grad_input,
-        gain_grads[0],
-        gain_grads[1],
+        gain_grads[0, :bite_gain],
+        gain_grads[1, :bite_gain],
         rnn_grads[:width].T,
         rnn_grads[width : 2 * width].T,
         rnn_grads[2 * width : 3 * width],
         flat_grads[:size].reshape(heads, bite, block),
         flat_grads[size : 2 * size].reshape(heads, bite, block),
         flat_grads[2 * size : used].reshape(channel_params.shape),
-        grad_gate,
-        grad_up,
-        grad_down,
+        grad_gate.astype(SINGLE),
+        grad_up.astype(SINGLE),
+        grad_down.T.astype(SINGLE),
     )
 
 

time: 957 us -> 655 us (0.68)
  waiting for transfers between devices: 307 us -> 24.1 us
  Pallas kernels: 423 us -> 482 us
  blocking collectives: 43.6 us -> 0 us
  matrix products: 96.6 us -> 73.8 us
  local copies, waits for them, and re-layouts: 29.6 us -> 16.9 us
    reduce_scatter x4 -> x5, waiting for transfers between devices: 255 us -> 10.4 us  [over_dp(): lax.psum_scatter(value.astype(HALF), 'dp', scatter_dimension=dimension, t...]
    unnamed x10 -> x9, waiting for transfers between devices: 52.6 us -> 0.81 us
    pallas_call x0 -> x2, Pallas kernels: none -> 45.9 us  [the longest x1 24.8 us: share(): pl.pallas_call(share_kernel, out_shape=jax.ShapeDtypeStruct((1 << len(bit...]
    all_gather x1 -> x0, blocking collectives: 43.6 us -> none  [on_device(): lax.all_gather(jnp.stack([norm_in, norm_mid]).astype(HALF), ('dp', 'mp'),...]
    dot_general x6 -> x3, matrix products: 54.3 us -> 32.1 us  [dot_tn(): lax.dot_general(left, right, (((0,), (0,)), ((), ())), preferred_element_...]
    all_gather x1, waiting for transfers between devices: 0.01 us -> 12.8 us  [on_device(): down = lax.all_gather(w_mlp_down.astype(HALF), 'dp', axis=1, tiled=True)]
    dot_general x1 -> x0, local copies, waits for them, and re-layouts: 12.6 us -> none  [dot_tn(): lax.dot_general(left, right, (((0,), (0,)), ((), ())), preferred_element_...]
    pallas_call x1, Pallas kernels: 34.4 us -> 47 us  [backward_channels(): pl.pallas_call(backward_kernel, grid=(count,), out_shape=(full(HALF), ful...]
  transfers between devices with their start and end apart: 9 -> 9, of which waited for: 5 -> 3; matrix products, arithmetic and copies ran while one was open for 13% -> 13% of each run, Pallas kernels for 21% -> 74%
where the time goes in v2:
time: 655 us; the launch traced here: 649 us
  Pallas kernels  482 us (74%)
  matrix products  73.8 us (11%)
  other arithmetic  37.5 us (6%)
  waiting for transfers between devices  24.1 us (4%)
  local copies, waits for them, and re-layouts  16.9 us (3%)
  between operations  14.5 us (2%)
    pallas_call x4, Pallas kernels, scatter_products(): pl.pallas_call(functools.partial(scatter_kernel, products, tile), out_sha...  193 us
    pallas_call x4, Pallas kernels, gather_rows(): pl.pallas_call(functools.partial(gather_kernel, count), out_shape=jax.Sha...  161 us
    pallas_call x1, Pallas kernels, backward_channels(): pl.pallas_call(backward_kernel, grid=(count,), out_shape=(full(HALF), ful...  47 us
    pallas_call x1, Pallas kernels, forward_channels(): pl.pallas_call(forward_kernel, grid=(count,), out_shape=(jax.ShapeDtypeSt...  35.5 us
    dot_general x3, matrix products, dot_tn(): lax.dot_general(left, right, (((0,), (0,)), ((), ())), preferred_element_...  32.1 us
    pallas_call x1, Pallas kernels, share(): pl.pallas_call(share_kernel, out_shape=jax.ShapeDtypeStruct((1 << len(bit...  24.8 us
    dot_general x2, matrix products, dot_nn(): lax.dot_general(left, right, (((1,), (0,)), ((), ())), preferred_element_...  23.6 us
    pallas_call x1, Pallas kernels, total(): pl.pallas_call(total_kernel, out_shape=jax.ShapeDtypeStruct(x.shape[1:],...  21.1 us
  transfers between devices with their start and end apart: 9, of which 3 were waited for; matrix products, arithmetic and copies ran while one was open for 13% of the time, Pallas kernels for 74%

profile of v2, /device:TPU:0, one launch (start us, length us, event | category | flops | bytes accessed | tf_op | source)
XLA Modules:
  0.0 649.4 jit_solution(2901457871357513190)
XLA Ops:
  8.0 0.9 convert_element_type.116
  9.0 0.9 convert_element_type.117
  10.1 1.2 convert_element_type.115
  11.4 1.4 convert_bitcast_fusion.1
  12.7 1.0 pad_maximum_fusion
  13.9 1.0 convert_element_type.124
  14.9 1.0 convert_element_type.123
  16.5 1.0 convert_element_type.126
  18.3 24.8 %share.1 = f32[32,8,128]{2,1,0:T(8,128)} custom-call(f32[8,128]{1,0:T(8,128)} %fusion.23.x_ref), custom_call_target="tpu_custom_call" | custom-call | tf_op jit(solution)/shard_map/share/pallas_call | solution.py:103
  43.0 1.1 slice_reduce_fusion
  44.8 39.7 %gather_rows.6 = bf16[8,256,2048]{2,1,0:T(8,128)(2,1)} custom-call(bf16[256,2048]{1,0:T(8,128)(2,1)} %x_ref.3), custom_call_target="tpu_custom_call" | custom-call | bytes 67108864 | tf_op jit(solution)/shard_map/gather_rows/pallas_call | solution.py:229
  84.5 41.7 %gather_rows.4.x_ref = bf16[8,256,2048]{2,1,0:T(8,128)(2,1)} custom-call(bf16[256,2048]{1,0:T(8,128)(2,1)} %x_ref.2), custom_call_target="tpu_custom_call" | custom-call | bytes 67108864 | tf_op jit(solution)/shard_map/gather_rows/pallas_call | solution.py:229
  126.3 1.0 slice_bitcast_fusion.3
  128.8 0.9 mul.252.ba_ref
  129.7 0.9 mul.248.bin_ref
  131.3 35.5 %forward_channels.1 = (bf16[2048,2048]{1,0:T(8,128)(2,1)}, bf16[2048,320]{1,0:T(8,128)(2,1)}, f32[2048,320]{1,0:T(8,128)}, f32[2048,320]{1,0:T(8,128)}, f32[2048...) custom-call(s32[1,3]{1,0:T(1,128)} %lens_ref.3, ...), custom_call_target="tpu_custom_call" | custom-call | flops 5368709120 | bytes 32505856 | tf_op jit(solution)/shard_map/forward_channels/pallas_call | solution.py:546
  166.8 45.5 %scatter_products.4 = f32[256,2048]{1,0:T(8,128)} custom-call(bf16[2048,320]{1,0:T(8,128)(2,1)} %get-tuple-element.43.refs_0_.ob_ref, bf16[4,1024,512]{2,1,0:T(8,128)(2,1)} %bitcast.86), custom_call_target="tpu_custom_call" | custom-call | flops 2684354560 | bytes 67108864 | tf_op jit(solution)/shard_map/scatter_products/pallas_call | solution.py:385
  212.3 2.1 multiply_reduce_fusion.2
  214.4 1.2 multiply_convert_fusion.3.x_ref
  215.6 40.4 %gather_rows.5 = bf16[8,256,2048]{2,1,0:T(8,128)(2,1)} custom-call(bf16[256,2048]{1,0:T(8,128)(2,1)} %multiply_convert_fusion.3.x_ref), custom_call_target="tpu_custom_call" | custom-call | bytes 67108864 | tf_op jit(solution)/shard_map/gather_rows/pallas_call | solution.py:229
  256.0 11.8 %fusion.30 = f32[2048,768]{1,0:T(8,128)} fusion(bf16[2048,2048]{1,0:T(8,128)(2,1)} %bitcast.80, bf16[2048,768]{1,0:T(8,128)(2,1)} %all-gather.8.cloned.1.call-done.refs_3_), kind=kOutput, calls=%fused_computation.87 | convolution fusion | flops 6442450944 | bytes 17825792 | tf_op jit(solution)/shard_map/dot_general | solution.py:22
  267.8 11.8 %fusion.29 = f32[2048,768]{1,0:T(8,128)} fusion(bf16[2048,2048]{1,0:T(8,128)(2,1)} %bitcast.81, bf16[2048,768]{1,0:T(8,128)(2,1)} %all-gather.6.cloned.1.call-done.refs_2_), kind=kOutput, calls=%fused_computation.86 | convolution fusion | flops 6442450944 | bytes 17825792 | tf_op jit(solution)/shard_map/dot_general | solution.py:22
  279.6 12.8 %all-gather.10.cloned.1.call-done.refs_1_ = bf16[768,2048]{1,0:T(8,128)(2,1)} async-done(((bf16[768,512]{1,0:T(8,128)(2,1)}), bf16[768,2048]{1,0:T(8,128)(2,1)}) %all-gather.10.cloned.1.call-update) | async-done | bytes 3145744 | tf_op jit(solution)/shard_map/all_gather | solution.py:834
  292.4 18.1 %multiply_convert_fusion = (bf16[2048,768]{1,0:T(8,128)(2,1)S(1)}, bf16[2048,768]{1,0:T(8,128)(2,1)}, bf16[2048,768]{1,0:T(8,128)(2,1)}) fusion(f32[2048,768]{1,0:T(8,128)} %fusion.29, f32[2048,768]{1,0:T(8,128)} %fusion.30, bf16[2048,2048]{1,0:T(8,128)(2,1)} %bitcast.78, bf16[768,2048]{1,0:T(8,128)(2,1)} %all-gather.10.cloned.1.call-done.refs_1_), kind=kOutput, calls=%fused_computation | convolution fusion | flops 6480199680 | bytes 33554432 | tf_op jit(solution)/shard_map/dot_general | solution.py:28
  310.5 1.6 copy-done.12
  312.2 10.4 %convolution_convert_fusion.1 = bf16[2048,768]{1,0:T(8,128)(2,1)} fusion(bf16[2048,2048]{1,0:T(8,128)(2,1)} %bitcast.82, bf16[2048,768]{1,0:T(8,128)(2,1)S(1)} %get-tuple-element.83.refs_1_), kind=kOutput, calls=%fused_computation.11 | convolution fusion | flops 6444023808 | bytes 14680064 | tf_op jit(solution)/shard_map/dot_general | solution.py:34
  322.6 11.4 %convolution_convert_fusion.2 = bf16[2048,768]{1,0:T(8,128)(2,1)} fusion(bf16[2048,2048]{1,0:T(8,128)(2,1)} %bitcast.83, bf16[2048,768]{1,0:T(8,128)(2,1)} %get-tuple-element.44.refs_0_), kind=kOutput, calls=%fused_computation.12 | convolution fusion | flops 6444023808 | bytes 14680064 | tf_op jit(solution)/shard_map/dot_general | solution.py:34
  334.1 51.8 %scatter_products.5 = f32[256,2048]{1,0:T(8,128)} custom-call(bf16[2048,768]{1,0:T(8,128)(2,1)} %get-tuple-element.44.refs_0_, bf16[2048,768]{1,0:T(8,128)(2,1)} %copy-done.12, bf16[2048,768]{1,0:T(8,128)(2,1)} %all-gather.6.cloned.1.call-done.refs_2_, bf16[2048,768]{1,0:T(8,128)(2,1)} %all-gather.8.cloned.1.call-done.refs_3_), custom_call_target="tpu_custom_call" | custom-call | flops 12884901888 | bytes 67108864 | tf_op jit(solution)/shard_map/scatter_products/pallas_call | solution.py:385
  385.9 10.3 %fusion = bf16[2048,768]{0,1:T(8,128)(2,1)} fusion(bf16[2048,768]{1,0:T(8,128)(2,1)S(1)} %copy-done.11, bf16[2048,2048]{1,0:T(8,128)(2,1)} %bitcast.79), kind=kOutput, calls=%fused_computation.13 | convolution fusion | flops 6444023808 | bytes 14680064 | tf_op jit(solution)/shard_map/dot_general | solution.py:34
  396.3 2.3 multiply_reduce_fusion
  398.9 2.3 fusion.24
  401.2 39.6 %gather_rows.7.dt_ref = bf16[8,256,2048]{2,1,0:T(8,128)(2,1)} custom-call(bf16[256,2048]{1,0:T(8,128)(2,1)} %get-tuple-element.48.x_ref), custom_call_target="tpu_custom_call" | custom-call | bytes 67108864 | tf_op jit(solution)/shard_map/gather_rows/pallas_call | solution.py:229
  440.8 3.4 reduce-scatter.8.cloned.1.call-done
  444.2 47.0 %backward_channels.1 = (bf16[2048,320]{1,0:T(8,128)(2,1)}, bf16[2048,320]{1,0:T(8,128)(2,1)}, f32[320,320]{1,0:T(8,128)}, f32[320,320]{1,0:T(8,128)}, f32[8,320]{1,0:T(8,128)}, /*index=5*/bf16[4,960,512]{2,1,0:T(8,128)(2,1)}) custom-call(s32[1,3]{1,0:T(1,128)} %lens_ref.3, bf16[8,256,2048]{2,1,0:T(8,128)(2,1)} %gather_rows.7.dt_ref, ...), custom_call_target="tpu_custom_call" | custom-call | flops 2684354560 | bytes 26738688 | tf_op jit(solution)/shard_map/backward_channels/pallas_call | solution.py:733
  492.7 1.1 convert.47
  494.2 1.1 convert.48
  497.4 2.4 convert_element_type.140
  499.8 7.0 %reduce-scatter.10.cloned.1.call-done = bf16[512,768]{0,1:T(8,128)(2,1)} async-done(((bf16[2048,768]{0,1:T(8,128)(2,1)}), bf16[512,768]{0,1:T(8,128)(2,1)}) %reduce-scatter.10.cloned.1.call-update) | async-done | bytes 786448 | tf_op jit(solution)/shard_map/reduce_scatter | solution.py:878
  506.8 48.9 %scatter_products.6 = f32[256,2048]{1,0:T(8,128)} custom-call(bf16[2048,320]{1,0:T(8,128)(2,1)} %get-tuple-element.60.refs_0_, bf16[2048,320]{1,0:T(8,128)(2,1)} %get-tuple-element.61.refs_1_, bf16[4,1024,512]{2,1,0:T(8,128)(2,1)} %bitcast.88, bf16[4,1024,512]{2,1,0:T(8,128)(2,1)} %bitcast.89), custom_call_target="tpu_custom_call" | custom-call | flops 5368709120 | bytes 67108864 | tf_op jit(solution)/shard_map/scatter_products/pallas_call | solution.py:385
  555.6 2.1 fusion.6
  558.6 21.1 %total.1 = f32[8,128]{1,0:T(8,128)} custom-call(f32[32,8,128]{2,1,0:T(8,128)} %pad.22.x_ref), custom_call_target="tpu_custom_call" | custom-call | tf_op jit(solution)/shard_map/total/pallas_call | solution.py:148
  579.7 2.4 convert_element_type.139
  582.1 1.3 slice_bitcast_fusion.4
  583.4 2.5 convert_bitcast_fusion
  585.9 46.5 %scatter_products.7 = f32[256,2048]{1,0:T(8,128)} custom-call(bf16[2048,768]{1,0:T(8,128)(2,1)} %get-tuple-element.62.refs_0_, bf16[768,2048]{1,0:T(8,128)(2,1)} %all-gather.10.cloned.1.call-done.refs_1_), custom_call_target="tpu_custom_call" | custom-call | flops 6442450944 | bytes 67108864 | tf_op jit(solution)/shard_map/scatter_products/pallas_call | solution.py:385
  632.4 1.9 fusion.3
  638.1 2.9 add_convert_fusion
  641.3 1.3 slice_bitcast_fusion
  (102 shorter events, 14.9 us)
Async XLA Ops:
  7.2 119.1 %all-gather.12.cloned.1.call-start = ((), (), s32[]{:S(2)}) async-start(), calls=%async_computation.13 | async-start | bytes 5242880 | tf_op jit(solution)/shard_map/all_gather | solution.py:833
  10.0 3.8 copy-start.5
  12.7 2.2 copy-start.6
  13.8 242.2 %all-gather.8.cloned.1.call-start = ((), (), s32[]{:S(2)}) async-start(), calls=%async_computation.6 | async-start | bytes 3932160 | tf_op jit(solution)/shard_map/all_gather | solution.py:836
  14.8 1.7 copy-start.7
  14.9 2.8 copy-start.9
  14.9 2.8 copy-start.10
  14.9 252.9 %all-gather.6.cloned.1.call-start = ((), (), s32[]{:S(2)}) async-start(), calls=%async_computation.5 | async-start | bytes 3932160 | tf_op jit(solution)/shard_map/all_gather | solution.py:835
  15.9 276.5 %all-gather.10.cloned.1.call-start = ((), (), s32[]{:S(2)}) async-start(), calls=%async_computation.7 | async-start | bytes 3932160 | tf_op jit(solution)/shard_map/all_gather | solution.py:834
  17.6 383.6 %reduce-scatter.6.cloned.1.call-start = ((), (), s32[]{:S(2)}) async-start(), calls=%async_computation.8 | async-start | bytes 3932160 | tf_op jit(solution)/shard_map/reduce_scatter | solution.py:878
  166.8 45.5 %copy-start = (bf16[256,2048]{1,0:T(8,128)(2,1)S(1)}, bf16[256,2048]{1,0:T(8,128)(2,1)}, u32[]{:S(2)}) copy-start(bf16[256,2048]{1,0:T(8,128)(2,1)} %x_ref.2) | copy-start | bytes 3145732
  310.5 1.6 copy-start.12
  322.6 121.6 %reduce-scatter.8.cloned.1.call-start = ((), (), s32[]{:S(2)}) async-start(), calls=%async_computation.9 | async-start | bytes 3932160 | tf_op jit(solution)/shard_map/reduce_scatter | solution.py:878
  334.0 172.7 %reduce-scatter.10.cloned.1.call-start = ((), (), s32[]{:S(2)}) async-start(), calls=%async_computation.10 | async-start | bytes 3932160 | tf_op jit(solution)/shard_map/reduce_scatter | solution.py:878
  334.1 51.8 %copy-start.11 = (bf16[2048,768]{1,0:T(8,128)(2,1)S(1)}, bf16[2048,768]{1,0:T(8,128)(2,1)}, u32[]{:S(2)}) copy-start(bf16[2048,768]{1,0:T(8,128)(2,1)} %get-tuple-element.62.refs_0_) | copy-start | bytes 9437188
  396.3 238.0 %reduce-scatter.14.cloned.1.call-start = ((), (), s32[]{:S(2)}) async-start(), calls=%async_computation.12 | async-start | bytes 327680 | tf_op jit(solution)/shard_map/reduce_scatter | solution.py:878
  396.3 2.4 copy-start.3
  396.3 2.6 copy-start.4
  496.5 141.7 %reduce-scatter.12.cloned.1.call-start = ((), (), s32[]{:S(2)}) async-start(), calls=%async_computation.11 | async-start | bytes 4915200 | tf_op jit(solution)/shard_map/reduce_scatter | solution.py:878
  585.9 46.5 %copy-start.1 = (f32[256,2048]{1,0:T(8,128)S(1)}, f32[256,2048]{1,0:T(8,128)}, u32[]{:S(2)}) copy-start(f32[256,2048]{1,0:T(8,128)} %scatter_products.6) | copy-start | bytes 6291460
  585.9 46.5 %copy-start.2 = (f32[256,2048]{1,0:T(8,128)S(1)}, f32[256,2048]{1,0:T(8,128)}, u32[]{:S(2)}) copy-start(f32[256,2048]{1,0:T(8,128)} %get-tuple-element.80) | copy-start | bytes 6291460
  638.1 2.9 copy-start.8
Sparse Core Ops, SparseCore 0:
  13.9 86.1 all-gather.11
  102.3 61.9 all-gather.7
  166.4 62.2 all-gather.5
  230.2 62.1 all-gather.9
  322.7 58.9 reduce-scatter.5
  383.8 60.2 reduce-scatter.7
  446.5 60.2 reduce-scatter.9
  509.6 19.7 reduce-scatter.13
  531.8 72.9 reduce-scatter.11

commit v3 on v2

--- a/solution.py
+++ b/solution.py
@@ -58,109 +58,111 @@
     return place
 
 
-def all_bits():
-    inner, outer = lax.axis_size("mp"), lax.axis_size("dp")
-    bits = [(1 << b, "mp", 1 << b) for b in range(inner.bit_length() - 1)]
-    return bits + [(inner << b, "dp", 1 << b) for b in range(outer.bit_length() - 1)]
-
-
-def across(axis, bit):
-    return {axis: flip(lax.axis_index(axis), bit, 2 * bit)}
-
-
-def greet(bits):
+def ring_peers(axis):
+    me, count = lax.axis_index(axis), lax.axis_size(axis)
+    return [(k, {axis: (me + k) % count}) for k in range(1, count)]
+
+
+def greet(peers):
     barrier = pltpu.get_barrier_semaphore()
-    for _, axis, bit in bits:
-        pl.semaphore_signal(barrier, inc=1, device_id=across(axis, bit), device_id_type=MESH)
-    pl.semaphore_wait(barrier, len(bits))
-
-
-def share_kernel(x_ref, o_ref, send, recv):
-    bits = all_bits()
-    place = lax.axis_index("dp") * lax.axis_size("mp") + lax.axis_index("mp")
-    o_ref[place] = x_ref[...]
-    greet(bits)
+    for _, peer in peers:
+        pl.semaphore_signal(barrier, inc=1, device_id=peer, device_id_type=MESH)
+    pl.semaphore_wait(barrier, len(peers))
+
+
+def exchange(peers, source, target, send, recv):
     copies = []
-    for j, (size, axis, bit) in enumerate(bits):
-        window = o_ref.at[pl.ds(place // size * size, size)]
+    for k, peer in peers:
         copy = pltpu.make_async_remote_copy(
-            src_ref=window,
-            dst_ref=window,
-            send_sem=send.at[j],
-            recv_sem=recv.at[j],
-            device_id=across(axis, bit),
+            src_ref=source(k),
+            dst_ref=target(k),
+            send_sem=send.at[k],
+            recv_sem=recv.at[k],
+            device_id=peer,
             device_id_type=MESH,
         )
         copy.start()
-        copy.wait_recv()
         copies.append(copy)
     for copy in copies:
+        copy.wait_recv()
+    return copies
+
+
+def share_kernel(x_ref, o_ref, send_mp, recv_mp, send_dp, recv_dp):
+    inner, outer = ring_peers("mp"), ring_peers("dp")
+    count = len(inner) + 1
+    first = lax.axis_index("dp") * count
+    place = first + lax.axis_index("mp")
+    o_ref[place] = x_ref[...]
+    greet(inner + outer)
+    mine = lambda k: o_ref.at[place]
+    plane = lambda k: o_ref.at[pl.ds(first, count)]
+    copies = exchange(inner, mine, mine, send_mp, recv_mp)
+    copies += exchange(outer, plane, plane, send_dp, recv_dp)
+    for copy in copies:
         copy.wait_send()
 
 
-def share(x, collective_id):
-    bits = all_bits()
+def small_call(kernel, x, out_shape, scratch, collective_id, name):
+    inner, outer = lax.axis_size("mp"), lax.axis_size("dp")
+    sems = [pltpu.SemaphoreType.DMA((c,)) for c in (inner, inner, outer, outer)]
     return pl.pallas_call(
-        share_kernel,
-        out_shape=jax.ShapeDtypeStruct((1 << len(bits),) + x.shape, x.dtype),
+        kernel,
+        out_shape=jax.ShapeDtypeStruct(out_shape, x.dtype),
         in_specs=[pl.BlockSpec(memory_space=pltpu.VMEM)],
         out_specs=pl.BlockSpec(memory_space=pltpu.VMEM),
-        scratch_shapes=[
-            pltpu.SemaphoreType.DMA((len(bits),)),
-            pltpu.SemaphoreType.DMA((len(bits),)),
-        ],
+        scratch_shapes=scratch + sems,
         compiler_params=pltpu.CompilerParams(
             collective_id=collective_id, has_side_effects=True
         ),
-        name="share",
+        name=name,
     )(x)
 
 
-def total_kernel(x_ref, o_ref, kept, landed, send, recv):
-    bits = all_bits()
-    place = lax.axis_index("dp") * lax.axis_size("mp") + lax.axis_index("mp")
-    kept[...] = x_ref[...]
-    greet(bits)
-    copies = []
-    for j, (size, axis, bit) in reversed(list(enumerate(bits))):
-        first = place // size * size
-        other = first + (1 - 2 * ((place // size) % 2)) * size
-        copy = pltpu.make_async_remote_copy(
-            src_ref=kept.at[pl.ds(other, size)],
-            dst_ref=landed.at[pl.ds(size, size)],
-            send_sem=send.at[j],
-            recv_sem=recv.at[j],
-            device_id=across(axis, bit),
-            device_id_type=MESH,
-        )
-        copy.start()
-        copy.wait_recv()
-        mine = pl.ds(first, size)
-        kept[mine] = kept[mine] + landed[size : 2 * size]
-        copies.append(copy)
-    o_ref[...] = kept[place]
+def share(x, collective_id):
+    devices = lax.axis_size("mp") * lax.axis_size("dp")
+    return small_call(share_kernel, x, (devices,) + x.shape, [], collective_id, "share")
+
+
+def total_kernel(x_ref, o_ref, plane, landed_mp, landed_dp, send_mp, recv_mp, send_dp, recv_dp):
+    inner, outer = ring_peers("mp"), ring_peers("dp")
+    across, count = len(outer) + 1, len(inner) + 1
+    me, level = lax.axis_index("mp"), lax.axis_index("dp")
+    greet(inner + outer)
+    copies = exchange(
+        outer,
+        lambda k: x_ref.at[pl.ds((level + k) % across * count, count)],
+        lambda k: landed_dp.at[k],
+        send_dp,
+        recv_dp,
+    )
+    plane[...] = x_ref[pl.ds(level * count, count)]
+    for k, _ in outer:
+        plane[...] = plane[...] + landed_dp[k]
+    copies += exchange(
+        inner,
+        lambda k: plane.at[(me + k) % count],
+        lambda k: landed_mp.at[k],
+        send_mp,
+        recv_mp,
+    )
+    value = plane[me]
+    for k, _ in inner:
+        value = value + landed_mp[k]
+    o_ref[...] = value
     for copy in copies:
         copy.wait_send()
 
 
 def total(x, collective_id):
-    bits = all_bits()
-    return pl.pallas_call(
-        total_kernel,
-        out_shape=jax.ShapeDtypeStruct(x.shape[1:], x.dtype),
-        in_specs=[pl.BlockSpec(memory_space=pltpu.VMEM)],
-        out_specs=pl.BlockSpec(memory_space=pltpu.VMEM),
-        scratch_shapes=[
-            pltpu.VMEM(x.shape, x.dtype),
-            pltpu.VMEM(x.shape, x.dtype),
-            pltpu.SemaphoreType.DMA((len(bits),)),
-            pltpu.SemaphoreType.DMA((len(bits),)),
-        ],
-        compiler_params=pltpu.CompilerParams(
-            collective_id=collective_id, has_side_effects=True
-        ),
-        name="total",
-    )(x)
+    inner, outer = lax.axis_size("mp"), lax.axis_size("dp")
+    tile = x.shape[1:]
+    scratch = [
+        pltpu.VMEM((inner,) + tile, x.dtype),
+        pltpu.VMEM((inner,) + tile, x.dtype),
+        pltpu.VMEM((outer, inner) + tile, x.dtype),
+    ]
+    return small_call(total_kernel, x, tile, scratch, collective_id, "total")
 
 
 def gather_plan(count):
@@ -246,13 +248,33 @@
     )(x)
 
 
-def scatter_kernel(products, tile, *refs):
+def beside_products(pairs):
+    for left, right, out in pairs:
+        tokens, rows = left.shape
+        tile = min(256, rows)
+
+        def body(left_tile, out_tile):
+            out_tile[...] = dot_tn(left_tile[...], right[...]).astype(out_tile.dtype)
+
+        pltpu.emit_pipeline(
+            body,
+            grid=(rows // tile,),
+            in_specs=[pl.BlockSpec((tokens, tile), lambda i: (0, i))],
+            out_specs=[pl.BlockSpec((tile, right.shape[1]), lambda i: (i, 0))],
+        )(left, out)
+
+
+def scatter_kernel(products, tile, extra, *refs):
     count = 8
     pairs = len(products)
-    lefts, rights = refs[:pairs], refs[pairs : 2 * pairs]
-    out_ref = refs[2 * pairs]
-    acc, core_out, core_in, link_out, link_in = refs[2 * pairs + 1 : 2 * pairs + 6]
-    core_send, core_recv, link_send, link_recv = refs[2 * pairs + 6 :]
+    refs = list(refs)
+    take = lambda n: [refs.pop(0) for _ in range(n)]
+    lefts, rights = take(pairs), take(pairs)
+    beside = take(2 * extra)
+    (out_ref,) = take(1)
+    beside_out = take(extra)
+    acc, core_out, core_in, link_out, link_in = take(5)
+    core_send, core_recv, link_send, link_recv = refs
     rows, width = out_ref.shape
     me = lax.axis_index("mp")
     start_barrier((1, 2, 4), count)
@@ -363,6 +385,7 @@
     link(4, 1, 0, 1)
     link_sum(1, 2, 1)
     link(5, 2, 1, 2)
+    beside_products(list(zip(beside[:extra], beside[extra:], beside_out)))
     link_sum(2, 0, 1)
     link_sum(3, 0, 0)
     link_sum(4, 0, 0)
@@ -374,19 +397,27 @@
         copy.wait_send()
 
 
-def scatter_products(lefts, rights, products, fallback, width, tile, collective_id, flops):
+def scatter_products(
+    lefts, rights, products, fallback, width, tile, collective_id, flops, beside=()
+):
     count = lax.axis_size("mp")
     tokens = lefts[0].shape[0]
     rows = tokens // count
     if count != 8:
-        return lax.psum_scatter(
+        summed = lax.psum_scatter(
             fallback().astype(HALF), "mp", scatter_dimension=0, tiled=True
         ).astype(SINGLE)
+        return [summed] + [dot_tn(left, right).astype(HALF) for left, right in beside]
+    extra = len(beside)
+    in_vmem, in_hbm = pl.BlockSpec(memory_space=pltpu.VMEM), pl.BlockSpec(memory_space=pl.ANY)
     return pl.pallas_call(
-        functools.partial(scatter_kernel, products, tile),
-        out_shape=jax.ShapeDtypeStruct((rows, width), SINGLE),
-        in_specs=[pl.BlockSpec(memory_space=pltpu.VMEM)] * (len(lefts) + len(rights)),
-        out_specs=pl.BlockSpec(memory_space=pltpu.VMEM),
+        functools.partial(scatter_kernel, products, tile, extra),
+        out_shape=[jax.ShapeDtypeStruct((rows, width), SINGLE)]
+        + [
+            jax.ShapeDtypeStruct((left.shape[1], right.shape[1]), HALF) for left, right in beside
+        ],
+        in_specs=[in_vmem] * (len(lefts) + len(rights)) + [in_hbm] * extra + [in_vmem] * extra,
+        out_specs=[in_vmem] + [in_hbm] * extra,
         scratch_shapes=[
             pltpu.VMEM((4, rows, width), SINGLE),
             pltpu.VMEM((4, rows, width), HALF),
@@ -405,7 +436,7 @@
             flops=flops, bytes_accessed=tokens * width * 2 * 8, transcendentals=0
         ),
         name="scatter_products",
-    )(*lefts, *rights)
+    )(*lefts, *rights, *[pair[0] for pair in beside], *[pair[1] for pair in beside])
 
 
 def positions(lens_ref, first, shape):
@@ -857,7 +888,7 @@
         lengths, x_all, gain_first, pack, blocks_in, blocks_a, chan
     )
     inputs = layer_input.astype(SINGLE)
-    out = scatter_products(
+    (out,) = scatter_products(
         [ob],
         [pack],
         [lambda l, r, t, cols: dot_nn(l, r[t, 2 * width : 3 * width, :])],
@@ -883,16 +914,15 @@
     gate_pre = dot_nn(n2, gate_w)
     act, slope = gelu_both(gate_pre)
     d_up = (d_hidden * act).astype(HALF)
-    grad_up = over_dp(dot_tn(n2, d_up), 0)
+    grad_up = dot_tn(n2, d_up).astype(HALF)
+    up_w, grad_up = lax.optimization_barrier((up_w, grad_up))
+    grad_up = over_dp(grad_up, 0)
     up_pre = dot_nn(n2, up_w)
     hidden = (act * up_pre).astype(HALF)
     d_gate = (d_hidden * up_pre * slope).astype(HALF)
-    grad_gate = dot_tn(n2, d_gate).astype(HALF)
-    d_gate, grad_gate = lax.optimization_barrier((d_gate, grad_gate))
-    grad_gate = over_dp(grad_gate, 0)
     tile = 512
     by_rows = lambda l, r, t, cols: dot_nt(l, r[cols, :])
-    d_normed_mid = scatter_products(
+    d_normed_mid, grad_gate, grad_down = scatter_products(
         [d_gate, d_up],
         [gate_w, up_w],
         [by_rows, by_rows],
@@ -901,10 +931,9 @@
         tile,
         4,
         4 * tokens * model * up_w.shape[1],
-    )
-    hidden, d_normed_mid = lax.optimization_barrier((hidden, d_normed_mid))
-    grad_down = dot_tn(c_all, hidden).astype(HALF)
-    d_normed_mid, grad_down = lax.optimization_barrier((d_normed_mid, grad_down))
+        [(n2, d_gate), (c_all, hidden)],
+    )
+    grad_gate = over_dp(grad_gate, 0)
     grad_down = over_dp(grad_down, 0)
 
     weighted_second = gain_second * d_normed_mid
@@ -924,7 +953,7 @@
         lengths, dt_all, pack, blocks_in, blocks_a, chan, saved
     )
     d_bx, grad_down = lax.optimization_barrier((d_bx, grad_down))
-    d_normed = scatter_products(
+    (d_normed,) = scatter_products(
         [d_bx, d_by],
         [pack, pack],
         [
@@ -942,9 +971,20 @@
         7,
         4 * tokens * width * model,
     )
-    rnn_grads = over_dp(rnn_grads, 0)
+    own = lambda full: jnp.stack(
+        [full[j * block : (j + 1) * block, j * block : (j + 1) * block] for j in range(heads)]
+    )
+    decay_row = DECAY * jax.nn.sigmoid(-channel[2 * CONV - 1 :]) * gchan[2 * CONV - 1 :]
+    grad_channel = jnp.concatenate([gchan[: 2 * CONV - 1], decay_row], axis=0)
+    split = lambda v: v.reshape(heads, parts, bite, block).transpose(1, 0, 2, 3).reshape(parts, -1)
+    small_grads = jnp.concatenate(
+        [split(own(gin)), split(own(ga)), grad_channel.reshape(parts, -1)], axis=1
+    )
+    small_grads = jnp.pad(small_grads, ((0, 0), (0, small_rows * depth - used)))
+    small_grads = small_grads.reshape(parts, small_rows, depth).astype(HALF)
+    rnn_grads = over_dp(jnp.concatenate([rnn_grads, small_grads], axis=1), 0)
     hidden, d_normed = lax.optimization_barrier((hidden, d_normed))
-    mlp_out = scatter_products(
+    (mlp_out,) = scatter_products(
         [hidden],
         [down],
         [lambda l, r, t, cols: dot_nn(l, r[:, cols])],
@@ -967,19 +1007,8 @@
         - inputs * cube_first * jnp.mean(weighted_first * inputs, axis=-1, keepdims=True)
     )
 
-    own = lambda full: jnp.stack(
-        [full[j * block : (j + 1) * block, j * block : (j + 1) * block] for j in range(heads)]
-    )
-    decay_row = DECAY * jax.nn.sigmoid(-channel[2 * CONV - 1 :]) * gchan[2 * CONV - 1 :]
-    grad_channel = jnp.concatenate([gchan[: 2 * CONV - 1], decay_row], axis=0)
-    split = lambda v: v.reshape(heads, parts, bite, block).transpose(1, 0, 2, 3).reshape(parts, -1)
-    small_grads = jnp.concatenate(
-        [split(own(gin)), split(own(ga)), grad_channel.reshape(parts, -1)], axis=1
-    )
-    small_grads = jnp.pad(small_grads, ((0, 0), (0, small_rows * depth - used)))
-    small_grads = small_grads.reshape(parts, small_rows, depth)
     rnn_grads = rnn_grads[0].astype(SINGLE)
-    flat_grads = over_dp(small_grads, 0).astype(SINGLE).reshape(-1)
+    flat_grads = rnn_grads[3 * width :].reshape(-1)
     gain_grads = jnp.stack([grad_gain_first, grad_gain_second]).reshape(2, -1, bite_gain)
     gain_grads = jnp.pad(gain_grads.transpose(1, 0, 2), ((0, 0), (0, 6), (0, 128 - bite_gain)))
     gain_grads = total(gain_grads, 9)

time: 655 us -> 630 us (0.962)
  matrix products: 73.8 us -> 51.9 us
  Pallas kernels: 482 us -> 474 us
    dot_general x3 -> x1, matrix products: 32.1 us -> 8.91 us  [dot_tn(): lax.dot_general(left, right, (((0,), (0,)), ((), ())), preferred_element_...]
    all_gather x1, waiting for transfers between devices: 12.8 us -> 0.01 us  [on_device(): down = lax.all_gather(w_mlp_down.astype(HALF), 'dp', axis=1, tiled=True)]
    pallas_call x6, Pallas kernels: 238 us -> 230 us  [the longest x4 196 us: scatter_products(): pl.pallas_call(functools.partial(scatter_kernel, products, tile, extra),...]
    all_gather x1, waiting for transfers between devices: 0.02 us -> 7.68 us  [on_device(): up_w = lax.all_gather(w_mlp_up.astype(HALF), 'dp', axis=0, tiled=True)]
    reduce_scatter x5 -> x4, waiting for transfers between devices: 10.4 us -> 16.4 us  [over_dp(): lax.psum_scatter(value.astype(HALF), 'dp', scatter_dimension=dimension, t...]
  transfers between devices with their start and end apart: 9 -> 8, of which waited for: 3 -> 3; matrix products, arithmetic and copies ran while one was open for 13% -> 15% of each run, Pallas kernels for 74% -> 76%
where the time goes in v3:
time: 630 us; the launch traced here: 625 us
  Pallas kernels  474 us (75%)
  matrix products  51.9 us (8%)
  other arithmetic  40.5 us (6%)
  waiting for transfers between devices  25 us (4%)
  local copies, waits for them, and re-layouts  19.2 us (3%)
  between operations  14.8 us (2%)
    pallas_call x4, Pallas kernels, scatter_products(): pl.pallas_call(functools.partial(scatter_kernel, products, tile, extra),...  196 us
    pallas_call x4, Pallas kernels, gather_rows(): pl.pallas_call(functools.partial(gather_kernel, count), out_shape=jax.Sha...  161 us
    pallas_call x1, Pallas kernels, backward_channels(): pl.pallas_call(backward_kernel, grid=(count,), out_shape=(full(HALF), ful...  47 us
    pallas_call x1, Pallas kernels, forward_channels(): pl.pallas_call(forward_kernel, grid=(count,), out_shape=(jax.ShapeDtypeSt...  35.5 us
    pallas_call x2, Pallas kernels, small_call(): pl.pallas_call(kernel, out_shape=jax.ShapeDtypeStruct(out_shape, x.dtype)...  33.6 us
    dot_general x2, matrix products, dot_nn(): lax.dot_general(left, right, (((1,), (0,)), ((), ())), preferred_element_...  29.3 us
    reduce_scatter x4, waiting for transfers between devices, over_dp(): lax.psum_scatter(value.astype(HALF), 'dp', scatter_dimension=dimension, t...  16.4 us
    dot_general x1, matrix products, dot_nt(): lax.dot_general(left, right, (((1,), (1,)), ((), ())), preferred_element_...  13.6 us
  transfers between devices with their start and end apart: 8, of which 3 were waited for; matrix products, arithmetic and copies ran while one was open for 15% of the time, Pallas kernels for 76%

profile of v3, /device:TPU:0, one launch (start us, length us, event | category | flops | bytes accessed | tf_op | source)
XLA Modules:
  0.0 625.3 jit_solution(17020368584337939812)
XLA Ops:
  8.0 0.9 convert_element_type.104
  9.0 0.9 convert_element_type.105
  10.1 1.2 convert_element_type.103
  11.4 1.4 convert_bitcast_fusion.1
  12.7 1.0 pad_maximum_fusion.1
  13.9 1.0 convert_element_type.111
  14.9 1.0 convert_element_type.113
  16.5 1.0 convert_element_type.112
  18.2 17.7 %share.1 = f32[32,8,128]{2,1,0:T(8,128)} custom-call(f32[8,128]{1,0:T(8,128)} %fusion.22.x_ref), custom_call_target="tpu_custom_call" | custom-call | tf_op jit(solution)/shard_map/share/pallas_call | solution.py:109
  35.9 1.1 slice_reduce_fusion
  37.8 40.5 %gather_rows.6 = bf16[8,256,2048]{2,1,0:T(8,128)(2,1)} custom-call(bf16[256,2048]{1,0:T(8,128)(2,1)} %x_ref.3), custom_call_target="tpu_custom_call" | custom-call | bytes 67108864 | tf_op jit(solution)/shard_map/gather_rows/pallas_call | solution.py:231
  78.3 40.3 %gather_rows.4.x_ref = bf16[8,256,2048]{2,1,0:T(8,128)(2,1)} custom-call(bf16[256,2048]{1,0:T(8,128)(2,1)} %x_ref.2), custom_call_target="tpu_custom_call" | custom-call | bytes 67108864 | tf_op jit(solution)/shard_map/gather_rows/pallas_call | solution.py:231
  118.7 1.0 slice_bitcast_fusion.3
  122.1 0.9 mul.248.bin_ref
  123.7 35.5 %forward_channels.1 = (bf16[2048,2048]{1,0:T(8,128)(2,1)}, bf16[2048,320]{1,0:T(8,128)(2,1)}, f32[2048,320]{1,0:T(8,128)}, f32[2048,320]{1,0:T(8,128)}, f32[2048...) custom-call(s32[1,3]{1,0:T(1,128)} %lens_ref.3, ...), custom_call_target="tpu_custom_call" | custom-call | flops 5368709120 | bytes 32505856 | tf_op jit(solution)/shard_map/forward_channels/pallas_call | solution.py:577
  159.2 45.6 %scatter_products.4 = f32[256,2048]{1,0:T(8,128)} custom-call(bf16[2048,320]{1,0:T(8,128)(2,1)} %get-tuple-element.42.refs_0_.ob_ref, bf16[4,1024,512]{2,1,0:T(8,128)(2,1)} %bitcast.72), custom_call_target="tpu_custom_call" | custom-call | flops 2684354560 | bytes 67108864 | tf_op jit(solution)/shard_map/scatter_products/pallas_call | solution.py:413
  204.7 2.1 multiply_reduce_fusion.2
  206.9 1.2 multiply_convert_fusion.3.x_ref
  208.1 40.5 %gather_rows.5 = bf16[8,256,2048]{2,1,0:T(8,128)(2,1)} custom-call(bf16[256,2048]{1,0:T(8,128)(2,1)} %multiply_convert_fusion.3.x_ref), custom_call_target="tpu_custom_call" | custom-call | bytes 67108864 | tf_op jit(solution)/shard_map/gather_rows/pallas_call | solution.py:231
  248.6 11.8 %fusion.28 = f32[2048,768]{1,0:T(8,128)} fusion(bf16[2048,2048]{1,0:T(8,128)(2,1)} %bitcast.66, bf16[2048,768]{1,0:T(8,128)(2,1)} %all-gather.6.cloned.1.call-done.refs_2_), kind=kOutput, calls=%fused_computation.84 | convolution fusion | flops 6442450944 | bytes 17825792 | tf_op jit(solution)/shard_map/dot_general | solution.py:22
  260.4 13.6 %multiply_convert_fusion.2 = (bf16[2048,768]{1,0:T(8,128)(2,1)S(1)}, f32[2048,768]{1,0:T(8,128)}) fusion(f32[2048,768]{1,0:T(8,128)} %fusion.28, bf16[2048,2048]{1,0:T(8,128)(2,1)} %bitcast.64, bf16[768,2048]{1,0:T(8,128)(2,1)} %all-gather.10.cloned.1.call-done.refs_1_), kind=kOutput, calls=%fused_computation.2 | convolution fusion | flops 6458179584 | bytes 27262976 | tf_op jit(solution)/shard_map/dot_general | solution.py:28
  274.0 1.7 copy-done.12
  275.7 8.9 %convolution_convert_fusion = bf16[2048,768]{1,0:T(8,128)(2,1)} fusion(bf16[2048,2048]{1,0:T(8,128)(2,1)S(1)} %bitcast.69, bf16[2048,768]{1,0:T(8,128)(2,1)S(1)} %get-tuple-element.143.refs_1_), kind=kOutput, calls=%fused_computation.11 | convolution fusion | flops 6444023808 | bytes 14680064 | tf_op jit(solution)/shard_map/dot_general | solution.py:34
  284.6 7.7 %all-gather.8.cloned.1.call-done.refs_3_ = bf16[2048,768]{1,0:T(8,128)(2,1)} async-done(((bf16[512,768]{1,0:T(8,128)(2,1)}), bf16[2048,768]{1,0:T(8,128)(2,1)}) %all-gather.8.cloned.1.call-update) | async-done | bytes 3145744 | tf_op jit(solution)/shard_map/all_gather | solution.py:867
  292.4 17.5 %multiply_convert_fusion = (bf16[2048,768]{1,0:T(8,128)(2,1)}, bf16[2048,768]{1,0:T(8,128)(2,1)}) fusion(f32[2048,768]{1,0:T(8,128)} %get-tuple-element.144, f32[2048,768]{1,0:T(8,128)} %fusion.28, bf16[2048,2048]{1,0:T(8,128)(2,1)} %bitcast.67, bf16[2048,768]{1,0:T(8,128)(2,1)} %all-gather.8.cloned.1.call-done.refs_3_), kind=kOutput, calls=%fused_computation | convolution fusion | flops 6477053952 | bytes 30408704 | tf_op jit(solution)/shard_map/dot_general | solution.py:22
  309.9 55.6 %scatter_products.5 = (f32[256,2048]{1,0:T(8,128)}, bf16[2048,768]{1,0:T(8,128)(2,1)}, bf16[2048,768]{1,0:T(8,128)(2,1)}) custom-call(bf16[2048,768]{1,0:T(8,128)(2,1)} %get-tuple-element.120.refs_0_.refs_6_, bf16[2048,768]{1,0:T(8,128)(2,1)} %copy-done.12, bf16[2048,768]{1,0:T(8,128)(2,1)} %all-gather.6.cloned.1.call-done.refs_2_, ...), custom_call_target="tpu_custom_call" | custom-call | flops 12884901888 | bytes 67108864 | tf_op jit(solution)/shard_map/scatter_products/pallas_call | solution.py:413
  366.3 2.3 multiply_reduce_fusion
  368.8 2.3 fusion.23
  371.1 40.1 %gather_rows.7.dt_ref = bf16[8,256,2048]{2,1,0:T(8,128)(2,1)} custom-call(bf16[256,2048]{1,0:T(8,128)(2,1)} %get-tuple-element.46.x_ref), custom_call_target="tpu_custom_call" | custom-call | bytes 67108864 | tf_op jit(solution)/shard_map/gather_rows/pallas_call | solution.py:231
  411.2 12.4 %reduce-scatter.7.cloned.1.call-done = bf16[512,768]{1,0:T(8,128)(2,1)} async-done(((bf16[2048,768]{1,0:T(8,128)(2,1)}), bf16[512,768]{1,0:T(8,128)(2,1)}) %reduce-scatter.7.cloned.1.call-update) | async-done | bytes 786448 | tf_op jit(solution)/shard_map/reduce_scatter | solution.py:909
  423.5 47.0 %backward_channels.1 = (bf16[2048,320]{1,0:T(8,128)(2,1)}, bf16[2048,320]{1,0:T(8,128)(2,1)}, f32[320,320]{1,0:T(8,128)}, f32[320,320]{1,0:T(8,128)}, f32[8,320]{1,0:T(8,128)}, /*index=5*/bf16[4,960,512]{2,1,0:T(8,128)(2,1)}) custom-call(s32[1,3]{1,0:T(1,128)} %lens_ref.3, bf16[8,256,2048]{2,1,0:T(8,128)(2,1)} %gather_rows.7.dt_ref, ...), custom_call_target="tpu_custom_call" | custom-call | flops 2684354560 | bytes 26738688 | tf_op jit(solution)/shard_map/backward_channels/pallas_call | solution.py:764
  472.1 1.1 convert.47
  473.6 1.1 convert.48
  475.2 4.3 pad_maximum_fusion
  479.7 2.4 convert_element_type.124
  482.1 4.1 reduce-scatter.9.cloned.1.call-done
  486.2 48.6 %scatter_products.6 = f32[256,2048]{1,0:T(8,128)} custom-call(bf16[2048,320]{1,0:T(8,128)(2,1)} %get-tuple-element.58.refs_0_, bf16[2048,320]{1,0:T(8,128)(2,1)} %get-tuple-element.59.refs_1_, bf16[4,1024,512]{2,1,0:T(8,128)(2,1)} %bitcast.74, bf16[4,1024,512]{2,1,0:T(8,128)(2,1)} %bitcast.75), custom_call_target="tpu_custom_call" | custom-call | flops 5368709120 | bytes 67108864 | tf_op jit(solution)/shard_map/scatter_products/pallas_call | solution.py:413
  534.8 2.1 fusion.5
  537.8 15.9 %total.1 = f32[8,128]{1,0:T(8,128)} custom-call(f32[32,8,128]{2,1,0:T(8,128)} %pad.23.x_ref), custom_call_target="tpu_custom_call" | custom-call | tf_op jit(solution)/shard_map/total/pallas_call | solution.py:109
  553.7 2.4 convert_bitcast_fusion
  556.1 3.0 copy.37
  559.1 2.4 convert_element_type.123
  561.5 1.3 slice_bitcast_fusion.5
  562.8 46.3 %scatter_products.7 = f32[256,2048]{1,0:T(8,128)} custom-call(bf16[2048,768]{1,0:T(8,128)(2,1)} %get-tuple-element.60.refs_7_.refs_0_, bf16[768,2048]{1,0:T(8,128)(2,1)} %all-gather.10.cloned.1.call-done.refs_1_), custom_call_target="tpu_custom_call" | custom-call | flops 6442450944 | bytes 67108864 | tf_op jit(solution)/shard_map/scatter_products/pallas_call | solution.py:413
  609.1 1.9 fusion.2
  611.9 1.6 convert_element_type.122
  613.6 1.3 slice_bitcast_fusion
  614.9 1.3 add_convert_fusion
  (101 shorter events, 13.9 us)
Async XLA Ops:
  7.2 111.5 %all-gather.12.cloned.1.call-start = ((), (), s32[]{:S(2)}) async-start(), calls=%async_computation.11 | async-start | bytes 5242880 | tf_op jit(solution)/shard_map/all_gather | solution.py:864
  10.0 3.8 copy-start.7
  12.7 2.2 copy-start.8
  13.8 234.8 %all-gather.6.cloned.1.call-start = ((), (), s32[]{:S(2)}) async-start(), calls=%async_computation.4 | async-start | bytes 3932160 | tf_op jit(solution)/shard_map/all_gather | solution.py:866
  14.8 1.7 copy-start.9
  14.9 2.7 copy-start.10
  14.9 2.7 copy-start.11
  14.9 245.5 %all-gather.10.cloned.1.call-start = ((), (), s32[]{:S(2)}) async-start(), calls=%async_computation.6 | async-start | bytes 3932160 | tf_op jit(solution)/shard_map/all_gather | solution.py:865
  15.9 276.4 %all-gather.8.cloned.1.call-start = ((), (), s32[]{:S(2)}) async-start(), calls=%async_computation.5 | async-start | bytes 3932160 | tf_op jit(solution)/shard_map/all_gather | solution.py:867
  17.5 353.6 %reduce-scatter.5.cloned.1.call-start = ((), (), s32[]{:S(2)}) async-start(), calls=%async_computation.7 | async-start | bytes 3932160 | tf_op jit(solution)/shard_map/reduce_scatter | solution.py:909
  159.2 45.6 %copy-start = (bf16[256,2048]{1,0:T(8,128)(2,1)S(1)}, bf16[256,2048]{1,0:T(8,128)(2,1)}, u32[]{:S(2)}) copy-start(bf16[256,2048]{1,0:T(8,128)(2,1)} %x_ref.2) | copy-start | bytes 3145732
  260.4 15.4 %copy-start.2 = (bf16[8,256,2048]{2,1,0:T(8,128)(2,1)S(1)}, bf16[8,256,2048]{2,1,0:T(8,128)(2,1)}, u32[]{:S(2)}) copy-start(bf16[8,256,2048]{2,1,0:T(8,128)(2,1)} %gather_rows.5) | copy-start | bytes 25165828
  274.0 1.7 copy-start.12
  292.3 131.2 %reduce-scatter.7.cloned.1.call-start = ((), (), s32[]{:S(2)}) async-start(), calls=%async_computation.8 | async-start | bytes 3932160 | tf_op jit(solution)/shard_map/reduce_scatter | solution.py:909
  365.5 120.6 %reduce-scatter.9.cloned.1.call-start = ((), (), s32[]{:S(2)}) async-start(), calls=%async_computation.9 | async-start | bytes 3932160 | tf_op jit(solution)/shard_map/reduce_scatter | solution.py:909
  366.3 244.8 %reduce-scatter.11.cloned.1.call-start = ((), (), s32[]{:S(2)}) async-start(), calls=%async_computation.10 | async-start | bytes 5242880 | tf_op jit(solution)/shard_map/reduce_scatter | solution.py:909
  366.3 2.3 copy-start.4
  366.3 2.5 copy-start.5
  562.8 46.3 %copy-start.1 = (f32[256,2048]{1,0:T(8,128)S(1)}, f32[256,2048]{1,0:T(8,128)}, u32[]{:S(2)}) copy-start(f32[256,2048]{1,0:T(8,128)} %scatter_products.6) | copy-start | bytes 6291460
  562.8 46.3 %copy-start.3 = (f32[256,2048]{1,0:T(8,128)S(1)}, f32[256,2048]{1,0:T(8,128)}, u32[]{:S(2)}) copy-start(f32[256,2048]{1,0:T(8,128)} %get-tuple-element.117) | copy-start | bytes 6291460
  611.9 3.0 copy-start.6
Sparse Core Ops, SparseCore 0:
  13.9 86.2 all-gather.11
  102.4 61.9 all-gather.5
  166.5 62.0 all-gather.9
  230.0 62.2 all-gather.7
  294.5 58.8 reduce-scatter.4
  365.6 57.8 reduce-scatter.6
  425.8 60.2 reduce-scatter.8
  488.5 78.8 reduce-scatter.10

commit v4 on v3

--- a/solution.py
+++ b/solution.py
@@ -264,8 +264,137 @@
         )(left, out)
 
 
+class PlaneSum:
+    COUNT = 8
+    ORDER = (3, 1, 2, 0)
+    LINKS = ((3, 0, 2), (3, 1, 1), (1, 1, 1), (2, 0, 2), (1, 0, 1), (2, 1, 2))
+
+    @staticmethod
+    def scratch(rows, width):
+        middle = rows // 2
+        return [
+            pltpu.VMEM((rows, width), SINGLE),
+            pltpu.VMEM((2, middle, width), SINGLE),
+            pltpu.VMEM((2, rows, width), HALF),
+            pltpu.VMEM((4, rows, width), HALF),
+            pltpu.VMEM((6, middle, width), HALF),
+            pltpu.VMEM((6, middle, width), HALF),
+            pltpu.SemaphoreType.DMA((4,)),
+            pltpu.SemaphoreType.DMA((4,)),
+            pltpu.SemaphoreType.DMA((6,)),
+            pltpu.SemaphoreType.DMA((6,)),
+        ]
+
+    def __init__(self, products, tile, lefts, rights, scratch):
+        self.terms = list(zip(lefts, rights, products))
+        self.tile = tile
+        self.acc, self.side, self.core_out, self.core_in = scratch[:4]
+        self.link_out, self.link_in = scratch[4:6]
+        self.core_send, self.core_recv, self.link_send, self.link_recv = scratch[6:]
+        self.rows, self.width = self.acc.shape
+        self.halves = (slice(0, self.rows // 2), slice(self.rows // 2, self.rows))
+        self.me = lax.axis_index("mp")
+
+    def tiles(self, step):
+        def body(t, carry):
+            step(t, pl.ds(pl.multiple_of(t * self.tile, self.tile), self.tile))
+            return carry
+
+        lax.fori_loop(0, self.width // self.tile, body, 0)
+
+    def partial(self, slot, t, columns):
+        span = pl.ds(pl.multiple_of(slot * self.rows, self.rows), self.rows)
+        value = None
+        for left, right, product in self.terms:
+            term = product(left[span, :], right, t, columns)
+            value = term if value is None else value + term
+        return value
+
+    def core_copy(self, c):
+        return pltpu.make_async_remote_copy(
+            src_ref=self.core_out.at[self.ORDER.index(c) % 2],
+            dst_ref=self.core_in.at[c],
+            send_sem=self.core_send.at[c],
+            recv_sem=self.core_recv.at[c],
+            device_id={"mp": flip(self.me, 1, self.COUNT)},
+            device_id_type=MESH,
+        )
+
+    def link_copy(self, index):
+        return pltpu.make_async_remote_copy(
+            src_ref=self.link_out.at[index],
+            dst_ref=self.link_in.at[index],
+            send_sem=self.link_send.at[index],
+            recv_sem=self.link_recv.at[index],
+            device_id={"mp": flip(self.me, 2 * self.LINKS[index][2], self.COUNT)},
+            device_id_type=MESH,
+        )
+
+    def greet(self):
+        start_barrier((1, 2, 4), self.COUNT)
+
+    def send(self, c):
+        place = self.ORDER.index(c)
+        if place >= 2:
+            self.core_copy(self.ORDER[place - 2]).wait_send()
+        slot = flip(self.me, 2 * c + 1, self.COUNT)
+
+        def step(t, columns):
+            self.core_out[place % 2, :, columns] = self.partial(slot, t, columns).astype(HALF)
+
+        self.tiles(step)
+        self.core_copy(c).start()
+
+    def take(self, c):
+        self.core_copy(c).wait_recv()
+        slot = flip(self.me, 2 * c, self.COUNT)
+        ways = [i for i in range(4) if self.LINKS[i][0] == c]
+        kept = [h for h in (0, 1) if c and h not in [self.LINKS[i][1] for i in ways]]
+
+        def step(t, columns):
+            value = self.partial(slot, t, columns) + self.core_in[c, :, columns].astype(SINGLE)
+            if c == 0:
+                self.acc[:, columns] = value
+            for i in ways:
+                self.link_out[i, :, columns] = value[self.halves[self.LINKS[i][1]]].astype(HALF)
+            for h in kept:
+                self.side[h, :, columns] = value[self.halves[h]]
+
+        self.tiles(step)
+        for i in ways:
+            self.link_copy(i).start()
+
+    def relay(self):
+        for index, landed, half in ((4, 0, 0), (5, 1, 1)):
+            self.link_copy(landed).wait_recv()
+
+            def step(t, columns):
+                value = self.side[half, :, columns]
+                value = value + self.link_in[landed, :, columns].astype(SINGLE)
+                self.link_out[index, :, columns] = value.astype(HALF)
+
+            self.tiles(step)
+            self.link_copy(index).start()
+
+    def finish(self, out_ref):
+        for index in (2, 3, 4, 5):
+            self.link_copy(index).wait_recv()
+
+        def step(t, columns):
+            for half, (one, two) in enumerate(((3, 4), (2, 5))):
+                value = self.acc[self.halves[half], columns]
+                value = value + self.link_in[one, :, columns].astype(SINGLE)
+                value = value + self.link_in[two, :, columns].astype(SINGLE)
+                out_ref[self.halves[half], columns] = value
+
+        self.tiles(step)
+        for c in self.ORDER[2:]:
+            self.core_copy(c).wait_send()
+        for index in range(6):
+            self.link_copy(index).wait_send()
+
+
 def scatter_kernel(products, tile, extra, *refs):
-    count = 8
     pairs = len(products)
     refs = list(refs)
     take = lambda n: [refs.pop(0) for _ in range(n)]
@@ -273,128 +402,19 @@
     beside = take(2 * extra)
     (out_ref,) = take(1)
     beside_out = take(extra)
-    acc, core_out, core_in, link_out, link_in = take(5)
-    core_send, core_recv, link_send, link_recv = refs
-    rows, width = out_ref.shape
-    me = lax.axis_index("mp")
-    start_barrier((1, 2, 4), count)
-
-    def partial(slot, store):
-        first = pl.multiple_of(slot * rows, rows)
-
-        def step(t, carry):
-            columns = pl.ds(pl.multiple_of(t * tile, tile), tile)
-            total = None
-            for left, right, product in zip(lefts, rights, products):
-                term = product(left[pl.ds(first, rows), :], right, t, columns)
-                total = term if total is None else total + term
-            store(columns, total)
-            return carry
-
-        lax.fori_loop(0, width // tile, step, 0)
-
-    def into_core(c):
-        def store(columns, total):
-            core_out[c, :, columns] = total.astype(HALF)
-
-        return store
-
-    def into_acc(c):
-        def store(columns, total):
-            acc[c, :, columns] = total
-
-        return store
-
-    core_copies = {}
-    link_copies = {}
-    middle = rows // 2
-
-    def core_half(c):
-        partial(flip(me, 2 * c + 1, count), into_core(c))
-        copy = pltpu.make_async_remote_copy(
-            src_ref=core_out.at[c],
-            dst_ref=core_in.at[c],
-            send_sem=core_send.at[c],
-            recv_sem=core_recv.at[c],
-            device_id={"mp": flip(me, 1, count)},
-            device_id_type=MESH,
-        )
-        copy.start()
-        core_copies[c] = copy
-
-    def core_sum(c):
-        core_copies[c].wait_recv()
-
-        def step(t, carry):
-            columns = pl.ds(pl.multiple_of(t * tile, tile), tile)
-            acc[c, :, columns] = acc[c, :, columns] + core_in[c, :, columns].astype(SINGLE)
-            return carry
-
-        lax.fori_loop(0, width // tile, step, 0)
-
-    def link(index, c, half, axis):
-        span = pl.ds(half * middle, middle)
-
-        def step(t, carry):
-            columns = pl.ds(pl.multiple_of(t * tile, tile), tile)
-            link_out[index, :, columns] = acc[c, span, columns].astype(HALF)
-            return carry
-
-        lax.fori_loop(0, width // tile, step, 0)
-        copy = pltpu.make_async_remote_copy(
-            src_ref=link_out.at[index],
-            dst_ref=link_in.at[index],
-            send_sem=link_send.at[index],
-            recv_sem=link_recv.at[index],
-            device_id={"mp": flip(me, 2 * axis, count)},
-            device_id_type=MESH,
-        )
-        copy.start()
-        link_copies[index] = copy
-
-    def link_sum(index, c, half):
-        link_copies[index].wait_recv()
-        span = pl.ds(half * middle, middle)
-
-        def step(t, carry):
-            columns = pl.ds(pl.multiple_of(t * tile, tile), tile)
-            acc[c, span, columns] = acc[c, span, columns] + link_in[index, :, columns].astype(
-                SINGLE
-            )
-            return carry
-
-        lax.fori_loop(0, width // tile, step, 0)
-
-    core_half(3)
-    partial(flip(me, 6, count), into_acc(3))
-    core_half(1)
-    core_sum(3)
-    link(0, 3, 0, 2)
-    link(1, 3, 1, 1)
-    partial(flip(me, 2, count), into_acc(1))
-    core_half(2)
-    core_sum(1)
-    link(2, 1, 1, 1)
-    partial(flip(me, 4, count), into_acc(2))
-    core_half(0)
-    core_sum(2)
-    link(3, 2, 0, 2)
-    partial(me, into_acc(0))
-    core_sum(0)
-    link_sum(0, 1, 0)
-    link(4, 1, 0, 1)
-    link_sum(1, 2, 1)
-    link(5, 2, 1, 2)
+    plane = PlaneSum(products, tile, lefts, rights, refs)
+    plane.greet()
+    plane.send(3)
+    plane.send(1)
+    plane.take(3)
+    plane.send(2)
+    plane.take(1)
+    plane.send(0)
+    plane.take(2)
+    plane.take(0)
+    plane.relay()
     beside_products(list(zip(beside[:extra], beside[extra:], beside_out)))
-    link_sum(2, 0, 1)
-    link_sum(3, 0, 0)
-    link_sum(4, 0, 0)
-    link_sum(5, 0, 1)
-    out_ref[...] = acc[0]
-    for copy in core_copies.values():
-        copy.wait_send()
-    for copy in link_copies.values():
-        copy.wait_send()
+    plane.finish(out_ref)
 
 
 def scatter_products(
@@ -418,17 +438,7 @@
         ],
         in_specs=[in_vmem] * (len(lefts) + len(rights)) + [in_hbm] * extra + [in_vmem] * extra,
         out_specs=[in_vmem] + [in_hbm] * extra,
-        scratch_shapes=[
-            pltpu.VMEM((4, rows, width), SINGLE),
-            pltpu.VMEM((4, rows, width), HALF),
-            pltpu.VMEM((4, rows, width), HALF),
-            pltpu.VMEM((6, rows // 2, width), HALF),
-            pltpu.VMEM((6, rows // 2, width), HALF),
-            pltpu.SemaphoreType.DMA((4,)),
-            pltpu.SemaphoreType.DMA((4,)),
-            pltpu.SemaphoreType.DMA((6,)),
-            pltpu.SemaphoreType.DMA((6,)),
-        ],
+        scratch_shapes=PlaneSum.scratch(rows, width),
         compiler_params=pltpu.CompilerParams(
             collective_id=collective_id, has_side_effects=True, vmem_limit_bytes=VMEM_BYTES
         ),
@@ -613,7 +623,12 @@
     )(lens, x_all, gain, pack, blocks_in, blocks_a, chan)
 
 
+def by_columns(left, right, t, columns):
+    return dot_nn(left, right[:, columns])
+
+
 def backward_kernel(
+    plane_tile,
     lens_ref,
     dt_ref,
     pack_ref,
@@ -629,18 +644,34 @@
     hprev_ref,
     ob_ref,
     n1_ref,
+    hidden_ref,
+    down_ref,
     dbx_ref,
     dby_ref,
     gin_ref,
     ga_ref,
     gchan_ref,
     grads_ref,
+    mlp_ref,
     grads,
     lift,
     coef,
     drive,
     carry,
+    *plane_scratch,
 ):
+    if plane_scratch:
+        plane = PlaneSum([by_columns], plane_tile, [hidden_ref], [down_ref], plane_scratch)
+        schedule = {
+            0: lambda: (plane.greet(), plane.send(3), plane.send(1)),
+            1: lambda: (plane.take(3), plane.send(2)),
+            2: lambda: (plane.take(1), plane.send(0)),
+            3: lambda: (plane.take(2), plane.take(0)),
+            5: plane.relay,
+            7: lambda: plane.finish(mlp_ref),
+        }
+        for when, act in schedule.items():
+            pl.when(pl.program_id(0) == when)(lambda act=act: (act(), None)[1])
     step = pl.program_id(0)
     chunk = pl.num_programs(0) - 1 - step
     rows, width = bx_ref.shape
@@ -662,7 +693,7 @@
     d_out = None
     for d in range(pack_ref.shape[0]):
         term = dot_nt(
-            dt_ref[0, :, d * depth : (d + 1) * depth], pack_ref[d, 2 * width : 3 * width, :]
+            dt_ref[0, :, d * depth : (d + 1) * depth], pack_ref[d]
         )
         d_out = term if d_out is None else d_out + term
     pos, live = positions(lens_ref, chunk * rows, (rows, width))
@@ -747,7 +778,7 @@
         grads_ref[...] = grads[...].astype(HALF)
 
 
-def backward_channels(lens, dt_all, pack, blocks_in, blocks_a, chan, saved):
+def backward_channels(lens, dt_all, pack, blocks_in, blocks_a, chan, saved, hidden, down, collective_id):
     bx, by, conv, gate_in, gate_a, h, ob, n1 = saved
     count, rows, model = dt_all.shape
     width = chan.shape[1]
@@ -761,8 +792,13 @@
     full = lambda kind: jax.ShapeDtypeStruct((tokens, width), kind)
     square = jax.ShapeDtypeStruct((width, width), SINGLE)
     grads = (pack.shape[0], 3 * width, pack.shape[2])
-    return pl.pallas_call(
-        backward_kernel,
+    fused = count == PlaneSum.COUNT
+    once = lambda shape, at=None: pl.BlockSpec(
+        shape, lambda i: at or (0,) * len(shape), pipeline_mode=pl.Buffered(1)
+    )
+    tokens_kept = pl.BlockSpec(memory_space=pl.ANY)
+    outs = pl.pallas_call(
+        functools.partial(backward_kernel, 512),
         grid=(count,),
         out_shape=(
             full(HALF),
@@ -771,11 +807,12 @@
             square,
             jax.ShapeDtypeStruct((8, width), SINGLE),
             jax.ShapeDtypeStruct(grads, HALF),
+            jax.ShapeDtypeStruct((rows, model), SINGLE),
         ),
         in_specs=[
             pl.BlockSpec(memory_space=pltpu.SMEM),
             pl.BlockSpec((1, rows, model), lambda i: (last - i, 0, 0)),
-            whole(pack.shape),
+            once((pack.shape[0], width, pack.shape[2]), (0, 2, 0)),
             whole(blocks_in.shape),
             whole(blocks_a.shape),
             whole(chan.shape),
@@ -788,6 +825,8 @@
             before,
             part,
             pl.BlockSpec((rows, model), lambda i: (last - i, 0)),
+            once(hidden.shape) if fused else tokens_kept,
+            once(down.shape) if fused else tokens_kept,
         ],
         out_specs=(
             part,
@@ -795,7 +834,8 @@
             whole((width, width)),
             whole((width, width)),
             whole((8, width)),
-            whole(grads),
+            once(grads),
+            once((rows, model)),
         ),
         scratch_shapes=[
             pltpu.VMEM(grads, SINGLE),
@@ -803,15 +843,28 @@
             pltpu.VMEM((len(lane_tiles(width)), rows, 128), SINGLE),
             pltpu.VMEM((len(lane_tiles(width)), rows, 128), SINGLE),
             pltpu.VMEM((len(lane_tiles(width)), 8, 128), SINGLE),
-        ],
-        compiler_params=pltpu.CompilerParams(vmem_limit_bytes=VMEM_BYTES),
+        ]
+        + (PlaneSum.scratch(rows, model) if fused else []),
+        compiler_params=pltpu.CompilerParams(
+            vmem_limit_bytes=VMEM_BYTES,
+            **(dict(collective_id=collective_id, has_side_effects=True) if fused else {}),
+        ),
         cost_estimate=pl.CostEstimate(
-            flops=2 * tokens * model * width,
-            bytes_accessed=tokens * (model * 2 + width * 28),
+            flops=8 * tokens * model * width,
+            bytes_accessed=tokens * (model * 4 + width * 28),
             transcendentals=8 * tokens * width,
         ),
         name="backward_channels",
-    )(lens, dt_all, pack, blocks_in, blocks_a, chan, bx, by, conv, gate_in, gate_a, h, h, ob, n1)
+    )(
+        lens, dt_all, pack, blocks_in, blocks_a, chan,
+        bx, by, conv, gate_in, gate_a, h, h, ob, n1, hidden, down,
+    )
+    if fused:
+        return outs
+    summed = lax.psum_scatter(
+        dot_nn(hidden, down).astype(HALF), "mp", scatter_dimension=0, tiled=True
+    ).astype(SINGLE)
+    return outs[:-1] + (summed,)
 
 
 def diagonal(blocks):
@@ -949,8 +1002,8 @@
     dt_all, grad_gate = lax.optimization_barrier((dt_all, grad_gate))
 
     saved = (bx, by, conv, gate_in, gate_a, h, ob, n1)
-    d_bx, d_by, gin, ga, gchan, rnn_grads = backward_channels(
-        lengths, dt_all, pack, blocks_in, blocks_a, chan, saved
+    d_bx, d_by, gin, ga, gchan, rnn_grads, mlp_out = backward_channels(
+        lengths, dt_all, pack, blocks_in, blocks_a, chan, saved, hidden, down, 5
     )
     d_bx, grad_down = lax.optimization_barrier((d_bx, grad_down))
     (d_normed,) = scatter_products(
@@ -983,18 +1036,6 @@
     small_grads = jnp.pad(small_grads, ((0, 0), (0, small_rows * depth - used)))
     small_grads = small_grads.reshape(parts, small_rows, depth).astype(HALF)
     rnn_grads = over_dp(jnp.concatenate([rnn_grads, small_grads], axis=1), 0)
-    hidden, d_normed = lax.optimization_barrier((hidden, d_normed))
-    (mlp_out,) = scatter_products(
-        [hidden],
-        [down],
-        [lambda l, r, t, cols: dot_nn(l, r[:, cols])],
-        lambda: dot_nn(hidden, down),
-        model,
-        tile,
-        5,
-        2 * tokens * model * up_w.shape[1],
-    )
-    mlp_out, rnn_grads = lax.optimization_barrier((mlp_out, rnn_grads))
     layer_output = (residual + mlp_out).astype(HALF)
 
     scale_first = lax.rsqrt(jnp.mean(inputs * inputs, axis=-1, keepdims=True) + EPS)

time: 630 us -> 599 us (0.951)
  Pallas kernels: 474 us -> 447 us
    pallas_call x4 -> x3, Pallas kernels: 196 us -> 151 us  [scatter_products(): pl.pallas_call(functools.partial(scatter_kernel, products, tile, extra),...]
    pallas_call x1, Pallas kernels: 47 us -> 66.7 us  [backward_channels(): pl.pallas_call(functools.partial(backward_kernel, 512), grid=(count,), ou...]
  transfers between devices with their start and end apart: 8 -> 8, of which waited for: 3 -> 2; matrix products, arithmetic and copies ran while one was open for 15% -> 17% of each run, Pallas kernels for 76% -> 75%
where the time goes in v4:
time: 599 us; the launch traced here: 595 us
  Pallas kernels  447 us (75%)
  matrix products  51.5 us (9%)
  other arithmetic  42.6 us (7%)
  local copies, waits for them, and re-layouts  19.1 us (3%)
  waiting for transfers between devices  18.8 us (3%)
  between operations  14.8 us (2%)
    pallas_call x4, Pallas kernels, gather_rows(): pl.pallas_call(functools.partial(gather_kernel, count), out_shape=jax.Sha...  161 us
    pallas_call x3, Pallas kernels, scatter_products(): pl.pallas_call(functools.partial(scatter_kernel, products, tile, extra),...  151 us
    pallas_call x1, Pallas kernels, backward_channels(): pl.pallas_call(functools.partial(backward_kernel, 512), grid=(count,), ou...  66.7 us
    pallas_call x1, Pallas kernels, forward_channels(): pl.pallas_call(forward_kernel, grid=(count,), out_shape=(jax.ShapeDtypeSt...  35.5 us
    pallas_call x2, Pallas kernels, small_call(): pl.pallas_call(kernel, out_shape=jax.ShapeDtypeStruct(out_shape, x.dtype)...  33.5 us
    dot_general x2, matrix products, dot_nn(): lax.dot_general(left, right, (((1,), (0,)), ((), ())), preferred_element_...  29.1 us
    dot_general x1, matrix products, dot_nt(): lax.dot_general(left, right, (((1,), (1,)), ((), ())), preferred_element_...  13.7 us
  transfers between devices with their start and end apart: 8, of which 2 were waited for; matrix products, arithmetic and copies ran while one was open for 17% of the time, Pallas kernels for 75%

profile of v4, /device:TPU:0, one launch (start us, length us, event | category | flops | bytes accessed | tf_op | source)
XLA Modules:
  0.0 594.6 jit_solution(3921106882829693096)
XLA Ops:
  8.0 0.9 convert_element_type.104
  9.0 0.9 convert_element_type.105
  10.1 1.2 convert_element_type.103
  11.4 1.4 convert_bitcast_fusion.1
  12.7 1.0 pad_maximum_fusion.1
  13.9 1.0 convert_element_type.114
  14.9 1.0 convert_element_type.111
  16.5 1.0 convert_element_type.113
  18.2 17.7 %share.1 = f32[32,8,128]{2,1,0:T(8,128)} custom-call(f32[8,128]{1,0:T(8,128)} %fusion.22.x_ref), custom_call_target="tpu_custom_call" | custom-call | tf_op jit(solution)/shard_map/share/pallas_call | solution.py:109
  35.9 1.1 slice_reduce_fusion
  37.8 40.5 %gather_rows.5 = bf16[8,256,2048]{2,1,0:T(8,128)(2,1)} custom-call(bf16[256,2048]{1,0:T(8,128)(2,1)} %x_ref.3), custom_call_target="tpu_custom_call" | custom-call | bytes 67108864 | tf_op jit(solution)/shard_map/gather_rows/pallas_call | solution.py:231
  78.3 40.3 %gather_rows.4.x_ref = bf16[8,256,2048]{2,1,0:T(8,128)(2,1)} custom-call(bf16[256,2048]{1,0:T(8,128)(2,1)} %x_ref.2), custom_call_target="tpu_custom_call" | custom-call | bytes 67108864 | tf_op jit(solution)/shard_map/gather_rows/pallas_call | solution.py:231
  118.7 1.0 slice_bitcast_fusion.3
  121.2 0.9 mul.252.ba_ref
  122.1 0.9 mul.248.bin_ref
  123.7 35.5 %forward_channels.1 = (bf16[2048,2048]{1,0:T(8,128)(2,1)}, bf16[2048,320]{1,0:T(8,128)(2,1)}, f32[2048,320]{1,0:T(8,128)}, f32[2048,320]{1,0:T(8,128)}, f32[2048...) custom-call(s32[1,3]{1,0:T(1,128)} %lens_ref.3, ...), custom_call_target="tpu_custom_call" | custom-call | flops 5368709120 | bytes 32505856 | tf_op jit(solution)/shard_map/forward_channels/pallas_call | solution.py:587
  159.2 46.3 %scatter_products.3 = f32[256,2048]{1,0:T(8,128)} custom-call(bf16[2048,320]{1,0:T(8,128)(2,1)} %get-tuple-element.39.refs_0_.ob_ref, bf16[4,1024,512]{2,1,0:T(8,128)(2,1)} %bitcast.72), custom_call_target="tpu_custom_call" | custom-call | flops 2684354560 | bytes 67108864 | tf_op jit(solution)/shard_map/scatter_products/pallas_call | solution.py:433
  205.5 2.1 multiply_reduce_fusion.2
  207.6 1.2 multiply_convert_fusion.3.x_ref
  208.8 40.5 %gather_rows.6 = bf16[8,256,2048]{2,1,0:T(8,128)(2,1)} custom-call(bf16[256,2048]{1,0:T(8,128)(2,1)} %multiply_convert_fusion.3.x_ref), custom_call_target="tpu_custom_call" | custom-call | bytes 67108864 | tf_op jit(solution)/shard_map/gather_rows/pallas_call | solution.py:231
  249.3 11.8 %fusion.28 = f32[2048,768]{1,0:T(8,128)} fusion(bf16[2048,2048]{1,0:T(8,128)(2,1)} %bitcast.66, bf16[2048,768]{1,0:T(8,128)(2,1)} %all-gather.10.cloned.1.call-done.refs_2_), kind=kOutput, calls=%fused_computation.84 | convolution fusion | flops 6442450944 | bytes 17825792 | tf_op jit(solution)/shard_map/dot_general | solution.py:22
  261.1 13.7 %multiply_convert_fusion.2 = (bf16[2048,768]{1,0:T(8,128)(2,1)S(1)}, f32[2048,768]{1,0:T(8,128)}) fusion(f32[2048,768]{1,0:T(8,128)} %fusion.28, bf16[2048,2048]{1,0:T(8,128)(2,1)} %bitcast.64, bf16[768,2048]{1,0:T(8,128)(2,1)} %all-gather.6.cloned.1.call-done.down_ref), kind=kOutput, calls=%fused_computation.2 | convolution fusion | flops 6458179584 | bytes 27262976 | tf_op jit(solution)/shard_map/dot_general | solution.py:28
  274.8 1.7 copy-done.10
  276.5 8.7 %convolution_convert_fusion = bf16[2048,768]{1,0:T(8,128)(2,1)} fusion(bf16[2048,2048]{1,0:T(8,128)(2,1)S(1)} %bitcast.69, bf16[2048,768]{1,0:T(8,128)(2,1)S(1)} %get-tuple-element.137.refs_1_), kind=kOutput, calls=%fused_computation.11 | convolution fusion | flops 6444023808 | bytes 14680064 | tf_op jit(solution)/shard_map/dot_general | solution.py:34
  285.2 7.1 %all-gather.8.cloned.1.call-done.refs_3_ = bf16[2048,768]{1,0:T(8,128)(2,1)} async-done(((bf16[512,768]{1,0:T(8,128)(2,1)}), bf16[2048,768]{1,0:T(8,128)(2,1)}) %all-gather.8.cloned.1.call-update) | async-done | bytes 3145744 | tf_op jit(solution)/shard_map/all_gather | solution.py:920
  292.4 17.3 %multiply_convert_fusion = (bf16[2048,768]{1,0:T(8,128)(2,1)}, bf16[2048,768]{1,0:T(8,128)(2,1)}) fusion(f32[2048,768]{1,0:T(8,128)} %fusion.28, f32[2048,768]{1,0:T(8,128)} %get-tuple-element.138, bf16[2048,2048]{1,0:T(8,128)(2,1)} %bitcast.67, bf16[2048,768]{1,0:T(8,128)(2,1)} %all-gather.8.cloned.1.call-done.refs_3_), kind=kOutput, calls=%fused_computation | convolution fusion | flops 6477053952 | bytes 30408704 | tf_op jit(solution)/shard_map/dot_general | solution.py:22
  309.8 54.9 %scatter_products.4 = (f32[256,2048]{1,0:T(8,128)}, bf16[2048,768]{1,0:T(8,128)(2,1)}, bf16[2048,768]{1,0:T(8,128)(2,1)}) custom-call(bf16[2048,768]{1,0:T(8,128)(2,1)} %get-tuple-element.115.refs_0_.refs_6_, bf16[2048,768]{1,0:T(8,128)(2,1)} %copy-done.10, bf16[2048,768]{1,0:T(8,128)(2,1)} %all-gather.10.cloned.1.call-done.refs_2_, ...), custom_call_target="tpu_custom_call" | custom-call | flops 12884901888 | bytes 67108864 | tf_op jit(solution)/shard_map/scatter_products/pallas_call | solution.py:433
  364.7 2.1 multiply_reduce_fusion
  367.0 4.5 fusion.23
  371.4 39.9 %gather_rows.7.dt_ref = bf16[8,256,2048]{2,1,0:T(8,128)(2,1)} custom-call(bf16[256,2048]{1,0:T(8,128)(2,1)} %get-tuple-element.43.x_ref), custom_call_target="tpu_custom_call" | custom-call | bytes 67108864 | tf_op jit(solution)/shard_map/gather_rows/pallas_call | solution.py:231
  411.3 11.5 %reduce-scatter.7.cloned.1.call-done = bf16[512,768]{1,0:T(8,128)(2,1)} async-done(((bf16[2048,768]{1,0:T(8,128)(2,1)}), bf16[512,768]{1,0:T(8,128)(2,1)}) %reduce-scatter.7.cloned.1.call-update) | async-done | bytes 786448 | tf_op jit(solution)/shard_map/reduce_scatter | solution.py:962
  422.8 66.7 %backward_channels.1 = (bf16[2048,320]{1,0:T(8,128)(2,1)}, bf16[2048,320]{1,0:T(8,128)(2,1)}, f32[320,320]{1,0:T(8,128)}, f32[320,320]{1,0:T(8,128)}, f32[8,320]...) custom-call(s32[1,3]{1,0:T(1,128)} %lens_ref.3, bf16[8,256,2048]{2,1,0:T(8,128)(2,1)} %gather_rows.7.dt_ref, ...), custom_call_target="tpu_custom_call" | custom-call | flops 10737418240 | bytes 35127296 | tf_op jit(solution)/shard_map/backward_channels/pallas_call | solution.py:800
  491.1 1.1 convert.47
  492.5 1.1 convert.48
  494.1 4.3 pad_maximum_fusion
  498.7 2.4 convert_element_type.124
  501.0 49.4 %scatter_products.5 = f32[256,2048]{1,0:T(8,128)} custom-call(bf16[2048,320]{1,0:T(8,128)(2,1)} %get-tuple-element.56.refs_0_, bf16[2048,320]{1,0:T(8,128)(2,1)} %get-tuple-element.57.refs_1_, bf16[4,1024,512]{2,1,0:T(8,128)(2,1)} %bitcast.74, bf16[4,1024,512]{2,1,0:T(8,128)(2,1)} %bitcast.75), custom_call_target="tpu_custom_call" | custom-call | flops 5368709120 | bytes 67108864 | tf_op jit(solution)/shard_map/scatter_products/pallas_call | solution.py:433
  550.5 2.1 fusion.5
  553.4 15.7 %total.1 = f32[8,128]{1,0:T(8,128)} custom-call(f32[32,8,128]{2,1,0:T(8,128)} %pad.22.x_ref), custom_call_target="tpu_custom_call" | custom-call | tf_op jit(solution)/shard_map/total/pallas_call | solution.py:109
  569.2 2.4 convert_bitcast_fusion
  571.6 3.0 copy.37
  574.6 2.5 convert_element_type.123
  577.1 1.4 slice_bitcast_fusion.5
  578.5 1.3 add_convert_fusion
  579.8 1.9 fusion.2
  581.7 1.5 convert_element_type.122
  583.2 1.3 slice_bitcast_fusion
  584.5 0.8 fusion.24
  (96 shorter events, 11.3 us)
Async XLA Ops:
  7.2 111.5 %all-gather.12.cloned.1.call-start = ((), (), s32[]{:S(2)}) async-start(), calls=%async_computation.11 | async-start | bytes 5242880 | tf_op jit(solution)/shard_map/all_gather | solution.py:917
  10.0 3.8 copy-start.5
  12.7 2.2 copy-start.6
  13.8 235.5 %all-gather.10.cloned.1.call-start = ((), (), s32[]{:S(2)}) async-start(), calls=%async_computation.6 | async-start | bytes 3932160 | tf_op jit(solution)/shard_map/all_gather | solution.py:919
  14.8 1.7 copy-start.7
  14.9 2.7 copy-start.8
  14.9 2.7 copy-start.9
  14.9 246.2 %all-gather.6.cloned.1.call-start = ((), (), s32[]{:S(2)}) async-start(), calls=%async_computation.4 | async-start | bytes 3932160 | tf_op jit(solution)/shard_map/all_gather | solution.py:918
  15.9 276.4 %all-gather.8.cloned.1.call-start = ((), (), s32[]{:S(2)}) async-start(), calls=%async_computation.5 | async-start | bytes 3932160 | tf_op jit(solution)/shard_map/all_gather | solution.py:920
  17.5 353.9 %reduce-scatter.5.cloned.1.call-start = ((), (), s32[]{:S(2)}) async-start(), calls=%async_computation.7 | async-start | bytes 3932160 | tf_op jit(solution)/shard_map/reduce_scatter | solution.py:962
  159.2 46.3 %copy-start = (bf16[256,2048]{1,0:T(8,128)(2,1)S(1)}, bf16[256,2048]{1,0:T(8,128)(2,1)}, u32[]{:S(2)}) copy-start(bf16[256,2048]{1,0:T(8,128)(2,1)} %x_ref.2) | copy-start | bytes 3145732
  261.1 15.4 %copy-start.2 = (bf16[8,256,2048]{2,1,0:T(8,128)(2,1)S(1)}, bf16[8,256,2048]{2,1,0:T(8,128)(2,1)}, u32[]{:S(2)}) copy-start(bf16[8,256,2048]{2,1,0:T(8,128)(2,1)} %gather_rows.6) | copy-start | bytes 25165828
  274.8 1.7 copy-start.10
  292.4 130.4 %reduce-scatter.7.cloned.1.call-start = ((), (), s32[]{:S(2)}) async-start(), calls=%async_computation.8 | async-start | bytes 3932160 | tf_op jit(solution)/shard_map/reduce_scatter | solution.py:962
  364.7 136.4 %reduce-scatter.9.cloned.1.call-start = ((), (), s32[]{:S(2)}) async-start(), calls=%async_computation.9 | async-start | bytes 3932160 | tf_op jit(solution)/shard_map/reduce_scatter | solution.py:962
  366.9 214.8 %reduce-scatter.11.cloned.1.call-start = ((), (), s32[]{:S(2)}) async-start(), calls=%async_computation.10 | async-start | bytes 5242880 | tf_op jit(solution)/shard_map/reduce_scatter | solution.py:962
  574.6 3.9 copy-start.4
  577.1 2.6 copy-start.1
  577.1 2.6 copy-start.3
Sparse Core Ops, SparseCore 0:
  13.9 86.2 all-gather.11
  102.4 61.9 all-gather.9
  166.5 62.1 all-gather.5
  230.1 62.1 all-gather.7
  294.5 58.8 reduce-scatter.4
  364.8 57.9 reduce-scatter.6
  425.1 60.2 reduce-scatter.8
  498.6 78.1 reduce-scatter.10

commit v5 on v4

v5 whole, which is shorter than its diff:
```python
import functools
import typing

import jax
import jax.numpy as jnp
from jax import lax
from jax.experimental import pallas as pl
from jax.experimental.pallas import tpu as pltpu
from jax.sharding import PartitionSpec as P

CONV = 4
AHEAD = 2
EPS = 1e-06
DECAY = 8.0
HALF = jnp.bfloat16
SINGLE = jnp.float32
MESH = pl.DeviceIdType.MESH
VMEM_BYTES = 60 * 1024 * 1024
GELU_C = 0.7978845608028654
GELU_K = 0.044715


def dot_nn(left, right):
    return lax.dot_general(
        left, right, (((1,), (0,)), ((), ())), preferred_element_type=SINGLE
    )


def dot_nt(left, right):
    return lax.dot_general(
        left, right, (((1,), (1,)), ((), ())), preferred_element_type=SINGLE
    )


def dot_tn(left, right):
    return lax.dot_general(
        left, right, (((0,), (0,)), ((), ())), preferred_element_type=SINGLE
    )


def gelu(v):
    return 0.5 * v * (1.0 + jnp.tanh(GELU_C * (v + GELU_K * v * v * v)))


def gelu_both(v):
    square = v * v
    t = jnp.tanh(GELU_C * (v + GELU_K * v * square))
    value = 0.5 * v * (1.0 + t)
    slope = 0.5 * (1.0 + t) + 0.5 * v * (1.0 - t * t) * (GELU_C * (1.0 + 3.0 * GELU_K * square))
    return value, slope


def flip(me, mask, count):
    place = me
    bit = 1
    while bit < count:
        if mask & bit:
            place = place + (1 - 2 * ((me // bit) % 2)) * bit
        bit *= 2
    return place


def ring_peers(axis):
    me, count = lax.axis_index(axis), lax.axis_size(axis)
    return [(k, {axis: (me + k) % count}) for k in range(1, count)]


def greet(peers):
    barrier = pltpu.get_barrier_semaphore()
    for _, peer in peers:
        pl.semaphore_signal(barrier, inc=1, device_id=peer, device_id_type=MESH)
    pl.semaphore_wait(barrier, len(peers))


def exchange(peers, source, target, send, recv):
    copies = []
    for k, peer in peers:
        copy = pltpu.make_async_remote_copy(
            src_ref=source(k),
            dst_ref=target(k),
            send_sem=send.at[k],
            recv_sem=recv.at[k],
            device_id=peer,
            device_id_type=MESH,
        )
        copy.start()
        copies.append(copy)
    return copies


def gather_plan(count):
    bits = [1 << b for b in range(count.bit_length() - 1)]
    outer = bits[1:]
    orders = (outer + bits[:1], outer[::-1] + bits[:1])
    sends = []
    for half, order in enumerate(orders):
        for stage, bit in enumerate(order):
            for pick in range(1 << stage):
                mask = sum(order[j] for j in range(stage) if pick >> j & 1)
                sends.append((bin(mask).count("1"), half, mask, bit))
    sends.sort(key=lambda s: s[0])
    return bits, [s[1:] for s in sends]


class PlaneGather:
    COUNT = 8

    @staticmethod
    def scratch():
        count = PlaneGather.COUNT
        return [
            pltpu.SemaphoreType.DMA,
            pltpu.SemaphoreType.DMA((2, count)),
            pltpu.SemaphoreType.DMA((2, count)),
        ]

    def __init__(self, x_ref, o_ref, scratch):
        self.x, self.o = x_ref, o_ref
        self.own_sem, self.send, self.recv = scratch
        self.me = lax.axis_index("mp")
        self.bits, self.plan = gather_plan(self.COUNT)

    def own(self):
        rows = self.x.shape[0]
        span = pl.ds(pl.multiple_of(self.me * rows, rows), rows)
        return pltpu.make_async_copy(self.x, self.o.at[span], self.own_sem)

    def copy(self, half, mask, bit):
        rows = self.x.shape[0] // 2
        slot = 2 * flip(self.me, mask, self.COUNT) + half
        span = pl.ds(pl.multiple_of(slot * rows, rows), rows)
        return pltpu.make_async_remote_copy(
            src_ref=self.o.at[span] if mask else self.x.at[pl.ds(half * rows, rows)],
            dst_ref=self.o.at[span],
            send_sem=self.send.at[half, mask | bit],
            recv_sem=self.recv.at[half, mask | bit],
            device_id={"mp": flip(self.me, bit, self.COUNT)},
            device_id_type=MESH,
        )

    def level(self, depth):
        landed = set()
        for half, mask, bit in self.plan:
            if bin(mask).count("1") != depth:
                continue
            if mask and (half, mask) not in landed:
                landed.add((half, mask))
                self.arrived(half, mask)
            self.copy(half, mask, bit).start()

    def arrived(self, half, mask):
        for other, before, bit in self.plan:
            if other == half and before | bit == mask:
                self.copy(half, before, bit).wait_recv()

    def start(self):
        self.own().start()
        self.level(0)

    def finish(self):
        waited = {(half, mask) for half, mask, _ in self.plan}
        for half, mask, bit in self.plan:
            if (half, mask | bit) not in waited:
                self.copy(half, mask, bit).wait_recv()
        for entry in self.plan:
            self.copy(*entry).wait_send()
        self.own().wait()


class LineGather:
    COUNT = 4
    ENDS = ((0, 3), (3, 0))

    @staticmethod
    def scratch(pieces):
        shapes = ((pieces, 4), (pieces, 4), (pieces,), (pieces,))
        return [pltpu.SemaphoreType.DMA(shape) for shape in shapes]

    def __init__(self, jobs, scratch):
        self.chunks, self.of = [], []
        for source, target, pieces in jobs:
            rows = source.shape[0] // pieces
            first = len(self.chunks)
            self.chunks += [(source, target, pl.ds(p * rows, rows)) for p in range(pieces)]
            self.of.append(range(first, len(self.chunks)))
        self.send, self.recv, self.onward, self.own_sem = scratch
        self.me = lax.axis_index("dp")

    def own(self, c):
        source, target, span = self.chunks[c]
        return pltpu.make_async_copy(
            source.at[span], target.at[self.me, span], self.own_sem.at[c]
        )

    def direct(self, c, to):
        source, target, span = self.chunks[c]
        return pltpu.make_async_remote_copy(
            src_ref=source.at[span],
            dst_ref=target.at[self.me, span],
            send_sem=self.send.at[c, to],
            recv_sem=self.recv.at[c, self.me],
            device_id={"dp": to},
            device_id_type=MESH,
        )

    def handed(self, c, block, to):
        _, target, span = self.chunks[c]
        return pltpu.make_async_remote_copy(
            src_ref=target.at[block, span],
            dst_ref=target.at[block, span],
            send_sem=self.onward.at[c],
            recv_sem=self.recv.at[c, block],
            device_id={"dp": to},
            device_id_type=MESH,
        )

    def sends_to(self, to):
        senders = [z for z in range(self.COUNT) if z != to and (z, to) not in self.ENDS]
        return functools.reduce(jnp.logical_or, [self.me == z for z in senders])

    def start(self, chunks):
        for c in chunks:
            self.own(c).start()
            for to in range(self.COUNT):
                pl.when(self.sends_to(to))(lambda c=c, to=to: self.direct(c, to).start())

    def hand_on(self, chunks):
        for c in chunks:
            for first, last in self.ENDS:
                middle = 2 if last == 3 else 1

                @pl.when(self.me == middle)
                def _(c=c, first=first, last=last):
                    copy = self.handed(c, first, last)
                    copy.wait_recv()
                    copy.start()

    def begin(self, ahead):
        self.ahead, self.done = ahead, 0
        self.start(range(ahead))

    def tick(self, count=1):
        for _ in range(count):
            self.hand_on([self.done])
            if self.done + self.ahead < len(self.chunks):
                self.start([self.done + self.ahead])
            self.done += 1

    def landed(self, chunks):
        for c in chunks:
            for block in range(self.COUNT):
                early = 2 if block == 0 else 1 if block == 3 else None
                waits = self.me != block
                if early is not None:
                    waits = jnp.logical_and(waits, self.me != early)
                pl.when(waits)(lambda c=c, block=block: self.handed(c, block, 0).wait_recv())
            self.own(c).wait()

    def settle(self):
        for c in range(len(self.chunks)):
            for to in range(self.COUNT):
                pl.when(self.sends_to(to))(lambda c=c, to=to: self.direct(c, to).wait_send())
            pl.when(jnp.logical_or(self.me == 1, self.me == 2))(
                lambda c=c: self.handed(c, 0, 0).wait_send()
            )


def kernel_params(collective_id):
    return pltpu.CompilerParams(
        collective_id=collective_id, has_side_effects=True, vmem_limit_bytes=VMEM_BYTES
    )


def share(x_ref, o_ref, sems):
    send_mp, recv_mp, send_dp, recv_dp = sems
    inner, outer = ring_peers("mp"), ring_peers("dp")
    count = len(inner) + 1
    first = lax.axis_index("dp") * count
    place = first + lax.axis_index("mp")
    o_ref[place] = x_ref[...]
    mine = lambda k: o_ref.at[place]
    plane = lambda k: o_ref.at[pl.ds(first, count)]
    copies = exchange(inner, mine, mine, send_mp, recv_mp)
    for copy in copies:
        copy.wait_recv()
    later = exchange(outer, plane, plane, send_dp, recv_dp)
    return later, copies + later


def beside_products(pairs):
    for left, right, out in pairs:
        tokens, rows = left.shape
        tile = min(256, rows)

        def body(left_tile, out_tile):
            out_tile[...] = dot_tn(left_tile[...], right[...]).astype(out_tile.dtype)

        pltpu.emit_pipeline(
            body,
            grid=(rows // tile,),
            in_specs=[pl.BlockSpec((tokens, tile), lambda i: (0, i))],
            out_specs=[pl.BlockSpec((tile, right.shape[1]), lambda i: (i, 0))],
        )(left, out)


class PlaneSum:
    COUNT = 8
    ORDER = (3, 1, 2, 0)
    LINKS = ((3, 0, 2), (3, 1, 1), (1, 1, 1), (2, 0, 2), (1, 0, 1), (2, 1, 2))

    @staticmethod
    def scratch(rows, width):
        middle = rows // 2
        return [
            pltpu.VMEM((rows, width), SINGLE),
            pltpu.VMEM((2, middle, width), SINGLE),
            pltpu.VMEM((2, rows, width), HALF),
            pltpu.VMEM((4, rows, width), HALF),
            pltpu.VMEM((6, middle, width), HALF),
            pltpu.VMEM((6, middle, width), HALF),
            pltpu.SemaphoreType.DMA((4,)),
            pltpu.SemaphoreType.DMA((4,)),
            pltpu.SemaphoreType.DMA((6,)),
            pltpu.SemaphoreType.DMA((6,)),
        ]

    def __init__(self, products, tile, lefts, rights, scratch):
        self.terms = list(zip(lefts, rights, products))
        self.tile = tile
        self.acc, self.side, self.core_out, self.core_in = scratch[:4]
        self.link_out, self.link_in = scratch[4:6]
        self.core_send, self.core_recv, self.link_send, self.link_recv = scratch[6:]
        self.rows, self.width = self.acc.shape
        self.halves = (slice(0, self.rows // 2), slice(self.rows // 2, self.rows))
        self.me = lax.axis_index("mp")

    def tiles(self, step):
        def body(t, carry):
            step(t, pl.ds(pl.multiple_of(t * self.tile, self.tile), self.tile))
            return carry

        lax.fori_loop(0, self.width // self.tile, body, 0)

    def partial(self, slot, t, columns):
        span = pl.ds(pl.multiple_of(slot * self.rows, self.rows), self.rows)
        value = None
        for left, right, product in self.terms:
            term = product(left[span, :], right, t, columns)
            value = term if value is None else value + term
        return value

    def core_copy(self, c):
        return pltpu.make_async_remote_copy(
            src_ref=self.core_out.at[self.ORDER.index(c) % 2],
            dst_ref=self.core_in.at[c],
            send_sem=self.core_send.at[c],
            recv_sem=self.core_recv.at[c],
            device_id={"mp": flip(self.me, 1, self.COUNT)},
            device_id_type=MESH,
        )

    def link_copy(self, index):
        return pltpu.make_async_remote_copy(
            src_ref=self.link_out.at[index],
            dst_ref=self.link_in.at[index],
            send_sem=self.link_send.at[index],
            recv_sem=self.link_recv.at[index],
            device_id={"mp": flip(self.me, 2 * self.LINKS[index][2], self.COUNT)},
            device_id_type=MESH,
        )

    def send(self, c):
        place = self.ORDER.index(c)
        if place >= 2:
            self.core_copy(self.ORDER[place - 2]).wait_send()
        slot = flip(self.me, 2 * c + 1, self.COUNT)

        def step(t, columns):
            self.core_out[place % 2, :, columns] = self.partial(slot, t, columns).astype(HALF)

        self.tiles(step)
        self.core_copy(c).start()

    def take(self, c):
        self.core_copy(c).wait_recv()
        slot = flip(self.me, 2 * c, self.COUNT)
        ways = [i for i in range(4) if self.LINKS[i][0] == c]
        kept = [h for h in (0, 1) if c and h not in [self.LINKS[i][1] for i in ways]]

        def step(t, columns):
            value = self.partial(slot, t, columns) + self.core_in[c, :, columns].astype(SINGLE)
            if c == 0:
                self.acc[:, columns] = value
            for i in ways:
                self.link_out[i, :, columns] = value[self.halves[self.LINKS[i][1]]].astype(HALF)
            for h in kept:
                self.side[h, :, columns] = value[self.halves[h]]

        self.tiles(step)
        for i in ways:
            self.link_copy(i).start()

    def spread(self, between=lambda: None):
        self.send(3)
        self.send(1)
        self.take(3)
        self.send(2)
        self.take(1)
        between()
        self.send(0)
        self.take(2)
        self.take(0)
        self.relay()

    def relay(self):
        for index, landed, half in ((4, 0, 0), (5, 1, 1)):
            self.link_copy(landed).wait_recv()

            def step(t, columns):
                value = self.side[half, :, columns]
                value = value + self.link_in[landed, :, columns].astype(SINGLE)
                self.link_out[index, :, columns] = value.astype(HALF)

            self.tiles(step)
            self.link_copy(index).start()

    def finish(self, out_ref):
        for index in (2, 3, 4, 5):
            self.link_copy(index).wait_recv()

        def step(t, columns):
            for half, (one, two) in enumerate(((3, 4), (2, 5))):
                value = self.acc[self.halves[half], columns]
                value = value + self.link_in[one, :, columns].astype(SINGLE)
                value = value + self.link_in[two, :, columns].astype(SINGLE)
                out_ref[self.halves[half], columns] = value

        self.tiles(step)
        for c in self.ORDER[2:]:
            self.core_copy(c).wait_send()
        for index in range(6):
            self.link_copy(index).wait_send()


class LineSum:
    COUNT = 4

    @staticmethod
    def scratch(pieces):
        shapes = ((pieces, 4), (pieces, 4), (pieces,), (pieces,))
        return [pltpu.SemaphoreType.DMA(shape) for shape in shapes] + [pltpu.SemaphoreType.DMA]

    def __init__(self, jobs, scratch):
        self.jobs, self.chunks, self.of = jobs, [], []
        for job in jobs:
            _, landed, _, pieces, _, _ = job
            rows = landed.shape[1] // pieces
            first = len(self.chunks)
            self.chunks += [(job, p, rows) for p in range(pieces)]
            self.of.append(range(first, len(self.chunks)))
        self.send, self.recv, self.relay_send, self.relay_recv, self.load_sem = scratch
        self.me = lax.axis_index("dp")

    def part(self, c, block):
        (source, landed, *_), p, rows = self.chunks[c]
        return source.at[pl.ds(pl.multiple_of(block * landed.shape[1] + p * rows, 16), rows)]

    def place(self, c, sender):
        (_, landed, *_), p, rows = self.chunks[c]
        return landed.at[sender, pl.ds(p * rows, rows)]

    def relay(self, c):
        (*_, relay, _), p, _ = self.chunks[c]
        return relay.at[p]

    def direct(self, c, to, source=None):
        return pltpu.make_async_remote_copy(
            src_ref=self.part(c, to) if source is None else source,
            dst_ref=self.place(c, self.me),
            send_sem=self.send.at[c, to],
            recv_sem=self.recv.at[c, self.me],
            device_id={"dp": to},
            device_id_type=MESH,
        )

    def by_middle(self, c, block, to):
        return pltpu.make_async_remote_copy(
            src_ref=self.part(c, block),
            dst_ref=self.relay(c),
            send_sem=self.relay_send.at[c],
            recv_sem=self.relay_recv.at[c],
            device_id={"dp": to},
            device_id_type=MESH,
        )

    def among(self, places):
        return functools.reduce(jnp.logical_or, [self.me == z for z in places])

    DIRECT = ((1,), (0, 2, 3), (0, 1, 3), (2,))
    ROUND = ((0, 3, 1), (3, 0, 2))

    def start(self, chunks):
        for c in chunks:
            for end, block, middle in self.ROUND:
                pl.when(self.me == end)(
                    lambda c=c, block=block, middle=middle: self.by_middle(c, block, middle).start()
                )
            for to, senders in enumerate(self.DIRECT):
                pl.when(self.among(senders))(lambda c=c, to=to: self.direct(c, to).start())

    def hand_on(self, chunks):
        for c in chunks:
            *_, other = self.chunks[c][0]
            for _, block, middle in self.ROUND:

                @pl.when(self.me == middle)
                def _(c=c, block=block, middle=middle, other=other):
                    mine = pltpu.make_async_copy(self.part(c, block), other, self.load_sem)
                    mine.start()
                    self.by_middle(c, block, middle).wait_recv()
                    mine.wait()
                    relay = self.relay(c)
                    value = relay[...].astype(SINGLE) + other[...].astype(SINGLE)
                    relay[...] = value.astype(HALF)
                    self.direct(c, block, relay).start()

    def begin(self, ahead):
        self.ahead, self.done = ahead, 0
        self.start(range(ahead))

    def tick(self, count=1):
        for _ in range(count):
            self.hand_on([self.done])
            if self.done + self.ahead < len(self.chunks):
                self.start([self.done + self.ahead])
            self.done += 1

    SENDERS = ((1, 2), (0, 2, 3), (0, 1, 3), (1, 2))

    def collect(self, j):
        source, landed, target, _, _, _ = self.jobs[j]
        for c in self.of[j]:
            for sender in range(self.COUNT):
                takers = [z for z in range(self.COUNT) if sender in self.SENDERS[z]]
                pl.when(self.among(takers))(
                    lambda c=c, sender=sender: self.wait_from(c, sender)
                )
        rows, columns = target.shape
        tile = rows // 2 if rows >= 256 else rows

        def add(*refs):
            value = refs[0][...].astype(SINGLE)
            for ref in refs[1:-1]:
                value = value + ref[0].astype(SINGLE)
            refs[-1][...] = value

        def run(senders):
            pltpu.emit_pipeline(
                add,
                grid=(rows // tile,),
                in_specs=[
                    pl.BlockSpec((tile, columns), lambda t: (self.me * (rows // tile) + t, 0))
                ]
                + [
                    pl.BlockSpec((1, tile, columns), lambda t, sender=sender: (sender, t, 0))
                    for sender in senders
                ],
                out_specs=[pl.BlockSpec((tile, columns), lambda t: (t, 0))],
            )(source, *[landed] * len(senders), target)

        pl.when(self.among((0, 3)))(lambda: run((1, 2)))
        pl.when(self.among((1, 2)))(lambda: run((0, 3 - self.me, 3)))

    def wait_from(self, c, sender):
        pltpu.make_async_remote_copy(
            src_ref=self.place(c, sender),
            dst_ref=self.place(c, sender),
            send_sem=self.relay_send.at[c],
            recv_sem=self.recv.at[c, sender],
            device_id={"dp": 0},
            device_id_type=MESH,
        ).wait_recv()

    def settle(self):
        for c in range(len(self.chunks)):
            for to, senders in enumerate(self.DIRECT):
                pl.when(self.among(senders))(lambda c=c, to=to: self.direct(c, to).wait_send())
            for end, block, middle in self.ROUND:
                pl.when(self.me == end)(
                    lambda c=c, block=block, middle=middle: self.by_middle(
                        c, block, middle
                    ).wait_send()
                )
                pl.when(self.me == middle)(
                    lambda c=c, block=block: self.direct(c, block, self.relay(c)).wait_send()
                )


def positions(lens_ref, first, shape):
    place = lax.broadcasted_iota(jnp.int32, shape, 0) + first
    begin = jnp.zeros(shape, jnp.int32)
    total = 0
    for j in range(lens_ref.shape[1]):
        total = total + lens_ref[0, j]
        begin = jnp.where(place >= total, total, begin)
    return place - begin, place < total


def split_dot(dot, left, right):
    high = left.astype(HALF)
    low = (left - high.astype(SINGLE)).astype(HALF)
    return dot(high, right) + dot(low, right)


def lane_tiles(width):
    return [(t, t * 128, min(128, width - t * 128)) for t in range(-(-width // 128))]


def put_tiles(ref, value):
    for t, first, lanes in lane_tiles(value.shape[1]):
        ref[t, :, :lanes] = value[:, first : first + lanes]


def scan_start(tiles, lanes):
    return [(jnp.zeros((lanes, 128), SINGLE), jnp.ones((lanes, 128), SINGLE)) for _ in tiles]


def sigmoid(v):
    return 1.0 / (1.0 + jnp.exp(-v))


def forward_step(
    step,
    lens_ref,
    x_ref,
    gain_ref,
    pack_ref,
    bin_ref,
    ba_ref,
    chan_ref,
    n1_ref,
    bx_ref,
    by_ref,
    conv_ref,
    gi_ref,
    ra_ref,
    h_ref,
    ob_ref,
    taps,
    coef,
    drive,
    carry,
):
    rows, width = bx_ref.shape
    depth = pack_ref.shape[2]
    lanes = 8
    span = rows // lanes

    @pl.when(step == 0)
    def _():
        taps[...] = jnp.zeros_like(taps)
        carry[...] = jnp.zeros_like(carry)
        coef[...] = jnp.zeros_like(coef)
        drive[...] = jnp.zeros_like(drive)

    x = x_ref[...].astype(SINGLE)
    scale = lax.rsqrt(jnp.mean(x * x, axis=-1, keepdims=True) + EPS)
    normed = (x * scale * gain_ref[...]).astype(HALF)
    n1_ref[...] = normed
    total = None
    for d in range(pack_ref.shape[0]):
        term = dot_nt(normed[:, d * depth : (d + 1) * depth], pack_ref[d, : 2 * width, :])
        total = term if total is None else total + term
    bx = total[:, :width].astype(HALF)
    by = total[:, width:]
    bx_ref[...] = bx
    by_ref[...] = by
    pos, live = positions(lens_ref, step * rows, (rows, width))
    taps[0:8, :] = taps[rows : rows + 8, :]
    taps[8 : rows + 8, :] = bx.astype(SINGLE)
    conv = jnp.zeros((rows, width), SINGLE) + chan_ref[CONV : CONV + 1, :]
    for k in range(CONV):
        moved = taps[8 - k : 8 - k + rows, :]
        conv = conv + jnp.where(pos >= k, moved * chan_ref[k : k + 1, :], 0.0)
    conv_ref[...] = conv
    high = conv.astype(HALF)
    low = (conv - high.astype(SINGLE)).astype(HALF)
    gate_in = sigmoid(
        dot_nn(high, bin_ref[...]) + dot_nn(low, bin_ref[...]) + chan_ref[CONV + 1 : CONV + 2, :]
    )
    gate_a = sigmoid(
        dot_nn(high, ba_ref[...]) + dot_nn(low, ba_ref[...]) + chan_ref[CONV + 2 : CONV + 3, :]
    )
    gi_ref[...] = gate_in
    ra_ref[...] = gate_a
    decay = jnp.exp(-DECAY * gate_a * chan_ref[CONV + 4 : CONV + 5, :])
    root = jnp.sqrt(1.0 - decay * decay)
    put_tiles(coef, jnp.where(pos == 0, 0.0, decay))
    put_tiles(drive, gate_in * conv * root)
    tiles = lane_tiles(width)

    def scan(i, state):
        at = pl.ds(i, lanes, stride=span)
        result = []
        for (t, _, _), (h, prod) in zip(tiles, state):
            a = coef[t, at, :]
            h = a * h + drive[t, at, :]
            prod = prod * a
            drive[t, at, :] = h
            coef[t, at, :] = prod
            result.append((h, prod))
        return result

    state = lax.fori_loop(0, span, scan, scan_start(tiles, lanes), unroll=4)
    for (t, first, used), (h, prod) in zip(tiles, state):
        running = carry[t, 0:1, :]
        for s in range(lanes):
            at = slice(s * span, (s + 1) * span)
            value = drive[t, at, :] + coef[t, at, :] * running
            h_ref[at, first : first + used] = value[:, :used]
            running = h[s : s + 1, :] + prod[s : s + 1, :] * running
        carry[t, 0:1, :] = running
    mixed = h_ref[...].astype(HALF).astype(SINGLE)
    ob_ref[...] = jnp.where(live, gelu(by) * mixed, 0.0).astype(HALF)


def forward_kernel(*refs):
    forward_step(pl.program_id(0), *refs)


def forward_scratch(rows, width):
    tiles = len(lane_tiles(width))
    return [
        pltpu.VMEM((rows + 8, width), SINGLE),
        pltpu.VMEM((tiles, rows, 128), SINGLE),
        pltpu.VMEM((tiles, rows, 128), SINGLE),
        pltpu.VMEM((tiles, 8, 128), SINGLE),
    ]


def forward_channels(lens, x_all, gain, pack, blocks_in, blocks_a, chan):
    tokens, model = x_all.shape
    width = chan.shape[1]
    count = lax.axis_size("mp")
    rows = tokens // count
    whole = lambda shape: pl.BlockSpec(shape, lambda i: (0,) * len(shape))
    part = pl.BlockSpec((rows, width), lambda i: (i, 0))
    full = lambda kind: jax.ShapeDtypeStruct((tokens, width), kind)
    return pl.pallas_call(
        forward_kernel,
        grid=(count,),
        out_shape=(
            jax.ShapeDtypeStruct((tokens, model), HALF),
            full(HALF),
            full(SINGLE),
            full(SINGLE),
            full(SINGLE),
            full(SINGLE),
            full(SINGLE),
            full(HALF),
        ),
        in_specs=[
            pl.BlockSpec(memory_space=pltpu.SMEM),
            pl.BlockSpec((rows, model), lambda i: (i, 0)),
            whole(gain.shape),
            whole(pack.shape),
            whole(blocks_in.shape),
            whole(blocks_a.shape),
            whole(chan.shape),
        ],
        out_specs=(pl.BlockSpec((rows, model), lambda i: (i, 0)),) + (part,) * 7,
        scratch_shapes=forward_scratch(rows, width),
        compiler_params=pltpu.CompilerParams(vmem_limit_bytes=VMEM_BYTES),
        cost_estimate=pl.CostEstimate(
            flops=2 * tokens * model * 2 * width,
            bytes_accessed=tokens * (model * 4 + width * 24),
            transcendentals=8 * tokens * width,
        ),
        name="forward_channels",
    )(lens, x_all, gain, pack, blocks_in, blocks_a, chan)


def by_parts(left, right, t, columns):
    return dot_nn(left, right[t])


def backward_step(
    step,
    steps,
    lens_ref,
    dt_ref,
    pack_ref,
    bin_ref,
    ba_ref,
    chan_ref,
    bx_ref,
    by_ref,
    conv_ref,
    gi_ref,
    ra_ref,
    h_ref,
    hprev_ref,
    dbx_ref,
    dby_ref,
    gin_ref,
    ga_ref,
    gchan_ref,
    lift,
    coef,
    drive,
    carry,
):
    chunk = steps - 1 - step
    rows, width = bx_ref.shape
    depth = pack_ref.shape[2]
    lanes = 8
    span = rows // lanes

    @pl.when(step == 0)
    def _():
        lift[...] = jnp.zeros_like(lift)
        carry[...] = jnp.zeros_like(carry)
        coef[...] = jnp.zeros_like(coef)
        drive[...] = jnp.zeros_like(drive)
        gin_ref[...] = jnp.zeros_like(gin_ref)
        ga_ref[...] = jnp.zeros_like(ga_ref)
        gchan_ref[...] = jnp.zeros_like(gchan_ref)

    d_out = None
    for d in range(pack_ref.shape[0]):
        term = dot_nt(dt_ref[:, d * depth : (d + 1) * depth], pack_ref[d])
        d_out = term if d_out is None else d_out + term
    pos, live = positions(lens_ref, chunk * rows, (rows, width))
    by = by_ref[...]
    h = h_ref[...]
    side, slope = gelu_both(by)
    d_out = jnp.where(live, d_out, 0.0)
    dby_ref[...] = (d_out * h.astype(HALF).astype(SINGLE) * slope).astype(HALF)
    gate_a = ra_ref[...]
    soft = chan_ref[CONV + 4 : CONV + 5, :]
    decay = jnp.exp(-DECAY * gate_a * soft)
    put_tiles(coef, jnp.where(pos == 0, 0.0, decay))
    put_tiles(drive, (d_out * side).astype(HALF).astype(SINGLE))
    tiles = lane_tiles(width)

    def scan(j, state):
        at = pl.ds(span - 1 - j, lanes, stride=span)
        result = []
        for (t, _, _), (after, prod) in zip(tiles, state):
            a = coef[t, at, :]
            lam = drive[t, at, :] + after
            drive[t, at, :] = lam
            coef[t, at, :] = prod
            result.append((a * lam, prod * a))
        return result

    state = lax.fori_loop(0, span, scan, scan_start(tiles, lanes), unroll=4)
    for (t, first, used), (after, prod) in zip(tiles, state):
        running = carry[t, 0:1, :]
        for s in reversed(range(lanes)):
            at = slice(s * span, (s + 1) * span)
            value = drive[t, at, :] + coef[t, at, :] * running
            lift[at, first : first + used] = value[:, :used]
            running = after[s : s + 1, :] + prod[s : s + 1, :] * running
        carry[t, 0:1, :] = running
    lam = lift[0:rows, :]
    last = jnp.where(chunk > 0, hprev_ref[7:8, :], 0.0)
    before = jnp.concatenate([last, h[: rows - 1, :]], axis=0)
    before = jnp.where(pos == 0, 0.0, before)
    conv = conv_ref[...]
    gate_in = gi_ref[...]
    root = jnp.sqrt(1.0 - decay * decay)
    d_decay = lam * before - lam * gate_in * conv * decay / root
    d_log = d_decay * decay
    d_a = d_log * (-DECAY * soft)
    d_in = lam * conv * root
    d_logit_in = d_in * gate_in * (1.0 - gate_in)
    d_logit_a = d_a * gate_a * (1.0 - gate_a)
    d_conv = (
        lam * gate_in * root
        + split_dot(dot_nt, d_logit_in, bin_ref[...])
        + split_dot(dot_nt, d_logit_a, ba_ref[...])
    )
    low = conv.astype(HALF)
    gin_ref[...] += dot_tn(low, d_logit_in.astype(HALF))
    ga_ref[...] += dot_tn(low, d_logit_a.astype(HALF))
    lift[0:rows, :] = d_conv
    bx = bx_ref[...].astype(SINGLE)
    d_bx = jnp.zeros((rows, width), SINGLE)
    for k in range(CONV):
        if k:
            ahead, _ = positions(lens_ref, chunk * rows + k, (rows, width))
            moved = jnp.where(ahead >= k, lift[k : k + rows, :], 0.0)
        else:
            moved = d_conv
        d_bx = d_bx + moved * chan_ref[k : k + 1, :]
        gchan_ref[k : k + 1, :] += jnp.sum(moved * bx, axis=0, keepdims=True)
    dbx_ref[...] = d_bx.astype(HALF)
    lift[rows : rows + 8, :] = d_conv[0:8, :]
    sums = (d_conv, d_logit_in, d_logit_a, d_log * gate_a)
    for j, value in enumerate(sums):
        gchan_ref[CONV + j : CONV + j + 1, :] += jnp.sum(value, axis=0, keepdims=True)


def backward_kernel(*refs):
    refs = list(refs)
    inputs, (ob_ref, n1_ref), outputs, grads_ref, grads, scratch = (
        refs[:13], refs[13:15], refs[15:20], refs[20], refs[21], refs[22:],
    )
    step, steps = pl.program_id(0), pl.num_programs(0)

    @pl.when(step == 0)
    def _():
        grads[...] = jnp.zeros_like(grads)

    backward_step(step, steps, *inputs, *outputs, *scratch)
    dt_ref, (dbx_ref, dby_ref) = inputs[1], outputs[:2]
    width, depth = dbx_ref.shape[1], grads.shape[2]
    lefts = (dbx_ref[...], dby_ref[...], ob_ref[...])
    for d in range(grads.shape[0]):
        columns = slice(d * depth, (d + 1) * depth)
        rights = (n1_ref[:, columns], n1_ref[:, columns], dt_ref[:, columns])
        for j, (left, right) in enumerate(zip(lefts, rights)):
            grads[d, j * width : (j + 1) * width, :] += dot_tn(left, right)

    @pl.when(step == steps - 1)
    def _():
        grads_ref[...] = grads[...].astype(HALF)


def backward_channels(lens, dt_all, pack, blocks_in, blocks_a, chan, saved):
    bx, by, conv, gate_in, gate_a, h, ob, n1 = saved
    tokens, model = dt_all.shape
    width = chan.shape[1]
    count = lax.axis_size("mp")
    rows = tokens // count
    last = count - 1
    whole = lambda shape: pl.BlockSpec(shape, lambda i: (0,) * len(shape))
    part = pl.BlockSpec((rows, width), lambda i: (last - i, 0))
    across = pl.BlockSpec((rows, model), lambda i: (last - i, 0))
    before = pl.BlockSpec(
        (8, width), lambda i: (jnp.maximum((last - i) * (rows // 8) - 1, 0), 0)
    )
    full = jax.ShapeDtypeStruct((tokens, width), HALF)
    square = jax.ShapeDtypeStruct((width, width), SINGLE)
    grads = (pack.shape[0], 3 * width, pack.shape[2])
    return pl.pallas_call(
        backward_kernel,
        grid=(count,),
        out_shape=(
            full,
            full,
            square,
            square,
            jax.ShapeDtypeStruct((8, width), SINGLE),
            jax.ShapeDtypeStruct(grads, HALF),
        ),
        in_specs=[
            pl.BlockSpec(memory_space=pltpu.SMEM),
            across,
            whole(pack.shape),
            whole(blocks_in.shape),
            whole(blocks_a.shape),
            whole(chan.shape),
            part,
            part,
            part,
            part,
            part,
            part,
            before,
            part,
            across,
        ],
        out_specs=(
            part,
            part,
            whole((width, width)),
            whole((width, width)),
            whole((8, width)),
            whole(grads),
        ),
        scratch_shapes=[pltpu.VMEM(grads, SINGLE)] + forward_scratch(rows, width),
        compiler_params=pltpu.CompilerParams(vmem_limit_bytes=VMEM_BYTES),
        cost_estimate=pl.CostEstimate(
            flops=8 * tokens * model * width,
            bytes_accessed=tokens * (model * 4 + width * 28),
            transcendentals=8 * tokens * width,
        ),
        name="backward_channels",
    )(
        lens, dt_all, pack, blocks_in, blocks_a, chan,
        bx, by, conv, gate_in, gate_a, h, h, ob, n1,
    )


def log_one_plus(v):
    total = 1.0 + v
    exact = total - 1.0
    return jnp.where(exact == 0.0, v, jnp.log(total) * (v / jnp.where(exact == 0.0, 1.0, exact)))


def small_weights(small, bin_ref, ba_ref, chan_ref, heads, bite):
    parts = small.shape[0]
    width = bin_ref.shape[0]
    block = width // heads
    at_row = lax.broadcasted_iota(jnp.int32, (block, width), 0)
    at_column = lax.broadcasted_iota(jnp.int32, (block, width), 1)
    each = 2 * CONV // parts
    for d in range(parts):
        value = small[d].astype(SINGLE)
        for h in range(heads):
            place = (at_column == at_row + h * block).astype(HALF)
            for lane, target in ((0, bin_ref), (256, ba_ref)):
                piece = value[h * bite : (h + 1) * bite, lane : lane + block].astype(HALF)
                first = h * block + d * bite
                target[first : first + bite, :] = dot_nn(piece, place)
        row = heads * bite
        chan_ref[d * each : (d + 1) * each, :] = value[row : row + each, :width]
    v = -chan_ref[2 * CONV - 1 : 2 * CONV, :]
    chan_ref[2 * CONV : 2 * CONV + 1, :] = jnp.maximum(v, 0.0) + log_one_plus(
        jnp.exp(-jnp.abs(v))
    )


class ForwardIn(typing.NamedTuple):
    lens: typing.Any
    gains: typing.Any
    x: typing.Any
    cot: typing.Any
    small: typing.Any
    pack: typing.Any
    out: typing.Any
    down: typing.Any
    gate: typing.Any
    up: typing.Any


class ForwardOut(typing.NamedTuple):
    gain: typing.Any
    bin: typing.Any
    ba: typing.Any
    chan: typing.Any
    x_all: typing.Any
    c_all: typing.Any
    n2_all: typing.Any
    n1: typing.Any
    residual: typing.Any
    bx: typing.Any
    by: typing.Any
    conv: typing.Any
    gi: typing.Any
    ra: typing.Any
    h: typing.Any
    ob: typing.Any
    small4: typing.Any
    pack4: typing.Any
    out4: typing.Any
    gate4: typing.Any
    up4: typing.Any
    down4: typing.Any
    act: typing.Any
    hidden: typing.Any
    d_up: typing.Any
    d_gate: typing.Any
    grad_down: typing.Any


WEIGHT_PIECES = (1, 4, 2, 4, 4, 6)


def forward_pass_kernel(heads, bite, *refs):
    refs = list(refs)
    take = lambda n: [refs.pop(0) for _ in range(n)]
    i = ForwardIn(*take(len(ForwardIn._fields)))
    o = ForwardOut(*take(len(ForwardOut._fields)))
    tiles, bin32, ba32 = take(3)
    pack, out_w, down, gate, up = take(5)
    steps_scratch = take(4)
    ob, inputs, summed, n2_own, slope, hidden = take(6)
    load_sem, store_sem = take(2)
    share_sems = take(4)
    plane_x = PlaneGather(i.x, o.x_all, take(3))
    plane_c = PlaneGather(i.cot, o.c_all, take(3))
    plane_n = PlaneGather(n2_own, o.n2_all, take(3))
    plane = PlaneSum([by_parts], out_w.shape[2], [ob], [out_w], take(10))
    line = LineGather(
        list(
            zip(
                (i.small, i.pack, i.out, i.gate, i.up, i.down),
                (o.small4, o.pack4, o.out4, o.gate4, o.up4, o.down4),
                WEIGHT_PIECES,
            )
        ),
        refs,
    )
    small_at, pack_at, out_at, gate_at, up_at, down_at = line.of
    tokens, model = o.x_all.shape
    rows, count, width = i.x.shape[0], PlaneGather.COUNT, ob.shape[1]
    parts, _, depth = pack.shape

    greet(ring_peers("mp") + ring_peers("dp"))
    line.begin(AHEAD)
    gains_way, copies = share(i.gains, tiles, share_sems)
    plane_x.start()
    own_rows = pltpu.make_async_copy(i.x, inputs, load_sem.at[0])
    own_rows.start()
    bin32[...] = jnp.zeros_like(bin32)
    ba32[...] = jnp.zeros_like(ba32)
    o.chan[...] = jnp.zeros_like(o.chan)
    line.tick(2)
    plane_x.level(1)
    line.tick()
    plane_x.level(2)
    line.tick()
    plane_x.finish()
    plane_c.start()
    line.tick()
    for copy in gains_way:
        copy.wait_recv()
    group = 128 // (model // tiles.shape[0])
    for j in range(model // 128):
        value = tiles[group * j]
        for k in range(1, group):
            value = value + tiles[group * j + k]
        o.gain[:, j * 128 : (j + 1) * 128] = value
    line.landed(small_at)
    line.landed(pack_at)
    own_rows.wait()

    def load(source, target, j):
        copy = pltpu.make_async_copy(source, target, load_sem.at[j])
        copy.start()
        return copy

    loads = [load(o.pack4, pack, 1)]

    def with_small(small):
        copy = load(o.small4, small, 2)
        copy.wait()
        small_weights(small, bin32, ba32, o.chan, heads, bite)

    pl.run_scoped(with_small, pltpu.VMEM(o.small4.shape, HALF))
    o.bin[...] = bin32[...].astype(HALF)
    o.ba[...] = ba32[...].astype(HALF)
    loads[0].wait()

    def channels(x_tile, n1, bx, by, conv, gi, ra, h, ob_tile):
        step = pl.program_id(0)
        schedule = {
            2: line.tick,
            3: lambda: plane_c.level(1),
            4: line.tick,
            6: lambda: plane_c.level(2),
            7: line.tick,
        }
        for when, act in schedule.items():
            pl.when(step == when)(lambda act=act: (act(), None)[1])
        forward_step(
            step, i.lens, x_tile, o.gain.at[0:1], pack, o.bin, o.ba, o.chan,
            n1, bx, by, conv, gi, ra, h, ob_tile, *steps_scratch,
        )
        ob[pl.ds(pl.multiple_of(step * rows, rows), rows), :] = ob_tile[...]

    part = pl.BlockSpec((rows, width), lambda t: (t, 0))
    across = pl.BlockSpec((rows, model), lambda t: (t, 0))
    pltpu.emit_pipeline(
        channels,
        grid=(count,),
        in_specs=[across],
        out_specs=[across] + [part] * 7,
    )(o.x_all, o.n1, o.bx, o.by, o.conv, o.gi, o.ra, o.h, o.ob)
    line.landed(out_at)
    load(o.out4, out_w, 1).wait()
    plane.spread(line.tick)
    line.tick()
    plane_c.finish()
    line.tick()
    plane.finish(summed)

    def norm(t, carry):
        at = pl.ds(pl.multiple_of(t * 32, 32), 32)
        value = inputs[at, :].astype(SINGLE) + summed[at, :]
        scale = lax.rsqrt(jnp.mean(value * value, axis=-1, keepdims=True) + EPS)
        summed[at, :] = value
        n2_own[at, :] = (value * scale * o.gain[1:2, :]).astype(HALF)
        return carry

    lax.fori_loop(0, rows // 32, norm, 0)
    plane_n.start()
    stores = [pltpu.make_async_copy(summed, o.residual, store_sem)]
    stores[0].start()
    line.tick(2)
    plane_n.level(1)
    line.tick()
    plane_n.level(2)
    line.tick()
    plane_n.finish()
    line.landed(gate_at)
    line.landed(up_at)
    loads = [load(o.gate4, gate, 0), load(o.up4, up, 1)]
    for copy in loads:
        copy.wait()

    units = hidden.shape[1]
    thirds = [down_at[j : j + 2] for j in range(0, len(down_at), 2)]
    third = units // len(thirds)
    along = pl.BlockSpec((rows, units), lambda t: (t, 0))
    here = lambda: pl.ds(pl.multiple_of(pl.program_id(0) * rows, rows), rows)

    def blocks(left, right):
        value = None
        for d in range(parts):
            term = right(left[:, d * depth : (d + 1) * depth], d)
            value = term if value is None else value + term
        return value

    def activations(n2, act_tile, hidden_tile):
        for when in (3, 6):
            pl.when(pl.program_id(0) == when)(line.tick)
        value, rise = gelu_both(blocks(n2, lambda v, d: dot_nn(v, gate[d])))
        act_tile[...] = value
        above = blocks(n2, lambda v, d: dot_nn(v, up[d]))
        low = (value * above).astype(HALF)
        hidden_tile[...] = low
        hidden[here(), :] = low
        slope[here(), :] = rise * above

    pltpu.emit_pipeline(
        activations, grid=(count,), in_specs=[across], out_specs=[along, along]
    )(o.n2_all, o.act, o.hidden)
    beside_products([(o.c_all, hidden, o.grad_down)])
    line.tick()

    def gradients(act, total):
        for p, pieces in enumerate(thirds):
            if p:
                line.tick(pieces[-1] + 1 - line.done)
            span = pl.ds(p * third, third)
            act_load = load(o.act.at[:, span], act, 1)
            line.landed(pieces)
            load(o.down4.at[:, span], down.at[:, span], 0).wait()
            act_load.wait()

            def backs(c_tile, d_up_tile, d_gate_tile):
                d = pl.program_id(0)
                term = dot_nt(c_tile[...], down[d, span])

                @pl.when(d == 0)
                def _():
                    total[...] = term

                @pl.when(d > 0)
                def _():
                    total[...] += term

                @pl.when(d == parts - 1)
                def _():
                    def step(t, carry):
                        at = pl.ds(pl.multiple_of(t * 128, 128), 128)
                        back = total[at, :]
                        d_up_tile[at, :] = (back * act[at, :]).astype(HALF)
                        d_gate_tile[at, :] = (back * slope[at, span]).astype(HALF)
                        return carry

                    lax.fori_loop(0, tokens // 128, step, 0)

            piece = pl.BlockSpec((tokens, third), lambda d: (0, p))
            pltpu.emit_pipeline(
                backs,
                grid=(parts,),
                in_specs=[pl.BlockSpec((tokens, depth), lambda d: (0, d))],
                out_specs=[piece, piece],
            )(o.c_all, o.d_up, o.d_gate)

    pl.run_scoped(
        gradients, pltpu.VMEM((tokens, third), SINGLE), pltpu.VMEM((tokens, third), SINGLE)
    )
    line.settle()
    stores[0].wait()
    for copy in copies:
        copy.wait_send()


def forward_pass(lens, gains, x, cot, small, pack, out, down, gate, up, heads, bite, collective_id):
    parts, count = LineGather.COUNT, PlaneGather.COUNT
    rows, model = x.shape
    tokens = rows * count
    width, depth = out.shape
    units = down.shape[0]
    shape = jax.ShapeDtypeStruct
    four = lambda v: shape((parts,) + v.shape, HALF)
    plane_rows = shape((tokens, model), HALF)
    channel = shape((tokens, width), SINGLE)
    channel_low = shape((tokens, width), HALF)
    along = shape((tokens, units), HALF)
    square = shape((width, width), HALF)
    shapes = ForwardOut(
        gain=shape((8, model), SINGLE),
        bin=square,
        ba=square,
        chan=shape((16, width), SINGLE),
        x_all=plane_rows,
        c_all=plane_rows,
        n2_all=plane_rows,
        n1=plane_rows,
        residual=shape((rows, model), SINGLE),
        bx=channel_low,
        by=channel,
        conv=channel,
        gi=channel,
        ra=channel,
        h=channel,
        ob=channel_low,
        small4=four(small),
        pack4=four(pack),
        out4=four(out),
        gate4=four(gate),
        up4=four(up),
        down4=four(down),
        act=shape((tokens, units), SINGLE),
        hidden=along,
        d_up=along,
        d_gate=along,
        grad_down=shape((model, units), HALF),
    )
    in_vmem, in_hbm = pl.BlockSpec(memory_space=pltpu.VMEM), pl.BlockSpec(memory_space=pl.ANY)
    in_specs = ForwardIn(*[in_hbm] * len(ForwardIn._fields))._replace(
        lens=pl.BlockSpec(memory_space=pltpu.SMEM), gains=in_vmem
    )
    out_specs = ForwardOut(*[in_hbm] * len(shapes))._replace(
        gain=in_vmem, bin=in_vmem, ba=in_vmem, chan=in_vmem
    )
    inner, outer = lax.axis_size("mp"), lax.axis_size("dp")
    vmem = lambda v: pltpu.VMEM(v.shape, v.dtype)
    outs = pl.pallas_call(
        functools.partial(forward_pass_kernel, heads, bite),
        out_shape=list(shapes),
        in_specs=list(in_specs),
        out_specs=list(out_specs),
        scratch_shapes=[
            pltpu.VMEM((inner * outer,) + gains.shape, SINGLE),
            pltpu.VMEM((width, width), SINGLE),
            pltpu.VMEM((width, width), SINGLE),
        ]
        + [
            vmem(v) for v in (shapes.pack4, shapes.out4, shapes.down4, shapes.gate4, shapes.up4)
        ]
        + forward_scratch(rows, width)
        + [
            pltpu.VMEM((tokens, width), HALF),
            pltpu.VMEM((rows, model), HALF),
            pltpu.VMEM((rows, model), SINGLE),
            pltpu.VMEM((rows, model), HALF),
            pltpu.VMEM((tokens, units), SINGLE),
            pltpu.VMEM((tokens, units), HALF),
            pltpu.SemaphoreType.DMA((3,)),
            pltpu.SemaphoreType.DMA,
        ]
        + [pltpu.SemaphoreType.DMA((c,)) for c in (inner, inner, outer, outer)]
        + PlaneGather.scratch() * 3
        + PlaneSum.scratch(rows, model)
        + LineGather.scratch(sum(WEIGHT_PIECES)),
        compiler_params=kernel_params(collective_id),
        cost_estimate=pl.CostEstimate(
            flops=10 * tokens * model * units,
            bytes_accessed=40 * tokens * model,
            transcendentals=tokens * units,
        ),
        name="forward_pass",
    )(lens, gains, x, cot, small, pack, out, down, gate, up)
    return ForwardOut(*outs)


class BackwardIn(typing.NamedTuple):
    lens: typing.Any
    gain: typing.Any
    bin: typing.Any
    ba: typing.Any
    chan: typing.Any
    x: typing.Any
    cot: typing.Any
    residual: typing.Any
    n2_all: typing.Any
    n1: typing.Any
    bx: typing.Any
    by: typing.Any
    conv: typing.Any
    gi: typing.Any
    ra: typing.Any
    h: typing.Any
    ob: typing.Any
    hidden: typing.Any
    d_up: typing.Any
    d_gate: typing.Any
    grad_down: typing.Any
    out4: typing.Any
    pack4: typing.Any
    gate4: typing.Any
    up4: typing.Any
    down4: typing.Any


class BackwardOut(typing.NamedTuple):
    layer_output: typing.Any
    grad_input: typing.Any
    gain_grads: typing.Any
    dt_all: typing.Any
    grad_gate: typing.Any
    grad_up: typing.Any
    grad_out: typing.Any
    grad_pack: typing.Any
    landed_down: typing.Any
    landed_gate: typing.Any
    landed_up: typing.Any
    landed_out: typing.Any
    landed_pack: typing.Any
    landed_small: typing.Any
    sum_down: typing.Any
    sum_gate: typing.Any
    sum_up: typing.Any
    sum_out: typing.Any
    sum_pack: typing.Any
    sum_small: typing.Any


SUM_PIECES = (4, 4, 4, 2, 4, 1)


def small_gradients(small, gin, ga, gchan, chan, heads, bite):
    parts = LineSum.COUNT
    width = gin.shape[0]
    block = width // heads
    each = 2 * CONV // parts
    rows = small.shape[0] // parts
    at_row = lax.broadcasted_iota(jnp.int32, (block, width), 0)
    at_column = lax.broadcasted_iota(jnp.int32, (block, width), 1)
    small[...] = jnp.zeros_like(small)
    v = chan[2 * CONV - 1 : 2 * CONV, :]
    last = 2 * CONV - 1
    gchan[last : last + 1, :] = gchan[last : last + 1, :] * (DECAY * sigmoid(-v))
    for d in range(parts):
        for h in range(heads):
            place = (at_column == at_row + h * block).astype(HALF)
            first = h * block + d * bite
            to = d * rows + h * bite
            for lane, grads in ((0, gin), (256, ga)):
                piece = grads[first : first + bite, :].astype(HALF)
                small[to : to + bite, lane : lane + block] = dot_nt(piece, place)
        to = d * rows + heads * bite
        small[to : to + each, :width] = gchan[d * each : (d + 1) * each, :]


def backward_pass_kernel(heads, bite, *refs):
    refs = list(refs)
    take = lambda n: [refs.pop(0) for _ in range(n)]
    i = BackwardIn(*take(len(BackwardIn._fields)))
    o = BackwardOut(*take(len(BackwardOut._fields)))
    x, cot, residual, d_res, summed, dt_own, gain_sum = take(7)
    steps_scratch = take(4)
    gin, ga, gchan, small32, small = take(5)
    tiles, tiles_dp, tiles_mp = take(3)
    relays, others = take(6), take(6)
    load_sem, out_sem = take(2)
    total_sems = take(4)
    outward = [
        pltpu.make_async_copy(dt_own, o.layer_output, out_sem.at[0]),
        pltpu.make_async_copy(d_res, o.grad_input, out_sem.at[1]),
    ]
    plane_t = PlaneGather(dt_own, o.dt_all, take(3))
    shared = take(10)
    (free_sem,) = take(1)
    sources = (i.grad_down, o.grad_gate, o.grad_up, o.grad_out, o.grad_pack, small)
    landed = (
        o.landed_down, o.landed_gate, o.landed_up, o.landed_out, o.landed_pack, o.landed_small,
    )
    targets = (o.sum_down, o.sum_gate, o.sum_up, o.sum_out, o.sum_pack, o.sum_small)
    line = LineSum(list(zip(sources, landed, targets, SUM_PIECES, relays, others)), refs)
    tokens, model = o.dt_all.shape
    rows, width, units = x.shape[0], i.bx.shape[1], i.hidden.shape[1]
    count = PlaneGather.COUNT
    parts, _, depth = i.pack4.shape

    greet(ring_peers("mp") + ring_peers("dp"))
    line.begin(AHEAD)

    def load(pairs):
        copies = [
            pltpu.make_async_copy(source, target, load_sem.at[j])
            for j, (source, target) in enumerate(pairs)
        ]
        for copy in copies:
            copy.start()
        for copy in copies:
            copy.wait()

    def mlp(d_gate, d_up, gate, up):
        load(
            [
                (i.d_gate, d_gate), (i.gate4, gate), (i.d_up, d_up), (i.up4, up),
                (i.x, x), (i.cot, cot), (i.residual, residual),
            ]
        )
        by_rows = lambda left, right, t, columns: dot_nt(left, right[t])
        plane = PlaneSum([by_rows, by_rows], depth, [d_gate, d_up], [gate, up], shared)
        plane.spread(line.tick)

        def grads(n2_tile, gate_tile, up_tile):
            left = n2_tile[...]
            gate_tile[...] = dot_tn(left, d_gate[...]).astype(HALF)
            up_tile[...] = dot_tn(left, d_up[...]).astype(HALF)
            pl.when(pl.program_id(0) == 3)(line.tick)

        out_tile = pl.BlockSpec((256, units), lambda t: (t, 0))
        pltpu.emit_pipeline(
            grads,
            grid=(model // 256,),
            in_specs=[pl.BlockSpec((tokens, 256), lambda t: (0, t))],
            out_specs=[out_tile, out_tile],
        )(i.n2_all, o.grad_gate, o.grad_up)
        line.tick()
        plane.finish(summed)

    pl.run_scoped(
        mlp,
        pltpu.VMEM((tokens, units), HALF),
        pltpu.VMEM((tokens, units), HALF),
        pltpu.VMEM(i.gate4.shape, HALF),
        pltpu.VMEM(i.up4.shape, HALF),
    )
    gain_sum[...] = jnp.zeros_like(gain_sum)
    block = 32

    def norm_back(value, back, gain, row):
        scale = lax.rsqrt(jnp.mean(value * value, axis=-1, keepdims=True) + EPS)
        weighted = gain * back
        gain_sum[row : row + 1, :] += jnp.sum(back * value * scale, axis=0, keepdims=True)
        inner = jnp.mean(weighted * value, axis=-1, keepdims=True)
        return scale * weighted - value * (scale * scale * scale * inner)

    def middle(t, carry):
        at = pl.ds(pl.multiple_of(t * block, block), block)
        back = norm_back(residual[at, :], summed[at, :], i.gain[1:2, :], 1)
        back = cot[at, :].astype(SINGLE) + back
        d_res[at, :] = back
        dt_own[at, :] = back.astype(HALF)
        return carry

    lax.fori_loop(0, rows // block, middle, 0)
    plane_t.start()
    line.tick(2)
    plane_t.level(1)
    line.tick()
    plane_t.level(2)
    plane_t.finish()

    tall = pl.BlockSpec((tokens, depth), lambda t: (0, t))

    def out_gradients(ob):
        load([(i.ob, ob)])

        def body(dt_tile, out_tile):
            out_tile[...] = dot_tn(ob[...], dt_tile[...]).astype(HALF)

        pltpu.emit_pipeline(
            body,
            grid=(parts,),
            in_specs=[tall],
            out_specs=[pl.BlockSpec((width, depth), lambda t: (t, 0))],
        )(o.dt_all, o.grad_out)

    pl.run_scoped(out_gradients, pltpu.VMEM((tokens, width), HALF))
    line.tick()

    def temporal(hidden, down, out_w, d_bx, d_by):
        load([(i.hidden, hidden), (i.down4, down), (i.out4, out_w)])
        plane = PlaneSum([by_parts], depth, [hidden], [down], shared)

        def channels(dt_tile, bx, by, conv, gi, ra, h, before):
            step = pl.program_id(0)
            schedule = {
                0: lambda: (plane.send(3), plane.send(1)),
                1: lambda: (plane.take(3), plane.send(2), line.tick()),
                2: lambda: (plane.take(1), plane.send(0)),
                3: lambda: (plane.take(2), plane.take(0), line.tick()),
                5: lambda: (plane.relay(), line.tick()),
                7: line.tick,
            }
            for when, act in schedule.items():
                pl.when(step == when)(lambda act=act: (act(), None)[1])
            at = pl.ds(pl.multiple_of((count - 1 - step) * rows, rows), rows)
            backward_step(
                step, count, i.lens, dt_tile, out_w, i.bin, i.ba, i.chan,
                bx, by, conv, gi, ra, h, before, d_bx.at[at], d_by.at[at], gin, ga, gchan,
                *steps_scratch,
            )

        part = pl.BlockSpec((rows, width), lambda t: (count - 1 - t, 0))
        across = pl.BlockSpec((rows, model), lambda t: (count - 1 - t, 0))
        ahead = pl.BlockSpec(
            (8, width), lambda t: (jnp.maximum((count - 1 - t) * (rows // 8) - 1, 0), 0)
        )
        pltpu.emit_pipeline(
            channels, grid=(count,), in_specs=[across] + [part] * 6 + [ahead]
        )(o.dt_all, i.bx, i.by, i.conv, i.gi, i.ra, i.h, i.h)
        plane.finish(summed)
        for bit in plane_t.bits:
            pl.semaphore_signal(
                free_sem,
                inc=1,
                device_id={"mp": flip(lax.axis_index("mp"), bit, count)},
                device_id_type=MESH,
            )
        dt_own[...] = (residual[...] + summed[...]).astype(HALF)
        outward[0].start()
        small_gradients(small32, gin, ga, gchan, i.chan, heads, bite)
        small[...] = small32[...].astype(HALF)

    def block_input(pack, d_bx, d_by):
        pack_load = pltpu.make_async_copy(i.pack4, pack, load_sem.at[0])
        pack_load.start()

        def body(n1_tile, pack_tile):
            right = n1_tile[...]
            pack_tile[:width, :] = dot_tn(d_bx[...], right).astype(HALF)
            pack_tile[width:, :] = dot_tn(d_by[...], right).astype(HALF)

        pltpu.emit_pipeline(
            body,
            grid=(parts,),
            in_specs=[tall],
            out_specs=[pl.BlockSpec((2 * width, depth), lambda t: (t, 0))],
        )(i.n1, o.grad_pack)
        line.tick()
        pack_load.wait()
        plane = PlaneSum(
            [
                lambda left, right, t, columns: dot_nn(left, right[t, :width, :]),
                lambda left, right, t, columns: dot_nn(left, right[t, width:, :]),
            ],
            depth,
            [d_bx, d_by],
            [pack, pack],
            shared,
        )
        pl.semaphore_wait(free_sem, len(plane_t.bits))
        plane.spread(line.tick)
        line.tick()
        plane.finish(summed)

    def temporal_block(d_bx, d_by):
        pl.run_scoped(
            lambda hidden, down, out_w: temporal(hidden, down, out_w, d_bx, d_by),
            pltpu.VMEM((tokens, units), HALF),
            pltpu.VMEM(i.down4.shape, HALF),
            pltpu.VMEM(i.out4.shape, HALF),
        )
        pl.run_scoped(
            lambda pack: block_input(pack, d_bx, d_by), pltpu.VMEM(i.pack4.shape, HALF)
        )

    pl.run_scoped(
        temporal_block, pltpu.VMEM((tokens, width), HALF), pltpu.VMEM((tokens, width), HALF)
    )
    line.tick()

    def last(t, carry):
        at = pl.ds(pl.multiple_of(t * block, block), block)
        back = norm_back(x[at, :].astype(SINGLE), summed[at, :], i.gain[0:1, :], 0)
        d_res[at, :] = d_res[at, :] + back
        return carry

    lax.fori_loop(0, rows // block, last, 0)
    outward[1].start()

    for j in range(tiles.shape[0]):
        tiles[j] = gain_sum[:, j * 128 : (j + 1) * 128]
    inner, outer = ring_peers("mp"), ring_peers("dp")
    level, me = lax.axis_index("dp"), lax.axis_index("mp")
    held = tiles.shape[0] // parts
    copies = exchange(
        outer,
        lambda k: tiles.at[pl.ds((level + k) % parts * held, held)],
        lambda k: tiles_dp.at[k],
        *total_sems[:2],
    )
    line.tick()
    for j in range(3):
        line.collect(j)
    for copy in copies:
        copy.wait_recv()
    first = level * held
    for k, _ in outer:
        tiles_dp[0] = (tiles[pl.ds(first, held)] if k == 1 else tiles_dp[0]) + tiles_dp[k]
    pair = count // held
    late = exchange(
        inner,
        lambda k: tiles_dp.at[0, (me + k) % count // pair],
        lambda k: tiles_mp.at[k],
        *total_sems[2:],
    )
    line.tick(len(line.of[3]) + len(line.of[4]) - 1 - (line.done - line.of[3][0]))
    line.collect(3)
    for copy in late:
        copy.wait_recv()
    value = tiles_dp[0, me // pair]
    for k, _ in inner:
        value = value + tiles_mp[k]
    o.gain_grads[...] = value
    line.tick(len(line.chunks) - line.done)
    line.collect(4)
    line.collect(5)
    line.settle()
    for copy in copies + late:
        copy.wait_send()
    for copy in outward:
        copy.wait()


def backward_pass(values, small_rows, heads, bite, collective_id):
    parts, count = LineSum.COUNT, PlaneGather.COUNT
    rows, model = values.x.shape
    tokens = rows * count
    width = values.bx.shape[1]
    units = values.hidden.shape[1]
    depth = values.pack4.shape[2]
    sizes = (
        (depth, units), (depth, units), (depth, units),
        (width, depth), (2 * width, depth), (small_rows, depth),
    )
    shape = jax.ShapeDtypeStruct
    outs = BackwardOut(
        shape((rows, model), HALF),
        shape((rows, model), SINGLE),
        shape((8, 128), SINGLE),
        shape((tokens, model), HALF),
        shape((model, units), HALF),
        shape((model, units), HALF),
        shape((parts * width, depth), HALF),
        shape((parts * 2 * width, depth), HALF),
        *[shape((parts,) + size, HALF) for size in sizes],
        *[shape(size, SINGLE) for size in sizes],
    )
    in_vmem, in_hbm = pl.BlockSpec(memory_space=pltpu.VMEM), pl.BlockSpec(memory_space=pl.ANY)
    in_specs = BackwardIn(*[in_hbm] * len(values))._replace(
        lens=pl.BlockSpec(memory_space=pltpu.SMEM),
        gain=in_vmem,
        bin=in_vmem,
        ba=in_vmem,
        chan=in_vmem,
    )
    out_specs = BackwardOut(*[in_hbm] * len(outs))._replace(gain_grads=in_vmem)
    inner, outer = lax.axis_size("mp"), lax.axis_size("dp")
    pieces = [
        (count, (size[0] // count, size[1])) for size, count in zip(sizes, SUM_PIECES)
    ]
    tile = (8, 128)
    results = pl.pallas_call(
        functools.partial(backward_pass_kernel, heads, bite),
        out_shape=list(outs),
        in_specs=list(in_specs),
        out_specs=list(out_specs),
        scratch_shapes=[
            pltpu.VMEM((rows, model), HALF),
            pltpu.VMEM((rows, model), HALF),
            pltpu.VMEM((rows, model), SINGLE),
            pltpu.VMEM((rows, model), SINGLE),
            pltpu.VMEM((rows, model), SINGLE),
            pltpu.VMEM((rows, model), HALF),
            pltpu.VMEM((8, model), SINGLE),
        ]
        + forward_scratch(rows, width)
        + [
            pltpu.VMEM((width, width), SINGLE),
            pltpu.VMEM((width, width), SINGLE),
            pltpu.VMEM((8, width), SINGLE),
            pltpu.VMEM((parts * small_rows, depth), SINGLE),
            pltpu.VMEM((parts * small_rows, depth), HALF),
            pltpu.VMEM((model // 128,) + tile, SINGLE),
            pltpu.VMEM((outer, model // 128 // parts) + tile, SINGLE),
            pltpu.VMEM((inner,) + tile, SINGLE),
        ]
        + [pltpu.VMEM((count,) + size, HALF) for count, size in pieces]
        + [pltpu.VMEM(size, HALF) for _, size in pieces]
        + [pltpu.SemaphoreType.DMA((7,)), pltpu.SemaphoreType.DMA((2,))]
        + [pltpu.SemaphoreType.DMA((c,)) for c in (outer, outer, inner, inner)]
        + PlaneGather.scratch()
        + PlaneSum.scratch(rows, model)
        + [pltpu.SemaphoreType.REGULAR]
        + LineSum.scratch(sum(SUM_PIECES)),
        compiler_params=kernel_params(collective_id),
        cost_estimate=pl.CostEstimate(
            flops=14 * tokens * model * units,
            bytes_accessed=40 * tokens * model,
            transcendentals=tokens * units,
        ),
        name="backward_pass",
    )(*values)
    return BackwardOut(*results)


def diagonal(blocks):
    count, size, _ = blocks.shape
    spread = blocks[:, :, None, :] * jnp.eye(count, dtype=blocks.dtype)[:, None, :, None]
    return spread.reshape(count * size, count * size)


def on_device(
    layer_input,
    cotangent,
    norm_in,
    norm_mid,
    w_rnn_in,
    w_rnn_gate,
    w_rnn_out,
    gate_in_blocks,
    gate_a_blocks,
    channel_params,
    w_mlp_gate,
    w_mlp_up,
    w_mlp_down,
    lengths,
):
    parts = lax.axis_size("dp")
    rows, model = layer_input.shape
    depth, width = w_rnn_in.shape
    heads, bite, block = gate_in_blocks.shape
    tokens = rows * lax.axis_size("mp")

    fused = lax.axis_size("mp") == PlaneGather.COUNT and parts == LineGather.COUNT
    small_rows = -(-(heads * bite + 2 * CONV // parts) // 16) * 16
    lane_a = 256 if fused else block

    def small_pack(blocks_in, blocks_a, channels):
        wide = lambda v, lanes: jnp.pad(v, ((0, 0), (0, lanes - v.shape[1])))
        v = jnp.concatenate(
            [
                wide(blocks_in.reshape(-1, block), lane_a),
                wide(blocks_a.reshape(-1, block), small_lanes - lane_a),
            ],
            axis=1,
        )
        v = jnp.concatenate([v, wide(channels, small_lanes)], axis=0)
        return jnp.pad(v, ((0, small_rows - v.shape[0]), (0, 0)))

    small_lanes = 512
    small_mine = small_pack(
        gate_in_blocks.astype(HALF), gate_a_blocks.astype(HALF), channel_params.astype(HALF)
    )
    mine = jnp.concatenate([w_rnn_in.astype(HALF).T, w_rnn_gate.astype(HALF).T], axis=0)
    out_mine, down_mine = w_rnn_out.astype(HALF), w_mlp_down.astype(HALF)
    gate_mine, up_mine = w_mlp_gate.astype(HALF), w_mlp_up.astype(HALF)
    bite_gain = norm_in.shape[0]
    gains = jnp.stack([norm_in, norm_mid]).astype(HALF).astype(SINGLE)
    if fused:
        group = 128 // bite_gain
        spot = (lax.axis_index("mp") % group) * bite_gain
        gains = lax.dynamic_update_slice(jnp.zeros((8, 128), SINGLE), gains, (0, spot))
        o = forward_pass(
            lengths, gains, layer_input, cotangent, small_mine, mine, out_mine,
            down_mine, gate_mine, up_mine, heads, bite, 0,
        )
        known = BackwardIn(
            lengths, o.gain, o.bin, o.ba, o.chan, layer_input, cotangent, o.residual, o.n2_all,
            o.n1, o.bx, o.by, o.conv, o.gi, o.ra, o.h, o.ob, o.hidden, o.d_up, o.d_gate,
            o.grad_down, o.out4, o.pack4, o.gate4, o.up4, o.down4,
        )
        o = backward_pass(known, small_rows, heads, bite, 1)
        gain_grads = lax.dynamic_slice(o.gain_grads, (0, spot), (2, bite_gain))
        layer_output, grad_input = o.layer_output, o.grad_input
        grad_in, grad_side = o.sum_pack[:width], o.sum_pack[width:]
        grad_out, small_grads = o.sum_out, o.sum_small
        grad_gate, grad_up, grad_down = o.sum_gate, o.sum_up, o.sum_down
    else:
        inputs = layer_input.astype(SINGLE)
        over = lambda v: lax.all_gather(v, "dp", axis=0, tiled=False)
        gains = lax.all_gather(gains, ("dp", "mp"), axis=0, tiled=False)
        gain_first = gains[:, 0].reshape(1, model)
        gain_second = gains[:, 1].reshape(1, model)
        small, pack, out_w = over(small_mine), over(mine), over(out_mine)
        down, gate_w, up_w = over(down_mine), over(gate_mine), over(up_mine)
        whole_block = lambda v: diagonal(
            v.reshape(parts, heads, bite, block)
            .transpose(1, 0, 2, 3)
            .reshape(heads, block, block)
        )
        blocks_in = whole_block(small[:, : heads * bite, :block])
        blocks_a = whole_block(small[:, : heads * bite, lane_a : lane_a + block])
        channel = small[:, heads * bite : heads * bite + 2 * CONV // parts, :width]
        channel = channel.reshape(2 * CONV, width).astype(SINGLE)
        soft = jax.nn.softplus(-channel[2 * CONV - 1 :])
        chan = jnp.concatenate([channel, soft, jnp.zeros((7, width), SINGLE)], axis=0)
        x_all = lax.all_gather(layer_input, "mp", axis=0, tiled=True)
        c_all = lax.all_gather(cotangent, "mp", axis=0, tiled=True)
        n1, bx, by, conv, gate_in, gate_a, h, ob = forward_channels(
            lengths, x_all, gain_first, pack, blocks_in, blocks_a, chan
        )
        saved = (bx, by, conv, gate_in, gate_a, h, ob, n1)
        out = jnp.einsum("tc,dcm->tdm", ob, out_w, preferred_element_type=SINGLE)
        residual = inputs + lax.psum_scatter(
            out.reshape(tokens, model).astype(HALF), "mp", scatter_dimension=0, tiled=True
        ).astype(SINGLE)
        scale = lax.rsqrt(jnp.mean(residual * residual, axis=-1, keepdims=True) + EPS)
        normed_mid = (residual * scale * gain_second).astype(HALF)
        n2 = lax.all_gather(normed_mid, "mp", axis=0, tiled=True)
        d_hidden = dot_nt(c_all, down.transpose(1, 0, 2).reshape(-1, model))
        act, slope = gelu_both(dot_nn(n2, gate_w.reshape(model, -1)))
        d_up = (d_hidden * act).astype(HALF)
        up_pre = dot_nn(n2, up_w.reshape(model, -1))
        hidden = (act * up_pre).astype(HALF)
        d_gate = (d_hidden * up_pre * slope).astype(HALF)
        gate_w, up_w = gate_w.reshape(model, -1), up_w.reshape(model, -1)
        over_dp = lambda value: lax.psum_scatter(
            value.astype(HALF), "dp", scatter_dimension=0, tiled=True
        ).astype(SINGLE)
        over_mp = lambda value: lax.psum_scatter(
            value.astype(HALF), "mp", scatter_dimension=0, tiled=True
        ).astype(SINGLE)
        grad_down = over_dp(dot_tn(c_all, hidden))
        grad_gate, grad_up = over_dp(dot_tn(n2, d_gate)), over_dp(dot_tn(n2, d_up))
        layer_output = residual + over_mp(
            dot_nn(hidden, down.transpose(1, 0, 2).reshape(-1, model))
        )
        layer_output = layer_output.astype(HALF)
        back = over_mp(dot_nt(d_gate, gate_w) + dot_nt(d_up, up_w))
        weighted = gain_second * back
        gain_mid = jnp.sum(back * residual * scale, axis=0)
        d_residual = (
            cotangent.astype(SINGLE)
            + scale * weighted
            - residual * scale**3 * jnp.mean(weighted * residual, axis=-1, keepdims=True)
        )
        dt_all = lax.all_gather(d_residual.astype(HALF), "mp", axis=0, tiled=True)
        d_bx, d_by, gin, ga, gchan, rnn_grads = backward_channels(
            lengths, dt_all, out_w, blocks_in, blocks_a, chan, saved
        )
        back = over_mp(
            jnp.einsum(
                "tc,dcm->tdm",
                jnp.concatenate([d_bx, d_by], axis=1),
                pack,
                preferred_element_type=SINGLE,
            ).reshape(tokens, model)
        )
        own = lambda full: jnp.stack(
            [full[j * block : (j + 1) * block, j * block : (j + 1) * block] for j in range(heads)]
        )
        decay_row = DECAY * jax.nn.sigmoid(-channel[2 * CONV - 1 :]) * gchan[2 * CONV - 1 :]
        grad_channel = jnp.concatenate([gchan[: 2 * CONV - 1], decay_row], axis=0)
        split = lambda v: v.reshape(heads, parts, bite, block).transpose(1, 0, 2, 3)
        small_grads = jax.vmap(small_pack)(
            split(own(gin)), split(own(ga)), grad_channel.reshape(parts, -1, width)
        )
        small_grads = over_dp(small_grads)[0]
        rnn_grads = over_dp(rnn_grads)[0]
        grad_in, grad_side, grad_out = jnp.split(rnn_grads, 3, axis=0)
        scale = lax.rsqrt(jnp.mean(inputs * inputs, axis=-1, keepdims=True) + EPS)
        weighted = gain_first * back
        gain_in = jnp.sum(back * inputs * scale, axis=0)
        grad_input = (
            d_residual
            + scale * weighted
            - inputs * scale**3 * jnp.mean(weighted * inputs, axis=-1, keepdims=True)
        )
        gain_grads = lax.psum_scatter(
            jnp.stack([gain_in, gain_mid]), ("dp", "mp"), scatter_dimension=1, tiled=True
        )
    gate_rows = small_grads[: heads * bite]
    return (
        layer_output,
        grad_input,
        gain_grads[0],
        gain_grads[1],
        grad_in.T,
        grad_side.T,
        grad_out,
        gate_rows[:, :block].reshape(heads, bite, block),
        gate_rows[:, lane_a : lane_a + block].reshape(heads, bite, block),
        small_grads[heads * bite : heads * bite + 2 * CONV // parts, :width],
        grad_gate,
        grad_up,
        grad_down.T,
    )


def solution(mesh):
    rows = P(("dp", "mp"), None)
    return jax.shard_map(
        on_device,
        mesh=mesh,
        in_specs=(
            rows,
            rows,
            P(("dp", "mp")),
            P(("dp", "mp")),
            P("dp", "mp"),
            P("dp", "mp"),
            P("mp", "dp"),
            P("mp", "dp", None),
            P("mp", "dp", None),
            P("dp", "mp"),
            P("dp", "mp"),
            P("dp", "mp"),
            P("mp", "dp"),
            P("dp", None),
        ),
        out_specs=(
            rows,
            rows,
            P(("dp", "mp")),
            P(("dp", "mp")),
            P("dp", "mp"),
            P("dp", "mp"),
            P("mp", "dp"),
            P("mp", "dp", None),
            P("mp", "dp", None),
            P("dp", "mp"),
            P("dp", "mp"),
            P("dp", "mp"),
            P("mp", "dp"),
        ),
        check_vma=False,
    )
```

time: 599 us -> 547 us (0.913)
  Pallas kernels: 447 us -> 517 us
  matrix products: 51.5 us -> 0 us
  other arithmetic: 42.6 us -> 10.4 us
  waiting for transfers between devices: 18.8 us -> 0 us
  between operations: 14.8 us -> 0.73 us
    pallas_call x11 -> x2, Pallas kernels: 447 us -> 517 us  [the longest x1 264 us: forward_pass(): pl.pallas_call(functools.partial(forward_pass_kernel, heads, bite), out_s...]
    dot_general x4 -> x0, matrix products: 51.5 us -> none  [the longest x2 29.1 us: dot_nn(): lax.dot_general(left, right, (((1,), (0,)), ((), ())), preferred_element_...]
    convert_element_type x16 -> x8, other arithmetic: 22.4 us -> 7.23 us  [the longest x2 2.83 us: on_device(): out_mine, down_mine = (w_rnn_out.astype(HALF), w_mlp_down.astype(HALF))]
    reduce_scatter x4 -> x0, waiting for transfers between devices: 11.5 us -> none  [over_dp(): lax.psum_scatter(value.astype(HALF), 'dp', scatter_dimension=dimension, t...]
    all_gather x4 -> x0, waiting for transfers between devices: 7.17 us -> none  [the longest x1 7.15 us: on_device(): up_w = lax.all_gather(w_mlp_up.astype(HALF), 'dp', axis=0, tiled=True)]
    reduce_sum x3 -> x0, other arithmetic: 6.37 us -> none  [the longest x1 2.15 us: on_device(): grad_gain_second = jnp.sum(d_normed_mid * residual * scale_second, axis=0)]
  transfers between devices with their start and end apart: 8 -> 0, of which waited for: 2 -> 0; matrix products, arithmetic and copies ran while one was open for 17% -> 0% of each run, Pallas kernels for 75% -> 0%
where the time goes in v5:
time: 547 us; the launch traced here: 545 us
  Pallas kernels  517 us (95%)
  local copies, waits for them, and re-layouts  16.3 us (3%)
  other arithmetic  10.4 us (2%)
    pallas_call x1, Pallas kernels, forward_pass(): pl.pallas_call(functools.partial(forward_pass_kernel, heads, bite), out_s...  264 us
    pallas_call x1, Pallas kernels, backward_pass(): pl.pallas_call(functools.partial(backward_pass_kernel, heads, bite), out_...  253 us

profile of v5, /device:TPU:0, one launch (start us, length us, event | category | flops | bytes accessed | tf_op | source)
XLA Modules:
  0.0 545.0 jit_solution(10035473210297641682)
XLA Ops:
  0.6 0.0 copy-start.1
  0.7 0.8 convert_bitcast_fusion.2
  1.5 0.7 convert_element_type.41
  2.2 0.2 dynamic_update_slice.3.refs_1_
  2.4 0.0 copy-start.8
  2.4 0.9 convert_element_type.39
  3.3 0.9 convert_element_type.40
  4.2 0.7 pad.18.refs_4_
  4.9 1.9 convert_element_type.44.refs_6_
  6.7 0.0 copy-start.2
  6.7 1.5 convert_bitcast_fusion
  8.2 0.9 pad_maximum_fusion.refs_5_
  9.1 0.0 copy-done.1
  9.1 0.0 copy-start.3
  9.1 1.0 convert_element_type.46.refs_8_
  10.0 0.0 copy-done.8
  10.0 0.0 copy-done.2
  10.0 1.0 convert_element_type.47.refs_9_
  11.0 0.0 copy-done.3
  11.0 1.0 convert_element_type.45.refs_7_
  12.0 264.3 %forward_pass.1 = (f32[8,2048]{1,0:T(8,128)}, bf16[320,320]{1,0:T(8,128)(2,1)}, bf16[320,320]{1,0:T(8,128)(2,1)}, f32[16,320]{1,0:T(8,128)}, bf16[2048,2048]{1,0...) custom-call(s32[1,3]{1,0:T(1,128)} %refs_0_.3, ...), custom_call_target="tpu_custom_call" | custom-call | flops 32212254720 | bytes 167772160 | tf_op jit(solution)/shard_map/forward_pass/pallas_call | solution.py:1336
  276.3 253.2 %backward_pass.1 = (bf16[256,2048]{1,0:T(8,128)(2,1)}, f32[256,2048]{1,0:T(8,128)}, f32[8,128]{1,0:T(8,128)}, bf16[2048,2048]{1,0:T(8,128)(2,1)}, bf16[2048,768]...) custom-call(s32[1,3]{1,0:T(1,128)} %refs_0_.3, ...), custom_call_target="tpu_custom_call" | custom-call | flops 45097156608 | bytes 167772160 | tf_op jit(solution)/shard_map/backward_pass/pallas_call | solution.py:1758
  529.5 0.7 constant_dynamic-slice_fusion
  530.2 0.5 slice_bitcast_fusion.2
  530.7 1.3 slice.30
  532.0 1.6 fusion.9
  533.6 0.0 copy-start.6
  533.6 2.5 slice_bitcast_fusion
  536.1 0.0 copy-start
  536.1 3.2 copy.27
  539.3 0.0 copy-done.6
  539.3 1.0 copy.34
  540.3 0.0 copy-done
  540.3 0.0 copy-start.7
  540.3 0.0 copy-start.5
  540.3 1.3 copy.35
  541.6 0.2 copy-done.7
  541.8 0.0 copy-start.4
  541.8 0.8 copy.36
  542.7 0.0 copy-done.5
  542.7 1.1 copy.37
  543.8 0.0 copy-done.4
  543.8 1.1 copy.38
  (3 shorter events, 0.0 us)
Async XLA Ops:
  0.6 8.4 %copy-start.1 = (f32[512,768]{1,0:T(8,128)S(1)}, f32[512,768]{1,0:T(8,128)}, u32[]{:S(2)}) copy-start(f32[512,768]{1,0:T(8,128)} %param.24) | copy-start | bytes 4718596
  2.4 7.7 %copy-start.8 = (f32[8,128]{1,0:T(8,128)}, f32[8,128]{1,0:T(8,128)S(1)}, u32[]{:S(2)}) copy-start(f32[8,128]{1,0:T(8,128)S(1)} %dynamic_update_slice.3.refs_1_) | copy-start | bytes 12292
  6.7 3.3 copy-start.2
  9.1 1.9 copy-start.3
  533.6 5.7 %copy-start.6 = (bf16[256,2048]{1,0:T(8,128)(2,1)S(1)}, bf16[256,2048]{1,0:T(8,128)(2,1)}, u32[]{:S(2)}) copy-start(bf16[256,2048]{1,0:T(8,128)(2,1)} %get-tuple-element.113) | copy-start | bytes 3145732
  536.1 4.1 copy-start
  540.3 1.5 copy-start.7
  540.3 2.4 copy-start.5
  541.8 2.0 copy-start.4

commit v6 on v5

--- a/solution.py
+++ b/solution.py
@@ -9,7 +9,8 @@
 from jax.sharding import PartitionSpec as P
 
 CONV = 4
-AHEAD = 2
+AHEAD = 3
+SUM_AHEAD = 3
 EPS = 1e-06
 DECAY = 8.0
 HALF = jnp.bfloat16
@@ -73,9 +74,8 @@
 
 
 def exchange(peers, source, target, send, recv):
-    copies = []
-    for k, peer in peers:
-        copy = pltpu.make_async_remote_copy(
+    return [
+        pltpu.make_async_remote_copy(
             src_ref=source(k),
             dst_ref=target(k),
             send_sem=send.at[k],
@@ -83,9 +83,16 @@
             device_id=peer,
             device_id_type=MESH,
         )
-        copy.start()
-        copies.append(copy)
-    return copies
+        for k, peer in peers
+    ]
+
+
+def each(copies, act):
+    for copy in copies:
+        act(copy)
+
+
+START, LAND, SENT = (lambda c: c.start(), lambda c: c.wait_recv(), lambda c: c.wait_send())
 
 
 def gather_plan(count):
@@ -173,29 +180,23 @@
 
     @staticmethod
     def scratch(pieces):
-        shapes = ((pieces, 4), (pieces, 4), (pieces,), (pieces,))
+        shapes = ((pieces, 4), (pieces, 4), (pieces,))
         return [pltpu.SemaphoreType.DMA(shape) for shape in shapes]
 
-    def __init__(self, jobs, scratch):
+    def __init__(self, targets, pieces, scratch):
         self.chunks, self.of = [], []
-        for source, target, pieces in jobs:
-            rows = source.shape[0] // pieces
+        for target, count in zip(targets, pieces):
+            rows = target.shape[1] // count
             first = len(self.chunks)
-            self.chunks += [(source, target, pl.ds(p * rows, rows)) for p in range(pieces)]
+            self.chunks += [(target, pl.ds(p * rows, rows)) for p in range(count)]
             self.of.append(range(first, len(self.chunks)))
-        self.send, self.recv, self.onward, self.own_sem = scratch
+        self.send, self.recv, self.onward = scratch
         self.me = lax.axis_index("dp")
 
-    def own(self, c):
-        source, target, span = self.chunks[c]
-        return pltpu.make_async_copy(
-            source.at[span], target.at[self.me, span], self.own_sem.at[c]
-        )
-
     def direct(self, c, to):
-        source, target, span = self.chunks[c]
+        target, span = self.chunks[c]
         return pltpu.make_async_remote_copy(
-            src_ref=source.at[span],
+            src_ref=target.at[self.me, span],
             dst_ref=target.at[self.me, span],
             send_sem=self.send.at[c, to],
             recv_sem=self.recv.at[c, self.me],
@@ -204,7 +205,7 @@
         )
 
     def handed(self, c, block, to):
-        _, target, span = self.chunks[c]
+        target, span = self.chunks[c]
         return pltpu.make_async_remote_copy(
             src_ref=target.at[block, span],
             dst_ref=target.at[block, span],
@@ -220,7 +221,6 @@
 
     def start(self, chunks):
         for c in chunks:
-            self.own(c).start()
             for to in range(self.COUNT):
                 pl.when(self.sends_to(to))(lambda c=c, to=to: self.direct(c, to).start())
 
@@ -254,7 +254,6 @@
                 if early is not None:
                     waits = jnp.logical_and(waits, self.me != early)
                 pl.when(waits)(lambda c=c, block=block: self.handed(c, block, 0).wait_recv())
-            self.own(c).wait()
 
     def settle(self):
         for c in range(len(self.chunks)):
@@ -271,20 +270,17 @@
     )
 
 
-def share(x_ref, o_ref, sems):
+def sharing(o_ref, sems):
     send_mp, recv_mp, send_dp, recv_dp = sems
-    inner, outer = ring_peers("mp"), ring_peers("dp")
-    count = len(inner) + 1
+    count = lax.axis_size("mp")
     first = lax.axis_index("dp") * count
     place = first + lax.axis_index("mp")
-    o_ref[place] = x_ref[...]
     mine = lambda k: o_ref.at[place]
     plane = lambda k: o_ref.at[pl.ds(first, count)]
-    copies = exchange(inner, mine, mine, send_mp, recv_mp)
-    for copy in copies:
-        copy.wait_recv()
-    later = exchange(outer, plane, plane, send_dp, recv_dp)
-    return later, copies + later
+    return (
+        exchange(ring_peers("mp"), mine, mine, send_mp, recv_mp),
+        exchange(ring_peers("dp"), plane, plane, send_dp, recv_dp),
+    )
 
 
 def beside_products(pairs):
@@ -539,20 +535,29 @@
 
     def collect(self, j):
         source, landed, target, _, _, _ = self.jobs[j]
+        turned = target.shape[-1] != landed.shape[-1]
+        split = len(target.shape) == 3
         for c in self.of[j]:
             for sender in range(self.COUNT):
                 takers = [z for z in range(self.COUNT) if sender in self.SENDERS[z]]
                 pl.when(self.among(takers))(
                     lambda c=c, sender=sender: self.wait_from(c, sender)
                 )
-        rows, columns = target.shape
+        _, rows, columns = landed.shape
         tile = rows // 2 if rows >= 256 else rows
+        out_spec = pl.BlockSpec((tile, columns), lambda t: (t, 0))
+        if split:
+            shape = (1, columns, tile) if turned else (1, tile, columns)
+            out_spec = pl.BlockSpec(shape, lambda t: (t, 0, 0))
 
         def add(*refs):
             value = refs[0][...].astype(SINGLE)
             for ref in refs[1:-1]:
                 value = value + ref[0].astype(SINGLE)
-            refs[-1][...] = value
+            if split:
+                refs[-1][0] = value.T if turned else value
+            else:
+                refs[-1][...] = value
 
         def run(senders):
             pltpu.emit_pipeline(
@@ -565,7 +570,7 @@
                     pl.BlockSpec((1, tile, columns), lambda t, sender=sender: (sender, t, 0))
                     for sender in senders
                 ],
-                out_specs=[pl.BlockSpec((tile, columns), lambda t: (t, 0))],
+                out_specs=[out_spec],
             )(source, *[landed] * len(senders), target)
 
         pl.when(self.among((0, 3)))(lambda: run((1, 2)))
@@ -1023,365 +1028,31 @@
     )
 
 
-class ForwardIn(typing.NamedTuple):
+class LayerIn(typing.NamedTuple):
     lens: typing.Any
-    gains: typing.Any
+    norm_in: typing.Any
+    norm_mid: typing.Any
     x: typing.Any
     cot: typing.Any
-    small: typing.Any
-    pack: typing.Any
-    out: typing.Any
-    down: typing.Any
+    blocks_in: typing.Any
+    blocks_a: typing.Any
+    channels: typing.Any
+    w_in: typing.Any
+    w_gate: typing.Any
+    w_out: typing.Any
     gate: typing.Any
     up: typing.Any
-
-
-class ForwardOut(typing.NamedTuple):
-    gain: typing.Any
-    bin: typing.Any
-    ba: typing.Any
-    chan: typing.Any
+    down: typing.Any
+
+
+class LayerOut(typing.NamedTuple):
+    layer_output: typing.Any
+    grad_input: typing.Any
+    gain_grads: typing.Any
     x_all: typing.Any
     c_all: typing.Any
     n2_all: typing.Any
-    n1: typing.Any
-    residual: typing.Any
-    bx: typing.Any
-    by: typing.Any
-    conv: typing.Any
-    gi: typing.Any
-    ra: typing.Any
-    h: typing.Any
-    ob: typing.Any
-    small4: typing.Any
-    pack4: typing.Any
-    out4: typing.Any
-    gate4: typing.Any
-    up4: typing.Any
-    down4: typing.Any
-    act: typing.Any
-    hidden: typing.Any
-    d_up: typing.Any
-    d_gate: typing.Any
-    grad_down: typing.Any
-
-
-WEIGHT_PIECES = (1, 4, 2, 4, 4, 6)
-
-
-def forward_pass_kernel(heads, bite, *refs):
-    refs = list(refs)
-    take = lambda n: [refs.pop(0) for _ in range(n)]
-    i = ForwardIn(*take(len(ForwardIn._fields)))
-    o = ForwardOut(*take(len(ForwardOut._fields)))
-    tiles, bin32, ba32 = take(3)
-    pack, out_w, down, gate, up = take(5)
-    steps_scratch = take(4)
-    ob, inputs, summed, n2_own, slope, hidden = take(6)
-    load_sem, store_sem = take(2)
-    share_sems = take(4)
-    plane_x = PlaneGather(i.x, o.x_all, take(3))
-    plane_c = PlaneGather(i.cot, o.c_all, take(3))
-    plane_n = PlaneGather(n2_own, o.n2_all, take(3))
-    plane = PlaneSum([by_parts], out_w.shape[2], [ob], [out_w], take(10))
-    line = LineGather(
-        list(
-            zip(
-                (i.small, i.pack, i.out, i.gate, i.up, i.down),
-                (o.small4, o.pack4, o.out4, o.gate4, o.up4, o.down4),
-                WEIGHT_PIECES,
-            )
-        ),
-        refs,
-    )
-    small_at, pack_at, out_at, gate_at, up_at, down_at = line.of
-    tokens, model = o.x_all.shape
-    rows, count, width = i.x.shape[0], PlaneGather.COUNT, ob.shape[1]
-    parts, _, depth = pack.shape
-
-    greet(ring_peers("mp") + ring_peers("dp"))
-    line.begin(AHEAD)
-    gains_way, copies = share(i.gains, tiles, share_sems)
-    plane_x.start()
-    own_rows = pltpu.make_async_copy(i.x, inputs, load_sem.at[0])
-    own_rows.start()
-    bin32[...] = jnp.zeros_like(bin32)
-    ba32[...] = jnp.zeros_like(ba32)
-    o.chan[...] = jnp.zeros_like(o.chan)
-    line.tick(2)
-    plane_x.level(1)
-    line.tick()
-    plane_x.level(2)
-    line.tick()
-    plane_x.finish()
-    plane_c.start()
-    line.tick()
-    for copy in gains_way:
-        copy.wait_recv()
-    group = 128 // (model // tiles.shape[0])
-    for j in range(model // 128):
-        value = tiles[group * j]
-        for k in range(1, group):
-            value = value + tiles[group * j + k]
-        o.gain[:, j * 128 : (j + 1) * 128] = value
-    line.landed(small_at)
-    line.landed(pack_at)
-    own_rows.wait()
-
-    def load(source, target, j):
-        copy = pltpu.make_async_copy(source, target, load_sem.at[j])
-        copy.start()
-        return copy
-
-    loads = [load(o.pack4, pack, 1)]
-
-    def with_small(small):
-        copy = load(o.small4, small, 2)
-        copy.wait()
-        small_weights(small, bin32, ba32, o.chan, heads, bite)
-
-    pl.run_scoped(with_small, pltpu.VMEM(o.small4.shape, HALF))
-    o.bin[...] = bin32[...].astype(HALF)
-    o.ba[...] = ba32[...].astype(HALF)
-    loads[0].wait()
-
-    def channels(x_tile, n1, bx, by, conv, gi, ra, h, ob_tile):
-        step = pl.program_id(0)
-        schedule = {
-            2: line.tick,
-            3: lambda: plane_c.level(1),
-            4: line.tick,
-            6: lambda: plane_c.level(2),
-            7: line.tick,
-        }
-        for when, act in schedule.items():
-            pl.when(step == when)(lambda act=act: (act(), None)[1])
-        forward_step(
-            step, i.lens, x_tile, o.gain.at[0:1], pack, o.bin, o.ba, o.chan,
-            n1, bx, by, conv, gi, ra, h, ob_tile, *steps_scratch,
-        )
-        ob[pl.ds(pl.multiple_of(step * rows, rows), rows), :] = ob_tile[...]
-
-    part = pl.BlockSpec((rows, width), lambda t: (t, 0))
-    across = pl.BlockSpec((rows, model), lambda t: (t, 0))
-    pltpu.emit_pipeline(
-        channels,
-        grid=(count,),
-        in_specs=[across],
-        out_specs=[across] + [part] * 7,
-    )(o.x_all, o.n1, o.bx, o.by, o.conv, o.gi, o.ra, o.h, o.ob)
-    line.landed(out_at)
-    load(o.out4, out_w, 1).wait()
-    plane.spread(line.tick)
-    line.tick()
-    plane_c.finish()
-    line.tick()
-    plane.finish(summed)
-
-    def norm(t, carry):
-        at = pl.ds(pl.multiple_of(t * 32, 32), 32)
-        value = inputs[at, :].astype(SINGLE) + summed[at, :]
-        scale = lax.rsqrt(jnp.mean(value * value, axis=-1, keepdims=True) + EPS)
-        summed[at, :] = value
-        n2_own[at, :] = (value * scale * o.gain[1:2, :]).astype(HALF)
-        return carry
-
-    lax.fori_loop(0, rows // 32, norm, 0)
-    plane_n.start()
-    stores = [pltpu.make_async_copy(summed, o.residual, store_sem)]
-    stores[0].start()
-    line.tick(2)
-    plane_n.level(1)
-    line.tick()
-    plane_n.level(2)
-    line.tick()
-    plane_n.finish()
-    line.landed(gate_at)
-    line.landed(up_at)
-    loads = [load(o.gate4, gate, 0), load(o.up4, up, 1)]
-    for copy in loads:
-        copy.wait()
-
-    units = hidden.shape[1]
-    thirds = [down_at[j : j + 2] for j in range(0, len(down_at), 2)]
-    third = units // len(thirds)
-    along = pl.BlockSpec((rows, units), lambda t: (t, 0))
-    here = lambda: pl.ds(pl.multiple_of(pl.program_id(0) * rows, rows), rows)
-
-    def blocks(left, right):
-        value = None
-        for d in range(parts):
-            term = right(left[:, d * depth : (d + 1) * depth], d)
-            value = term if value is None else value + term
-        return value
-
-    def activations(n2, act_tile, hidden_tile):
-        for when in (3, 6):
-            pl.when(pl.program_id(0) == when)(line.tick)
-        value, rise = gelu_both(blocks(n2, lambda v, d: dot_nn(v, gate[d])))
-        act_tile[...] = value
-        above = blocks(n2, lambda v, d: dot_nn(v, up[d]))
-        low = (value * above).astype(HALF)
-        hidden_tile[...] = low
-        hidden[here(), :] = low
-        slope[here(), :] = rise * above
-
-    pltpu.emit_pipeline(
-        activations, grid=(count,), in_specs=[across], out_specs=[along, along]
-    )(o.n2_all, o.act, o.hidden)
-    beside_products([(o.c_all, hidden, o.grad_down)])
-    line.tick()
-
-    def gradients(act, total):
-        for p, pieces in enumerate(thirds):
-            if p:
-                line.tick(pieces[-1] + 1 - line.done)
-            span = pl.ds(p * third, third)
-            act_load = load(o.act.at[:, span], act, 1)
-            line.landed(pieces)
-            load(o.down4.at[:, span], down.at[:, span], 0).wait()
-            act_load.wait()
-
-            def backs(c_tile, d_up_tile, d_gate_tile):
-                d = pl.program_id(0)
-                term = dot_nt(c_tile[...], down[d, span])
-
-                @pl.when(d == 0)
-                def _():
-                    total[...] = term
-
-                @pl.when(d > 0)
-                def _():
-                    total[...] += term
-
-                @pl.when(d == parts - 1)
-                def _():
-                    def step(t, carry):
-                        at = pl.ds(pl.multiple_of(t * 128, 128), 128)
-                        back = total[at, :]
-                        d_up_tile[at, :] = (back * act[at, :]).astype(HALF)
-                        d_gate_tile[at, :] = (back * slope[at, span]).astype(HALF)
-                        return carry
-
-                    lax.fori_loop(0, tokens // 128, step, 0)
-
-            piece = pl.BlockSpec((tokens, third), lambda d: (0, p))
-            pltpu.emit_pipeline(
-                backs,
-                grid=(parts,),
-                in_specs=[pl.BlockSpec((tokens, depth), lambda d: (0, d))],
-                out_specs=[piece, piece],
-            )(o.c_all, o.d_up, o.d_gate)
-
-    pl.run_scoped(
-        gradients, pltpu.VMEM((tokens, third), SINGLE), pltpu.VMEM((tokens, third), SINGLE)
-    )
-    line.settle()
-    stores[0].wait()
-    for copy in copies:
-        copy.wait_send()
-
-
-def forward_pass(lens, gains, x, cot, small, pack, out, down, gate, up, heads, bite, collective_id):
-    parts, count = LineGather.COUNT, PlaneGather.COUNT
-    rows, model = x.shape
-    tokens = rows * count
-    width, depth = out.shape
-    units = down.shape[0]
-    shape = jax.ShapeDtypeStruct
-    four = lambda v: shape((parts,) + v.shape, HALF)
-    plane_rows = shape((tokens, model), HALF)
-    channel = shape((tokens, width), SINGLE)
-    channel_low = shape((tokens, width), HALF)
-    along = shape((tokens, units), HALF)
-    square = shape((width, width), HALF)
-    shapes = ForwardOut(
-        gain=shape((8, model), SINGLE),
-        bin=square,
-        ba=square,
-        chan=shape((16, width), SINGLE),
-        x_all=plane_rows,
-        c_all=plane_rows,
-        n2_all=plane_rows,
-        n1=plane_rows,
-        residual=shape((rows, model), SINGLE),
-        bx=channel_low,
-        by=channel,
-        conv=channel,
-        gi=channel,
-        ra=channel,
-        h=channel,
-        ob=channel_low,
-        small4=four(small),
-        pack4=four(pack),
-        out4=four(out),
-        gate4=four(gate),
-        up4=four(up),
-        down4=four(down),
-        act=shape((tokens, units), SINGLE),
-        hidden=along,
-        d_up=along,
-        d_gate=along,
-        grad_down=shape((model, units), HALF),
-    )
-    in_vmem, in_hbm = pl.BlockSpec(memory_space=pltpu.VMEM), pl.BlockSpec(memory_space=pl.ANY)
-    in_specs = ForwardIn(*[in_hbm] * len(ForwardIn._fields))._replace(
-        lens=pl.BlockSpec(memory_space=pltpu.SMEM), gains=in_vmem
-    )
-    out_specs = ForwardOut(*[in_hbm] * len(shapes))._replace(
-        gain=in_vmem, bin=in_vmem, ba=in_vmem, chan=in_vmem
-    )
-    inner, outer = lax.axis_size("mp"), lax.axis_size("dp")
-    vmem = lambda v: pltpu.VMEM(v.shape, v.dtype)
-    outs = pl.pallas_call(
-        functools.partial(forward_pass_kernel, heads, bite),
-        out_shape=list(shapes),
-        in_specs=list(in_specs),
-        out_specs=list(out_specs),
-        scratch_shapes=[
-            pltpu.VMEM((inner * outer,) + gains.shape, SINGLE),
-            pltpu.VMEM((width, width), SINGLE),
-            pltpu.VMEM((width, width), SINGLE),
-        ]
-        + [
-            vmem(v) for v in (shapes.pack4, shapes.out4, shapes.down4, shapes.gate4, shapes.up4)
-        ]
-        + forward_scratch(rows, width)
-        + [
-            pltpu.VMEM((tokens, width), HALF),
-            pltpu.VMEM((rows, model), HALF),
-            pltpu.VMEM((rows, model), SINGLE),
-            pltpu.VMEM((rows, model), HALF),
-            pltpu.VMEM((tokens, units), SINGLE),
-            pltpu.VMEM((tokens, units), HALF),
-            pltpu.SemaphoreType.DMA((3,)),
-            pltpu.SemaphoreType.DMA,
-        ]
-        + [pltpu.SemaphoreType.DMA((c,)) for c in (inner, inner, outer, outer)]
-        + PlaneGather.scratch() * 3
-        + PlaneSum.scratch(rows, model)
-        + LineGather.scratch(sum(WEIGHT_PIECES)),
-        compiler_params=kernel_params(collective_id),
-        cost_estimate=pl.CostEstimate(
-            flops=10 * tokens * model * units,
-            bytes_accessed=40 * tokens * model,
-            transcendentals=tokens * units,
-        ),
-        name="forward_pass",
-    )(lens, gains, x, cot, small, pack, out, down, gate, up)
-    return ForwardOut(*outs)
-
-
-class BackwardIn(typing.NamedTuple):
-    lens: typing.Any
-    gain: typing.Any
-    bin: typing.Any
-    ba: typing.Any
-    chan: typing.Any
-    x: typing.Any
-    cot: typing.Any
-    residual: typing.Any
-    n2_all: typing.Any
+    dt_all: typing.Any
     n1: typing.Any
     bx: typing.Any
     by: typing.Any
@@ -1390,26 +1061,19 @@
     ra: typing.Any
     h: typing.Any
     ob: typing.Any
-    hidden: typing.Any
-    d_up: typing.Any
-    d_gate: typing.Any
+    act: typing.Any
+    slope: typing.Any
     grad_down: typing.Any
-    out4: typing.Any
-    pack4: typing.Any
-    gate4: typing.Any
-    up4: typing.Any
-    down4: typing.Any
-
-
-class BackwardOut(typing.NamedTuple):
-    layer_output: typing.Any
-    grad_input: typing.Any
-    gain_grads: typing.Any
-    dt_all: typing.Any
     grad_gate: typing.Any
     grad_up: typing.Any
     grad_out: typing.Any
     grad_pack: typing.Any
+    pack4: typing.Any
+    small4: typing.Any
+    out4: typing.Any
+    gate4: typing.Any
+    up4: typing.Any
+    down4: typing.Any
     landed_down: typing.Any
     landed_gate: typing.Any
     landed_up: typing.Any
@@ -1424,6 +1088,7 @@
     sum_small: typing.Any
 
 
+WEIGHT_PIECES = (4, 1, 2, 4, 4, 6)
 SUM_PIECES = (4, 4, 4, 2, 4, 1)
 
 
@@ -1451,113 +1116,319 @@
         small[to : to + each, :width] = gchan[d * each : (d + 1) * each, :]
 
 
-def backward_pass_kernel(heads, bite, *refs):
+def layer_kernel(*refs):
     refs = list(refs)
     take = lambda n: [refs.pop(0) for _ in range(n)]
-    i = BackwardIn(*take(len(BackwardIn._fields)))
-    o = BackwardOut(*take(len(BackwardOut._fields)))
-    x, cot, residual, d_res, summed, dt_own, gain_sum = take(7)
+    i = LayerIn(*take(len(LayerIn._fields)))
+    o = LayerOut(*take(len(LayerOut._fields)))
+    tiles, gain, gain_sum, bin_low, ba_low, chan = take(6)
+    inputs, own_low, residual, d_res, summed = take(5)
     steps_scratch = take(4)
-    gin, ga, gchan, small32, small = take(5)
-    tiles, tiles_dp, tiles_mp = take(3)
-    relays, others = take(6), take(6)
-    load_sem, out_sem = take(2)
-    total_sems = take(4)
+    gin, ga, gchan, small, turns, turns_dp, turns_mp = take(7)
+    relays, others = take(6), take(3)
+    load_sem, out_sem, free_sem = take(3)
+    share_sems, total_sems = take(4), take(4)
+    plane_x = PlaneGather(i.x, o.x_all, take(3))
+    plane_c = PlaneGather(i.cot, o.c_all, take(3))
+    plane_n = PlaneGather(own_low, o.n2_all, take(3))
+    plane_t = PlaneGather(own_low, o.dt_all, take(3))
+    shared = take(10)
+    line = LineGather(
+        (o.pack4, o.small4, o.out4, o.gate4, o.up4, o.down4), WEIGHT_PIECES, take(3)
+    )
+    pack_at, small_at, out_at, gate_at, up_at, down_at = line.of
+    sources = (o.grad_down, o.grad_gate, o.grad_up, o.grad_out, o.grad_pack, small)
+    landed = (
+        o.landed_down, o.landed_gate, o.landed_up, o.landed_out, o.landed_pack, o.landed_small,
+    )
+    targets = (o.sum_down, o.sum_gate, o.sum_up, o.sum_out, o.sum_pack, o.sum_small)
+    other = [others[j] for j in (0, 0, 0, 1, 1, 2)]
+    sums = LineSum(list(zip(sources, landed, targets, SUM_PIECES, relays, other)), take(5))
     outward = [
-        pltpu.make_async_copy(dt_own, o.layer_output, out_sem.at[0]),
+        pltpu.make_async_copy(own_low, o.layer_output, out_sem.at[0]),
         pltpu.make_async_copy(d_res, o.grad_input, out_sem.at[1]),
     ]
-    plane_t = PlaneGather(dt_own, o.dt_all, take(3))
-    shared = take(10)
-    (free_sem,) = take(1)
-    sources = (i.grad_down, o.grad_gate, o.grad_up, o.grad_out, o.grad_pack, small)
-    landed = (
-        o.landed_down, o.landed_gate, o.landed_up, o.landed_out, o.landed_pack, o.landed_small,
-    )
-    targets = (o.sum_down, o.sum_gate, o.sum_up, o.sum_out, o.sum_pack, o.sum_small)
-    line = LineSum(list(zip(sources, landed, targets, SUM_PIECES, relays, others)), refs)
-    tokens, model = o.dt_all.shape
-    rows, width, units = x.shape[0], i.bx.shape[1], i.hidden.shape[1]
-    count = PlaneGather.COUNT
-    parts, _, depth = i.pack4.shape
-
-    greet(ring_peers("mp") + ring_peers("dp"))
-    line.begin(AHEAD)
+    tokens, model = o.x_all.shape
+    rows, count = i.x.shape[0], PlaneGather.COUNT
+    width, units = o.bx.shape[1], o.act.shape[1]
+    parts, _, depth = o.pack4.shape
+    heads = width // i.blocks_in.shape[1]
+    bite = i.blocks_in.shape[0] // heads
+    level, me = lax.axis_index("dp"), lax.axis_index("mp")
+
+    def copy_of(source, target, j):
+        return pltpu.make_async_copy(source, target, load_sem.at[j])
 
     def load(pairs):
-        copies = [
-            pltpu.make_async_copy(source, target, load_sem.at[j])
-            for j, (source, target) in enumerate(pairs)
-        ]
+        copies = [copy_of(source, target, j) for j, (source, target) in enumerate(pairs)]
         for copy in copies:
             copy.start()
         for copy in copies:
             copy.wait()
 
-    def mlp(d_gate, d_up, gate, up):
-        load(
-            [
-                (i.d_gate, d_gate), (i.gate4, gate), (i.d_up, d_up), (i.up4, up),
-                (i.x, x), (i.cot, cot), (i.residual, residual),
-            ]
-        )
+    def stage(w_in, w_gate, w_out, gate, up, down, pack_low, out_low, gate_low, down_low, small_own):
+        arrivals = [
+            copy_of(source, target, j)
+            for j, (source, target) in enumerate(
+                (
+                    (i.w_in, w_in), (i.w_gate, w_gate), (i.w_out, w_out), (i.gate, gate),
+                    (i.up, up), (i.down, down), (i.x, inputs),
+                )
+            )
+        ]
+        for copy in arrivals:
+            copy.start()
+        greet(ring_peers("mp") + ring_peers("dp"))
+        plane_x.start()
+        for j, ref in enumerate((w_in, w_gate)):
+            arrivals[j].wait()
+            pack_low[j * width : (j + 1) * width, :] = ref[...].astype(HALF)
+        load([(pack_low, o.pack4.at[level])])
+        line.begin(AHEAD)
+        tiles[level * count + me] = norm_tile()
+        within, across_dp = sharing(tiles, share_sems)
+        each(within, START)
+        each(within, LAND)
+        each(across_dp, START)
+        small_own[...] = jnp.zeros_like(small_own)
+        gate_rows, block = i.blocks_in.shape
+        small_own[:gate_rows, :block] = i.blocks_in[...]
+        small_own[:gate_rows, 256 : 256 + block] = i.blocks_a[...]
+        small_own[gate_rows : gate_rows + i.channels.shape[0], :width] = i.channels[...]
+        small[: small_own.shape[0], :] = small_own[...].astype(HALF)
+        arrivals[2].wait()
+        out_low[...] = w_out[...].astype(HALF)
+        load([(small.at[: small_own.shape[0]], o.small4.at[level]), (out_low, o.out4.at[level])])
+        for j, ref, low, target in (
+            (3, gate, gate_low, o.gate4), (4, up, gate_low, o.up4), (5, down, down_low, o.down4),
+        ):
+            arrivals[j].wait()
+            low[...] = ref[...].astype(HALF)
+            load([(low, target.at[level])])
+        arrivals[6].wait()
+
+    def norm_tile():
+        bits = i.norm_in.shape[1]
+        spot = me % (128 // bits) * bits
+        at_column = lax.broadcasted_iota(jnp.int32, (bits, 128), 1)
+        place = lax.broadcasted_iota(jnp.int32, (bits, 128), 0) + spot == at_column
+        both = jnp.concatenate(
+            [i.norm_in[...], i.norm_mid[...], jnp.zeros((6, bits), SINGLE)], axis=0
+        )
+        return dot_nn(both.astype(HALF), place.astype(HALF))
+
+    pl.run_scoped(
+        stage,
+        pltpu.VMEM(i.w_in.shape, SINGLE),
+        pltpu.VMEM(i.w_gate.shape, SINGLE),
+        pltpu.VMEM(i.w_out.shape, SINGLE),
+        pltpu.VMEM(i.gate.shape, SINGLE),
+        pltpu.VMEM(i.up.shape, SINGLE),
+        pltpu.VMEM(i.down.shape, SINGLE),
+        pltpu.VMEM(o.pack4.shape[1:], HALF),
+        pltpu.VMEM(o.out4.shape[1:], HALF),
+        pltpu.VMEM(o.gate4.shape[1:], HALF),
+        pltpu.VMEM(o.down4.shape[1:], HALF),
+        pltpu.VMEM(o.small4.shape[1:], SINGLE),
+    )
+    gin[...] = jnp.zeros_like(gin)
+    ga[...] = jnp.zeros_like(ga)
+    chan[...] = jnp.zeros_like(chan)
+    line.tick()
+    plane_x.level(1)
+    line.tick()
+    plane_x.level(2)
+    line.tick()
+    plane_x.finish()
+    plane_c.start()
+    within, across_dp = sharing(tiles, share_sems)
+    each(across_dp, LAND)
+    group = 128 // (model // tiles.shape[0])
+    for j in range(model // 128):
+        value = tiles[group * j]
+        for k in range(1, group):
+            value = value + tiles[group * j + k]
+        gain[:, j * 128 : (j + 1) * 128] = value
+    line.tick(2)
+    line.landed(pack_at)
+    line.landed(small_at)
+
+    part = pl.BlockSpec((rows, width), lambda t: (t, 0))
+    across = pl.BlockSpec((rows, model), lambda t: (t, 0))
+    tall = pl.BlockSpec((tokens, depth), lambda t: (0, t))
+
+    def temporal(pack, out_w, ob, small4):
+        load([(o.pack4, pack), (o.small4, small4)])
+        small_weights(small4, gin, ga, chan, heads, bite)
+        bin_low[...] = gin[...].astype(HALF)
+        ba_low[...] = ga[...].astype(HALF)
+
+        def channels(x_tile, n1, bx, by, conv, gi, ra, h, ob_tile):
+            step = pl.program_id(0)
+            schedule = {
+                2: line.tick,
+                3: lambda: plane_c.level(1),
+                4: line.tick,
+                6: lambda: plane_c.level(2),
+                7: line.tick,
+            }
+            for when, act in schedule.items():
+                pl.when(step == when)(lambda act=act: (act(), None)[1])
+            forward_step(
+                step, i.lens, x_tile, gain.at[0:1], pack, bin_low, ba_low, chan,
+                n1, bx, by, conv, gi, ra, h, ob_tile, *steps_scratch,
+            )
+            ob[pl.ds(pl.multiple_of(step * rows, rows), rows), :] = ob_tile[...]
+
+        pltpu.emit_pipeline(
+            channels,
+            grid=(count,),
+            in_specs=[across],
+            out_specs=[across] + [part] * 7,
+        )(o.x_all, o.n1, o.bx, o.by, o.conv, o.gi, o.ra, o.h, o.ob)
+        line.landed(out_at)
+        load([(o.out4, out_w)])
+        plane = PlaneSum([by_parts], depth, [ob], [out_w], shared)
+        plane.spread(line.tick)
+        line.tick()
+        plane_c.finish()
+        line.tick()
+        plane.finish(summed)
+
+    pl.run_scoped(
+        temporal,
+        pltpu.VMEM(o.pack4.shape, HALF),
+        pltpu.VMEM(o.out4.shape, HALF),
+        pltpu.VMEM((tokens, width), HALF),
+        pltpu.VMEM(o.small4.shape, HALF),
+    )
+    block = 32
+
+    def norm(t, carry):
+        at = pl.ds(pl.multiple_of(t * block, block), block)
+        value = inputs[at, :].astype(SINGLE) + summed[at, :]
+        scale = lax.rsqrt(jnp.mean(value * value, axis=-1, keepdims=True) + EPS)
+        residual[at, :] = value
+        own_low[at, :] = (value * scale * gain[1:2, :]).astype(HALF)
+        return carry
+
+    lax.fori_loop(0, rows // block, norm, 0)
+    plane_n.start()
+    line.tick(2)
+    plane_n.level(1)
+    line.tick()
+    plane_n.level(2)
+    line.tick()
+    plane_n.finish()
+    line.landed(gate_at)
+    line.landed(up_at)
+
+    def blocks(left, right):
+        value = None
+        for d in range(parts):
+            term = right(left[:, d * depth : (d + 1) * depth], d)
+            value = term if value is None else value + term
+        return value
+
+    def mlp(hidden, down, gate, up, d_up, d_gate):
+        load([(o.gate4, gate), (o.up4, up), (i.cot, own_low)])
+        thirds = [down_at[j : j + 2] for j in range(0, len(down_at), 2)]
+        third = units // len(thirds)
+        along = pl.BlockSpec((rows, units), lambda t: (t, 0))
+
+        def activations(n2, act_tile, slope_tile):
+            for when in (3, 6):
+                pl.when(pl.program_id(0) == when)(line.tick)
+            value, rise = gelu_both(blocks(n2, lambda v, d: dot_nn(v, gate[d])))
+            act_tile[...] = value
+            above = blocks(n2, lambda v, d: dot_nn(v, up[d]))
+            at = pl.ds(pl.multiple_of(pl.program_id(0) * rows, rows), rows)
+            hidden[at, :] = (value * above).astype(HALF)
+            slope_tile[...] = rise * above
+
+        pltpu.emit_pipeline(
+            activations, grid=(count,), in_specs=[across], out_specs=[along, along]
+        )(o.n2_all, o.act, o.slope)
+        beside_products([(o.c_all, hidden, o.grad_down)])
+        line.tick()
+        whole, act_part, slope_part = summed, d_res, shared[0]
+
+        for p, pieces in enumerate(thirds):
+            if p:
+                line.tick(pieces[-1] + 1 - line.done)
+            if p == len(thirds) - 1:
+                sums.begin(SUM_AHEAD)
+            span = pl.ds(p * third, third)
+            parts_in = []
+            for t in range(count):
+                at = pl.ds(t * rows, rows)
+                columns = pl.ds(t * third, third)
+                parts_in.append((o.act.at[at, span], act_part.at[:, columns]))
+                parts_in.append((o.slope.at[at, span], slope_part.at[:, columns]))
+            arrivals = [copy_of(a, b, 1 + j) for j, (a, b) in enumerate(parts_in)]
+            for copy in arrivals:
+                copy.start()
+            line.landed(pieces)
+            load([(o.down4.at[:, span], down.at[:, span])])
+            for copy in arrivals:
+                copy.wait()
+
+            def backs(c_tile):
+                d = pl.program_id(0)
+                term = dot_nt(c_tile[...], down[d, span])
+                pieces_of = [
+                    (t, slice(t * rows, (t + 1) * rows), slice(t * third, (t + 1) * third))
+                    for t in range(count)
+                ]
+
+                @pl.when(d == 0)
+                def _():
+                    for _, at, columns in pieces_of:
+                        whole[:, columns] = term[at]
+
+                @pl.when(d > 0)
+                def _():
+                    for _, at, columns in pieces_of:
+                        whole[:, columns] += term[at]
+
+                @pl.when(d == parts - 1)
+                def _():
+                    for _, at, columns in pieces_of:
+                        back = whole[:, columns]
+                        d_up[at, span] = (back * act_part[:, columns]).astype(HALF)
+                        d_gate[at, span] = (back * slope_part[:, columns]).astype(HALF)
+
+            pltpu.emit_pipeline(backs, grid=(parts,), in_specs=[tall])(o.c_all)
+
         by_rows = lambda left, right, t, columns: dot_nt(left, right[t])
         plane = PlaneSum([by_rows, by_rows], depth, [d_gate, d_up], [gate, up], shared)
-        plane.spread(line.tick)
-
-        def grads(n2_tile, gate_tile, up_tile):
-            left = n2_tile[...]
-            gate_tile[...] = dot_tn(left, d_gate[...]).astype(HALF)
-            up_tile[...] = dot_tn(left, d_up[...]).astype(HALF)
-            pl.when(pl.program_id(0) == 3)(line.tick)
-
-        out_tile = pl.BlockSpec((256, units), lambda t: (t, 0))
-        pltpu.emit_pipeline(
-            grads,
-            grid=(model // 256,),
-            in_specs=[pl.BlockSpec((tokens, 256), lambda t: (0, t))],
-            out_specs=[out_tile, out_tile],
-        )(i.n2_all, o.grad_gate, o.grad_up)
-        line.tick()
+        plane.spread(sums.tick)
+
+        beside_products([(o.n2_all, d_gate, o.grad_gate)])
+        sums.tick()
+        beside_products([(o.n2_all, d_up, o.grad_up)])
+        sums.tick()
         plane.finish(summed)
 
-    pl.run_scoped(
-        mlp,
-        pltpu.VMEM((tokens, units), HALF),
-        pltpu.VMEM((tokens, units), HALF),
-        pltpu.VMEM(i.gate4.shape, HALF),
-        pltpu.VMEM(i.up4.shape, HALF),
-    )
     gain_sum[...] = jnp.zeros_like(gain_sum)
-    block = 32
-
-    def norm_back(value, back, gain, row):
+
+    def norm_back(value, back, row):
         scale = lax.rsqrt(jnp.mean(value * value, axis=-1, keepdims=True) + EPS)
-        weighted = gain * back
+        weighted = gain[row : row + 1, :] * back
         gain_sum[row : row + 1, :] += jnp.sum(back * value * scale, axis=0, keepdims=True)
         inner = jnp.mean(weighted * value, axis=-1, keepdims=True)
         return scale * weighted - value * (scale * scale * scale * inner)
 
     def middle(t, carry):
         at = pl.ds(pl.multiple_of(t * block, block), block)
-        back = norm_back(residual[at, :], summed[at, :], i.gain[1:2, :], 1)
-        back = cot[at, :].astype(SINGLE) + back
+        back = norm_back(residual[at, :], summed[at, :], 1)
+        back = own_low[at, :].astype(SINGLE) + back
         d_res[at, :] = back
-        dt_own[at, :] = back.astype(HALF)
+        own_low[at, :] = back.astype(HALF)
         return carry
 
-    lax.fori_loop(0, rows // block, middle, 0)
-    plane_t.start()
-    line.tick(2)
-    plane_t.level(1)
-    line.tick()
-    plane_t.level(2)
-    plane_t.finish()
-
-    tall = pl.BlockSpec((tokens, depth), lambda t: (0, t))
-
     def out_gradients(ob):
-        load([(i.ob, ob)])
+        load([(o.ob, ob)])
 
         def body(dt_tile, out_tile):
             out_tile[...] = dot_tn(ob[...], dt_tile[...]).astype(HALF)
@@ -1569,55 +1440,47 @@
             out_specs=[pl.BlockSpec((width, depth), lambda t: (t, 0))],
         )(o.dt_all, o.grad_out)
 
-    pl.run_scoped(out_gradients, pltpu.VMEM((tokens, width), HALF))
-    line.tick()
-
-    def temporal(hidden, down, out_w, d_bx, d_by):
-        load([(i.hidden, hidden), (i.down4, down), (i.out4, out_w)])
+    def temporal_back(hidden, down, out_w, d_bx, d_by):
+        load([(o.out4, out_w)])
         plane = PlaneSum([by_parts], depth, [hidden], [down], shared)
 
         def channels(dt_tile, bx, by, conv, gi, ra, h, before):
             step = pl.program_id(0)
             schedule = {
                 0: lambda: (plane.send(3), plane.send(1)),
-                1: lambda: (plane.take(3), plane.send(2), line.tick()),
+                1: lambda: (plane.take(3), plane.send(2), sums.tick()),
                 2: lambda: (plane.take(1), plane.send(0)),
-                3: lambda: (plane.take(2), plane.take(0), line.tick()),
-                5: lambda: (plane.relay(), line.tick()),
-                7: line.tick,
+                3: lambda: (plane.take(2), plane.take(0), sums.tick()),
+                5: lambda: (plane.relay(), sums.tick()),
+                7: sums.tick,
             }
             for when, act in schedule.items():
                 pl.when(step == when)(lambda act=act: (act(), None)[1])
             at = pl.ds(pl.multiple_of((count - 1 - step) * rows, rows), rows)
             backward_step(
-                step, count, i.lens, dt_tile, out_w, i.bin, i.ba, i.chan,
+                step, count, i.lens, dt_tile, out_w, bin_low, ba_low, chan,
                 bx, by, conv, gi, ra, h, before, d_bx.at[at], d_by.at[at], gin, ga, gchan,
                 *steps_scratch,
             )
 
-        part = pl.BlockSpec((rows, width), lambda t: (count - 1 - t, 0))
-        across = pl.BlockSpec((rows, model), lambda t: (count - 1 - t, 0))
+        late = pl.BlockSpec((rows, width), lambda t: (count - 1 - t, 0))
+        late_across = pl.BlockSpec((rows, model), lambda t: (count - 1 - t, 0))
         ahead = pl.BlockSpec(
             (8, width), lambda t: (jnp.maximum((count - 1 - t) * (rows // 8) - 1, 0), 0)
         )
         pltpu.emit_pipeline(
-            channels, grid=(count,), in_specs=[across] + [part] * 6 + [ahead]
-        )(o.dt_all, i.bx, i.by, i.conv, i.gi, i.ra, i.h, i.h)
+            channels, grid=(count,), in_specs=[late_across] + [late] * 6 + [ahead]
+        )(o.dt_all, o.bx, o.by, o.conv, o.gi, o.ra, o.h, o.h)
         plane.finish(summed)
         for bit in plane_t.bits:
             pl.semaphore_signal(
-                free_sem,
-                inc=1,
-                device_id={"mp": flip(lax.axis_index("mp"), bit, count)},
-                device_id_type=MESH,
+                free_sem, inc=1, device_id={"mp": flip(me, bit, count)}, device_id_type=MESH
             )
-        dt_own[...] = (residual[...] + summed[...]).astype(HALF)
+        own_low[...] = (residual[...] + summed[...]).astype(HALF)
         outward[0].start()
-        small_gradients(small32, gin, ga, gchan, i.chan, heads, bite)
-        small[...] = small32[...].astype(HALF)
 
     def block_input(pack, d_bx, d_by):
-        pack_load = pltpu.make_async_copy(i.pack4, pack, load_sem.at[0])
+        pack_load = copy_of(o.pack4, pack, 0)
         pack_load.start()
 
         def body(n1_tile, pack_tile):
@@ -1630,8 +1493,8 @@
             grid=(parts,),
             in_specs=[tall],
             out_specs=[pl.BlockSpec((2 * width, depth), lambda t: (t, 0))],
-        )(i.n1, o.grad_pack)
-        line.tick()
+        )(o.n1, o.grad_pack)
+        sums.tick()
         pack_load.wait()
         plane = PlaneSum(
             [
@@ -1644,159 +1507,210 @@
             shared,
         )
         pl.semaphore_wait(free_sem, len(plane_t.bits))
-        plane.spread(line.tick)
-        line.tick()
+        plane.spread(sums.tick)
+        sums.tick()
         plane.finish(summed)
 
-    def temporal_block(d_bx, d_by):
+    def with_hidden(hidden, down):
         pl.run_scoped(
-            lambda hidden, down, out_w: temporal(hidden, down, out_w, d_bx, d_by),
+            lambda *more: mlp(hidden, down, *more),
+            pltpu.VMEM(o.gate4.shape, HALF),
+            pltpu.VMEM(o.up4.shape, HALF),
             pltpu.VMEM((tokens, units), HALF),
-            pltpu.VMEM(i.down4.shape, HALF),
-            pltpu.VMEM(i.out4.shape, HALF),
-        )
+            pltpu.VMEM((tokens, units), HALF),
+        )
+        lax.fori_loop(0, rows // block, middle, 0)
+        plane_t.start()
+        sums.tick(2)
+        plane_t.level(1)
+        sums.tick()
+        plane_t.level(2)
+        plane_t.finish()
+        pl.run_scoped(out_gradients, pltpu.VMEM((tokens, width), HALF))
+        sums.tick()
+
+        def with_gradients(d_bx, d_by):
+            pl.run_scoped(
+                lambda out_w: temporal_back(hidden, down, out_w, d_bx, d_by),
+                pltpu.VMEM(o.out4.shape, HALF),
+            )
+            pl.run_scoped(
+                lambda small32: (
+                    small_gradients(small32, gin, ga, gchan, chan, heads, bite),
+                    small.__setitem__(Ellipsis, small32[...].astype(HALF)),
+                    None,
+                )[2],
+                pltpu.VMEM(small.shape, SINGLE),
+            )
+            pl.run_scoped(
+                lambda pack: block_input(pack, d_bx, d_by), pltpu.VMEM(o.pack4.shape, HALF)
+            )
+
         pl.run_scoped(
-            lambda pack: block_input(pack, d_bx, d_by), pltpu.VMEM(i.pack4.shape, HALF)
+            with_gradients, pltpu.VMEM((tokens, width), HALF), pltpu.VMEM((tokens, width), HALF)
         )
 
     pl.run_scoped(
-        temporal_block, pltpu.VMEM((tokens, width), HALF), pltpu.VMEM((tokens, width), HALF)
-    )
-    line.tick()
+        with_hidden, pltpu.VMEM((tokens, units), HALF), pltpu.VMEM(o.down4.shape, HALF)
+    )
+    sums.tick()
 
     def last(t, carry):
         at = pl.ds(pl.multiple_of(t * block, block), block)
-        back = norm_back(x[at, :].astype(SINGLE), summed[at, :], i.gain[0:1, :], 0)
+        back = norm_back(inputs[at, :].astype(SINGLE), summed[at, :], 0)
         d_res[at, :] = d_res[at, :] + back
         return carry
 
     lax.fori_loop(0, rows // block, last, 0)
     outward[1].start()
 
-    for j in range(tiles.shape[0]):
-        tiles[j] = gain_sum[:, j * 128 : (j + 1) * 128]
+    for j in range(turns.shape[0]):
+        turns[j] = gain_sum[:, j * 128 : (j + 1) * 128]
     inner, outer = ring_peers("mp"), ring_peers("dp")
-    level, me = lax.axis_index("dp"), lax.axis_index("mp")
-    held = tiles.shape[0] // parts
-    copies = exchange(
+    held = turns.shape[0] // parts
+    early = exchange(
         outer,
-        lambda k: tiles.at[pl.ds((level + k) % parts * held, held)],
-        lambda k: tiles_dp.at[k],
+        lambda k: turns.at[pl.ds((level + k) % parts * held, held)],
+        lambda k: turns_dp.at[k],
         *total_sems[:2],
     )
-    line.tick()
+    each(early, START)
+    sums.tick()
     for j in range(3):
-        line.collect(j)
-    for copy in copies:
-        copy.wait_recv()
+        sums.collect(j)
+    each(early, LAND)
     first = level * held
     for k, _ in outer:
-        tiles_dp[0] = (tiles[pl.ds(first, held)] if k == 1 else tiles_dp[0]) + tiles_dp[k]
+        turns_dp[0] = (turns[pl.ds(first, held)] if k == 1 else turns_dp[0]) + turns_dp[k]
     pair = count // held
     late = exchange(
         inner,
-        lambda k: tiles_dp.at[0, (me + k) % count // pair],
-        lambda k: tiles_mp.at[k],
+        lambda k: turns_dp.at[0, (me + k) % count // pair],
+        lambda k: turns_mp.at[k],
         *total_sems[2:],
     )
-    line.tick(len(line.of[3]) + len(line.of[4]) - 1 - (line.done - line.of[3][0]))
-    line.collect(3)
-    for copy in late:
-        copy.wait_recv()
-    value = tiles_dp[0, me // pair]
+    each(late, START)
+    sums.tick(len(sums.of[3]) + len(sums.of[4]) - 1 - (sums.done - sums.of[3][0]))
+    sums.collect(3)
+    each(late, LAND)
+    value = turns_dp[0, me // pair]
     for k, _ in inner:
-        value = value + tiles_mp[k]
+        value = value + turns_mp[k]
     o.gain_grads[...] = value
-    line.tick(len(line.chunks) - line.done)
-    line.collect(4)
-    line.collect(5)
+    sums.tick(len(sums.chunks) - sums.done)
+    sums.collect(4)
+    sums.collect(5)
     line.settle()
-    for copy in copies + late:
-        copy.wait_send()
+    sums.settle()
+    each(within + across_dp + early + late, SENT)
     for copy in outward:
         copy.wait()
 
 
-def backward_pass(values, small_rows, heads, bite, collective_id):
+def fused_layer(values, collective_id):
     parts, count = LineSum.COUNT, PlaneGather.COUNT
     rows, model = values.x.shape
     tokens = rows * count
-    width = values.bx.shape[1]
-    units = values.hidden.shape[1]
-    depth = values.pack4.shape[2]
+    width, depth = values.w_in.shape
+    units = values.gate.shape[1]
+    small_rows = -(-(values.blocks_in.shape[0] + values.channels.shape[0]) // 16) * 16
+    shape = jax.ShapeDtypeStruct
+    plane_rows = shape((tokens, model), HALF)
+    channel = shape((tokens, width), SINGLE)
+    channel_low = shape((tokens, width), HALF)
+    hidden_wide = shape((tokens, units), SINGLE)
+    hidden_grads = shape((model, units), HALF)
     sizes = (
         (depth, units), (depth, units), (depth, units),
         (width, depth), (2 * width, depth), (small_rows, depth),
     )
-    shape = jax.ShapeDtypeStruct
-    outs = BackwardOut(
+    outs = LayerOut(
         shape((rows, model), HALF),
         shape((rows, model), SINGLE),
         shape((8, 128), SINGLE),
-        shape((tokens, model), HALF),
-        shape((model, units), HALF),
-        shape((model, units), HALF),
+        *[plane_rows] * 5,
+        channel_low,
+        *[channel] * 5,
+        channel_low,
+        hidden_wide,
+        hidden_wide,
+        hidden_grads,
+        hidden_grads,
+        hidden_grads,
         shape((parts * width, depth), HALF),
         shape((parts * 2 * width, depth), HALF),
+        shape((parts, 2 * width, depth), HALF),
+        shape((parts, small_rows, depth), HALF),
+        shape((parts, width, depth), HALF),
+        shape((parts, depth, units), HALF),
+        shape((parts, depth, units), HALF),
+        shape((parts, units, depth), HALF),
         *[shape((parts,) + size, HALF) for size in sizes],
         *[shape(size, SINGLE) for size in sizes],
     )
+    outs = outs._replace(
+        sum_down=shape((2, units, depth // 2), SINGLE), sum_pack=shape((2, width, depth), SINGLE)
+    )
     in_vmem, in_hbm = pl.BlockSpec(memory_space=pltpu.VMEM), pl.BlockSpec(memory_space=pl.ANY)
-    in_specs = BackwardIn(*[in_hbm] * len(values))._replace(
+    in_specs = LayerIn(*[in_hbm] * len(values))._replace(
         lens=pl.BlockSpec(memory_space=pltpu.SMEM),
-        gain=in_vmem,
-        bin=in_vmem,
-        ba=in_vmem,
-        chan=in_vmem,
-    )
-    out_specs = BackwardOut(*[in_hbm] * len(outs))._replace(gain_grads=in_vmem)
+        norm_in=in_vmem,
+        norm_mid=in_vmem,
+        blocks_in=in_vmem,
+        blocks_a=in_vmem,
+        channels=in_vmem,
+    )
+    out_specs = LayerOut(*[in_hbm] * len(outs))._replace(gain_grads=in_vmem)
     inner, outer = lax.axis_size("mp"), lax.axis_size("dp")
-    pieces = [
-        (count, (size[0] // count, size[1])) for size, count in zip(sizes, SUM_PIECES)
-    ]
+    pieces = [(n, (size[0] // n, size[1])) for size, n in zip(sizes, SUM_PIECES)]
     tile = (8, 128)
+    vmem, sem = pltpu.VMEM, pltpu.SemaphoreType.DMA
     results = pl.pallas_call(
-        functools.partial(backward_pass_kernel, heads, bite),
+        layer_kernel,
         out_shape=list(outs),
         in_specs=list(in_specs),
         out_specs=list(out_specs),
         scratch_shapes=[
-            pltpu.VMEM((rows, model), HALF),
-            pltpu.VMEM((rows, model), HALF),
-            pltpu.VMEM((rows, model), SINGLE),
-            pltpu.VMEM((rows, model), SINGLE),
-            pltpu.VMEM((rows, model), SINGLE),
-            pltpu.VMEM((rows, model), HALF),
-            pltpu.VMEM((8, model), SINGLE),
+            vmem((inner * outer,) + tile, SINGLE),
+            vmem((8, model), SINGLE),
+            vmem((8, model), SINGLE),
+            vmem((width, width), HALF),
+            vmem((width, width), HALF),
+            vmem((16, width), SINGLE),
+            vmem((rows, model), HALF),
+            vmem((rows, model), HALF),
+            vmem((rows, model), SINGLE),
+            vmem((rows, model), SINGLE),
+            vmem((rows, model), SINGLE),
         ]
         + forward_scratch(rows, width)
         + [
-            pltpu.VMEM((width, width), SINGLE),
-            pltpu.VMEM((width, width), SINGLE),
-            pltpu.VMEM((8, width), SINGLE),
-            pltpu.VMEM((parts * small_rows, depth), SINGLE),
-            pltpu.VMEM((parts * small_rows, depth), HALF),
-            pltpu.VMEM((model // 128,) + tile, SINGLE),
-            pltpu.VMEM((outer, model // 128 // parts) + tile, SINGLE),
-            pltpu.VMEM((inner,) + tile, SINGLE),
+            vmem((width, width), SINGLE),
+            vmem((width, width), SINGLE),
+            vmem((8, width), SINGLE),
+            vmem((parts * small_rows, depth), HALF),
+            vmem((model // 128,) + tile, SINGLE),
+            vmem((outer, model // 128 // parts) + tile, SINGLE),
+            vmem((inner,) + tile, SINGLE),
         ]
-        + [pltpu.VMEM((count,) + size, HALF) for count, size in pieces]
-        + [pltpu.VMEM(size, HALF) for _, size in pieces]
-        + [pltpu.SemaphoreType.DMA((7,)), pltpu.SemaphoreType.DMA((2,))]
-        + [pltpu.SemaphoreType.DMA((c,)) for c in (outer, outer, inner, inner)]
-        + PlaneGather.scratch()
+        + [vmem((n,) + size, HALF) for n, size in pieces]
+        + [vmem(pieces[j][1], HALF) for j in (0, 3, 5)]
+        + [sem((1 + 2 * count,)), sem((2,)), pltpu.SemaphoreType.REGULAR]
+        + [sem((c,)) for c in (inner, inner, outer, outer)]
+        + [sem((c,)) for c in (outer, outer, inner, inner)]
+        + PlaneGather.scratch() * 4
         + PlaneSum.scratch(rows, model)
-        + [pltpu.SemaphoreType.REGULAR]
+        + LineGather.scratch(sum(WEIGHT_PIECES))
         + LineSum.scratch(sum(SUM_PIECES)),
         compiler_params=kernel_params(collective_id),
         cost_estimate=pl.CostEstimate(
-            flops=14 * tokens * model * units,
-            bytes_accessed=40 * tokens * model,
-            transcendentals=tokens * units,
+            flops=24 * tokens * model * units,
+            bytes_accessed=80 * tokens * model,
+            transcendentals=2 * tokens * units,
         ),
-        name="backward_pass",
+        name="layer",
     )(*values)
-    return BackwardOut(*results)
+    return LayerOut(*results)
 
 
 def diagonal(blocks):
@@ -1829,6 +1743,7 @@
 
     fused = lax.axis_size("mp") == PlaneGather.COUNT and parts == LineGather.COUNT
     small_rows = -(-(heads * bite + 2 * CONV // parts) // 16) * 16
+    small_lanes = 512
     lane_a = 256 if fused else block
 
     def small_pack(blocks_in, blocks_a, channels):
@@ -1843,36 +1758,32 @@
         v = jnp.concatenate([v, wide(channels, small_lanes)], axis=0)
         return jnp.pad(v, ((0, small_rows - v.shape[0]), (0, 0)))
 
-    small_lanes = 512
-    small_mine = small_pack(
-        gate_in_blocks.astype(HALF), gate_a_blocks.astype(HALF), channel_params.astype(HALF)
-    )
-    mine = jnp.concatenate([w_rnn_in.astype(HALF).T, w_rnn_gate.astype(HALF).T], axis=0)
-    out_mine, down_mine = w_rnn_out.astype(HALF), w_mlp_down.astype(HALF)
-    gate_mine, up_mine = w_mlp_gate.astype(HALF), w_mlp_up.astype(HALF)
     bite_gain = norm_in.shape[0]
-    gains = jnp.stack([norm_in, norm_mid]).astype(HALF).astype(SINGLE)
     if fused:
-        group = 128 // bite_gain
-        spot = (lax.axis_index("mp") % group) * bite_gain
-        gains = lax.dynamic_update_slice(jnp.zeros((8, 128), SINGLE), gains, (0, spot))
-        o = forward_pass(
-            lengths, gains, layer_input, cotangent, small_mine, mine, out_mine,
-            down_mine, gate_mine, up_mine, heads, bite, 0,
-        )
-        known = BackwardIn(
-            lengths, o.gain, o.bin, o.ba, o.chan, layer_input, cotangent, o.residual, o.n2_all,
-            o.n1, o.bx, o.by, o.conv, o.gi, o.ra, o.h, o.ob, o.hidden, o.d_up, o.d_gate,
-            o.grad_down, o.out4, o.pack4, o.gate4, o.up4, o.down4,
-        )
-        o = backward_pass(known, small_rows, heads, bite, 1)
+        o = fused_layer(
+            LayerIn(
+                lengths, norm_in.reshape(1, -1), norm_mid.reshape(1, -1), layer_input, cotangent,
+                gate_in_blocks.reshape(-1, block), gate_a_blocks.reshape(-1, block),
+                channel_params, w_rnn_in.T, w_rnn_gate.T, w_rnn_out, w_mlp_gate, w_mlp_up, w_mlp_down,
+            ),
+            0,
+        )
+        spot = (lax.axis_index("mp") % (128 // bite_gain)) * bite_gain
         gain_grads = lax.dynamic_slice(o.gain_grads, (0, spot), (2, bite_gain))
         layer_output, grad_input = o.layer_output, o.grad_input
-        grad_in, grad_side = o.sum_pack[:width], o.sum_pack[width:]
+        grad_in, grad_side = o.sum_pack[0].T, o.sum_pack[1].T
         grad_out, small_grads = o.sum_out, o.sum_small
-        grad_gate, grad_up, grad_down = o.sum_gate, o.sum_up, o.sum_down
+        grad_gate, grad_up = o.sum_gate, o.sum_up
+        grad_down = jnp.concatenate([o.sum_down[0], o.sum_down[1]], axis=1)
     else:
         inputs = layer_input.astype(SINGLE)
+        small_mine = small_pack(
+            gate_in_blocks.astype(HALF), gate_a_blocks.astype(HALF), channel_params.astype(HALF)
+        )
+        mine = jnp.concatenate([w_rnn_in.astype(HALF).T, w_rnn_gate.astype(HALF).T], axis=0)
+        out_mine, down_mine = w_rnn_out.astype(HALF), w_mlp_down.astype(HALF)
+        gate_mine, up_mine = w_mlp_gate.astype(HALF), w_mlp_up.astype(HALF)
+        gains = jnp.stack([norm_in, norm_mid]).astype(HALF).astype(SINGLE)
         over = lambda v: lax.all_gather(v, "dp", axis=0, tiled=False)
         gains = lax.all_gather(gains, ("dp", "mp"), axis=0, tiled=False)
         gain_first = gains[:, 0].reshape(1, model)
@@ -1954,6 +1865,7 @@
         small_grads = over_dp(small_grads)[0]
         rnn_grads = over_dp(rnn_grads)[0]
         grad_in, grad_side, grad_out = jnp.split(rnn_grads, 3, axis=0)
+        grad_in, grad_side, grad_down = grad_in.T, grad_side.T, grad_down.T
         scale = lax.rsqrt(jnp.mean(inputs * inputs, axis=-1, keepdims=True) + EPS)
         weighted = gain_first * back
         gain_in = jnp.sum(back * inputs * scale, axis=0)
@@ -1971,15 +1883,15 @@
         grad_input,
         gain_grads[0],
         gain_grads[1],
-        grad_in.T,
-        grad_side.T,
+        grad_in,
+        grad_side,
         grad_out,
         gate_rows[:, :block].reshape(heads, bite, block),
         gate_rows[:, lane_a : lane_a + block].reshape(heads, bite, block),
         small_grads[heads * bite : heads * bite + 2 * CONV // parts, :width],
         grad_gate,
         grad_up,
-        grad_down.T,
+        grad_down,
     )
 
 

time: 547 us -> 512 us (0.936)
  Pallas kernels: 517 us -> 497 us
  other arithmetic: 10.4 us -> 1.34 us
    pallas_call x2 -> x1, Pallas kernels: 517 us -> 497 us  [fused_layer(): pl.pallas_call(layer_kernel, out_shape=list(outs), in_specs=list(in_specs...]
    convert_element_type x8 -> x0, other arithmetic: 7.23 us -> none  [the longest x2 2.83 us: on_device(): out_mine, down_mine = (w_rnn_out.astype(HALF), w_mlp_down.astype(HALF))]
where the time goes in v6:
time: 512 us; the launch traced here: 510 us
  Pallas kernels  497 us (97%)
  local copies, waits for them, and re-layouts  11 us (2%)
    pallas_call x1, Pallas kernels, fused_layer(): pl.pallas_call(layer_kernel, out_shape=list(outs), in_specs=list(in_specs...  497 us

profile of v6, /device:TPU:0, one launch (start us, length us, event | category | flops | bytes accessed | tf_op | source)
XLA Modules:
  0.0 509.6 jit_solution(5991969902331305482)
XLA Ops:
  0.7 496.6 %layer.1 = (bf16[256,2048]{1,0:T(8,128)(2,1)}, f32[256,2048]{1,0:T(8,128)}, f32[8,128]{1,0:T(8,128)}, bf16[2048,2048]{1,0:T(8,128)(2,1)}, bf16[2048,2048]{1,0:T(...) custom-call(s32[1,3]{1,0:T(1,128)} %refs_0_.1, ...), custom_call_target="tpu_custom_call" | custom-call | flops 77309411328 | bytes 335544320 | tf_op jit(solution)/shard_map/layer/pallas_call | solution.py:1668
  497.2 0.0 copy-start.6
  497.2 0.0 copy-start.3
  497.2 0.9 constant_dynamic-slice_fusion
  498.1 0.5 slice_bitcast_fusion.4
  498.7 2.4 slice_bitcast_fusion.2
  501.1 0.0 copy-done.6
  501.1 0.7 fusion
  501.8 0.6 slice.36
  502.3 0.0 copy-done.3
  502.3 0.0 copy-start.4
  502.3 0.1 slice_bitcast_fusion.1
  502.5 0.0 copy-start
  502.5 1.3 pad_maximum_fusion
  503.8 0.0 copy-done.4
  503.8 1.0 copy.32
  504.8 0.2 copy-done
  505.0 0.0 copy-start.5
  505.0 0.0 copy-start.2
  505.0 1.3 copy.33
  506.3 0.2 copy-done.5
  506.5 0.0 copy-start.1
  506.5 0.8 copy.34
  507.3 0.0 copy-done.2
  507.3 1.1 copy.35
  508.5 0.0 copy-done.1
  508.5 1.1 copy.36
Async XLA Ops:
  497.2 3.9 copy-start.6
  497.2 5.1 %copy-start.3 = (f32[2,768,256]{2,1,0:T(8,128)S(1)}, f32[2,768,256]{2,1,0:T(8,128)}, u32[]{:S(2)}) copy-start(f32[2,768,256]{2,1,0:T(8,128)} %get-tuple-element.30) | copy-start | bytes 4718596
  502.3 1.5 copy-start.4
  502.5 2.5 copy-start
  505.0 1.5 copy-start.5
  505.0 2.4 copy-start.2
  506.5 2.0 copy-start.1

commit v7 on v6

--- a/solution.py
+++ b/solution.py
@@ -283,12 +283,14 @@
     )
 
 
-def beside_products(pairs):
+def beside_products(pairs, when=None, act=None):
     for left, right, out in pairs:
         tokens, rows = left.shape
         tile = min(256, rows)
 
         def body(left_tile, out_tile):
+            if act is not None:
+                pl.when(pl.program_id(0) == when)(act)
             out_tile[...] = dot_tn(left_tile[...], right[...]).astype(out_tile.dtype)
 
         pltpu.emit_pipeline(
@@ -495,14 +497,19 @@
     DIRECT = ((1,), (0, 2, 3), (0, 1, 3), (2,))
     ROUND = ((0, 3, 1), (3, 0, 2))
 
-    def start(self, chunks):
+    def start(self, chunks, places=(0, 1, 2, 3)):
         for c in chunks:
             for end, block, middle in self.ROUND:
-                pl.when(self.me == end)(
-                    lambda c=c, block=block, middle=middle: self.by_middle(c, block, middle).start()
-                )
+                if end in places:
+                    pl.when(self.me == end)(
+                        lambda c=c, block=block, middle=middle: self.by_middle(
+                            c, block, middle
+                        ).start()
+                    )
             for to, senders in enumerate(self.DIRECT):
-                pl.when(self.among(senders))(lambda c=c, to=to: self.direct(c, to).start())
+                senders = [z for z in senders if z in places]
+                if senders:
+                    pl.when(self.among(senders))(lambda c=c, to=to: self.direct(c, to).start())
 
     def hand_on(self, chunks):
         for c in chunks:
@@ -520,9 +527,9 @@
                     relay[...] = value.astype(HALF)
                     self.direct(c, block, relay).start()
 
-    def begin(self, ahead):
+    def begin(self, ahead, places):
         self.ahead, self.done = ahead, 0
-        self.start(range(ahead))
+        self.start(range(ahead), places)
 
     def tick(self, count=1):
         for _ in range(count):
@@ -1078,18 +1085,18 @@
     landed_gate: typing.Any
     landed_up: typing.Any
     landed_out: typing.Any
+    landed_small: typing.Any
     landed_pack: typing.Any
-    landed_small: typing.Any
     sum_down: typing.Any
     sum_gate: typing.Any
     sum_up: typing.Any
     sum_out: typing.Any
+    sum_small: typing.Any
     sum_pack: typing.Any
-    sum_small: typing.Any
 
 
 WEIGHT_PIECES = (4, 1, 2, 4, 4, 6)
-SUM_PIECES = (4, 4, 4, 2, 4, 1)
+SUM_PIECES = (4, 4, 4, 2, 1, 4)
 
 
 def small_gradients(small, gin, ga, gchan, chan, heads, bite):
@@ -1137,12 +1144,12 @@
         (o.pack4, o.small4, o.out4, o.gate4, o.up4, o.down4), WEIGHT_PIECES, take(3)
     )
     pack_at, small_at, out_at, gate_at, up_at, down_at = line.of
-    sources = (o.grad_down, o.grad_gate, o.grad_up, o.grad_out, o.grad_pack, small)
+    sources = (o.grad_down, o.grad_gate, o.grad_up, o.grad_out, small, o.grad_pack)
     landed = (
-        o.landed_down, o.landed_gate, o.landed_up, o.landed_out, o.landed_pack, o.landed_small,
-    )
-    targets = (o.sum_down, o.sum_gate, o.sum_up, o.sum_out, o.sum_pack, o.sum_small)
-    other = [others[j] for j in (0, 0, 0, 1, 1, 2)]
+        o.landed_down, o.landed_gate, o.landed_up, o.landed_out, o.landed_small, o.landed_pack,
+    )
+    targets = (o.sum_down, o.sum_gate, o.sum_up, o.sum_out, o.sum_small, o.sum_pack)
+    other = [others[j] for j in (0, 0, 0, 1, 2, 1)]
     sums = LineSum(list(zip(sources, landed, targets, SUM_PIECES, relays, other)), take(5))
     outward = [
         pltpu.make_async_copy(own_low, o.layer_output, out_sem.at[0]),
@@ -1199,6 +1206,7 @@
         arrivals[2].wait()
         out_low[...] = w_out[...].astype(HALF)
         load([(small.at[: small_own.shape[0]], o.small4.at[level]), (out_low, o.out4.at[level])])
+        line.tick()
         for j, ref, low, target in (
             (3, gate, gate_low, o.gate4), (4, up, gate_low, o.up4), (5, down, down_low, o.down4),
         ):
@@ -1238,7 +1246,6 @@
     plane_x.level(1)
     line.tick()
     plane_x.level(2)
-    line.tick()
     plane_x.finish()
     plane_c.start()
     within, across_dp = sharing(tiles, share_sems)
@@ -1266,11 +1273,9 @@
         def channels(x_tile, n1, bx, by, conv, gi, ra, h, ob_tile):
             step = pl.program_id(0)
             schedule = {
-                2: line.tick,
-                3: lambda: plane_c.level(1),
-                4: line.tick,
-                6: lambda: plane_c.level(2),
-                7: line.tick,
+                1: line.tick,
+                3: lambda: (plane_c.level(1), line.tick()),
+                6: lambda: (plane_c.level(2), line.tick()),
             }
             for when, act in schedule.items():
                 pl.when(step == when)(lambda act=act: (act(), None)[1])
@@ -1337,7 +1342,7 @@
         along = pl.BlockSpec((rows, units), lambda t: (t, 0))
 
         def activations(n2, act_tile, slope_tile):
-            for when in (3, 6):
+            for when in (2, 4):
                 pl.when(pl.program_id(0) == when)(line.tick)
             value, rise = gelu_both(blocks(n2, lambda v, d: dot_nn(v, gate[d])))
             act_tile[...] = value
@@ -1349,15 +1354,15 @@
         pltpu.emit_pipeline(
             activations, grid=(count,), in_specs=[across], out_specs=[along, along]
         )(o.n2_all, o.act, o.slope)
-        beside_products([(o.c_all, hidden, o.grad_down)])
-        line.tick()
+        beside_products([(o.c_all, hidden, o.grad_down)], 3, line.tick)
+        sums.begin(SUM_AHEAD, (0, 3))
         whole, act_part, slope_part = summed, d_res, shared[0]
 
         for p, pieces in enumerate(thirds):
             if p:
                 line.tick(pieces[-1] + 1 - line.done)
             if p == len(thirds) - 1:
-                sums.begin(SUM_AHEAD)
+                sums.begin(SUM_AHEAD, (1, 2))
             span = pl.ds(p * third, third)
             parts_in = []
             for t in range(count):
@@ -1508,7 +1513,7 @@
         )
         pl.semaphore_wait(free_sem, len(plane_t.bits))
         plane.spread(sums.tick)
-        sums.tick()
+        sums.tick(3)
         plane.finish(summed)
 
     def with_hidden(hidden, down):
@@ -1553,7 +1558,6 @@
     pl.run_scoped(
         with_hidden, pltpu.VMEM((tokens, units), HALF), pltpu.VMEM(o.down4.shape, HALF)
     )
-    sums.tick()
 
     def last(t, carry):
         at = pl.ds(pl.multiple_of(t * block, block), block)
@@ -1590,15 +1594,15 @@
         *total_sems[2:],
     )
     each(late, START)
-    sums.tick(len(sums.of[3]) + len(sums.of[4]) - 1 - (sums.done - sums.of[3][0]))
+    sums.tick(len(sums.chunks) - 1 - sums.done)
     sums.collect(3)
+    sums.collect(4)
     each(late, LAND)
     value = turns_dp[0, me // pair]
     for k, _ in inner:
         value = value + turns_mp[k]
     o.gain_grads[...] = value
-    sums.tick(len(sums.chunks) - sums.done)
-    sums.collect(4)
+    sums.tick()
     sums.collect(5)
     line.settle()
     sums.settle()
@@ -1622,7 +1626,7 @@
     hidden_grads = shape((model, units), HALF)
     sizes = (
         (depth, units), (depth, units), (depth, units),
-        (width, depth), (2 * width, depth), (small_rows, depth),
+        (width, depth), (small_rows, depth), (2 * width, depth),
     )
     outs = LayerOut(
         shape((rows, model), HALF),
@@ -1694,7 +1698,7 @@
             vmem((inner,) + tile, SINGLE),
         ]
         + [vmem((n,) + size, HALF) for n, size in pieces]
-        + [vmem(pieces[j][1], HALF) for j in (0, 3, 5)]
+        + [vmem(pieces[j][1], HALF) for j in (0, 3, 4)]
         + [sem((1 + 2 * count,)), sem((2,)), pltpu.SemaphoreType.REGULAR]
         + [sem((c,)) for c in (inner, inner, outer, outer)]
         + [sem((c,)) for c in (outer, outer, inner, inner)]

time: 512 us -> 507 us (level)
  no operation moved by 1% of the time
where the time goes in v7:
time: 507 us; the launch traced here: 505 us
  Pallas kernels  492 us (97%)
  local copies, waits for them, and re-layouts  11 us (2%)
    pallas_call x1, Pallas kernels, fused_layer(): pl.pallas_call(layer_kernel, out_shape=list(outs), in_specs=list(in_specs...  492 us

profile of v7, /device:TPU:0, one launch (start us, length us, event | category | flops | bytes accessed | tf_op | source)
XLA Modules:
  0.0 505.3 jit_solution(17218489472792685534)
XLA Ops:
  0.7 492.3 %layer.1 = (bf16[256,2048]{1,0:T(8,128)(2,1)}, f32[256,2048]{1,0:T(8,128)}, f32[8,128]{1,0:T(8,128)}, bf16[2048,2048]{1,0:T(8,128)(2,1)}, bf16[2048,2048]{1,0:T(...) custom-call(s32[1,3]{1,0:T(1,128)} %refs_0_.1, ...), custom_call_target="tpu_custom_call" | custom-call | flops 77309411328 | bytes 335544320 | tf_op jit(solution)/shard_map/layer/pallas_call | solution.py:1672
  492.9 0.0 copy-start.6
  492.9 0.0 copy-start.3
  493.0 0.9 constant_dynamic-slice_fusion
  493.9 0.5 slice_bitcast_fusion.4
  494.4 2.4 slice_bitcast_fusion.2
  496.8 0.0 copy-done.6
  496.8 0.7 fusion
  497.5 0.6 slice.36
  498.1 0.0 copy-done.3
  498.1 0.0 copy-start.4
  498.1 0.1 slice_bitcast_fusion.1
  498.2 0.0 copy-start
  498.2 1.3 pad_maximum_fusion
  499.5 0.0 copy-done.4
  499.5 1.0 copy.32
  500.5 0.2 copy-done
  500.7 0.0 copy-start.5
  500.7 0.0 copy-start.2
  500.7 1.3 copy.33
  502.0 0.2 copy-done.5
  502.2 0.0 copy-start.1
  502.2 0.8 copy.34
  503.0 0.0 copy-done.2
  503.0 1.1 copy.35
  504.2 0.0 copy-done.1
  504.2 1.1 copy.36
Async XLA Ops:
  492.9 3.9 copy-start.6
  492.9 5.1 %copy-start.3 = (f32[2,768,256]{2,1,0:T(8,128)S(1)}, f32[2,768,256]{2,1,0:T(8,128)}, u32[]{:S(2)}) copy-start(f32[2,768,256]{2,1,0:T(8,128)} %get-tuple-element.30) | copy-start | bytes 4718596
  498.1 1.5 copy-start.4
  498.2 2.5 copy-start
  500.7 1.5 copy-start.5
  500.7 2.4 copy-start.2
  502.2 2.0 copy-start.1

commit v8 on v7

--- a/solution.py
+++ b/solution.py
@@ -1476,30 +1476,38 @@
         pltpu.emit_pipeline(
             channels, grid=(count,), in_specs=[late_across] + [late] * 6 + [ahead]
         )(o.dt_all, o.bx, o.by, o.conv, o.gi, o.ra, o.h, o.h)
-        plane.finish(summed)
+
+    def block_input(pack, d_bx, d_by):
+        pack_load = copy_of(o.pack4, pack, 0)
+        pack_load.start()
+
+        def body(n1_tile, pack_tile):
+            right = n1_tile[...]
+            pack_tile[:width, :] = dot_tn(d_bx[...], right).astype(HALF)
+            pack_tile[width:, :] = dot_tn(d_by[...], right).astype(HALF)
+
+        pltpu.emit_pipeline(
+            body,
+            grid=(parts,),
+            in_specs=[tall],
+            out_specs=[pl.BlockSpec((2 * width, depth), lambda t: (t, 0))],
+        )(o.n1, o.grad_pack)
+        pl.run_scoped(
+            lambda small32: (
+                small_gradients(small32, gin, ga, gchan, chan, heads, bite),
+                small.__setitem__(Ellipsis, small32[...].astype(HALF)),
+                None,
+            )[2],
+            pltpu.VMEM(small.shape, SINGLE),
+        )
+        sums.tick()
+        PlaneSum([], depth, [], [], shared).finish(summed)
         for bit in plane_t.bits:
             pl.semaphore_signal(
                 free_sem, inc=1, device_id={"mp": flip(me, bit, count)}, device_id_type=MESH
             )
         own_low[...] = (residual[...] + summed[...]).astype(HALF)
         outward[0].start()
-
-    def block_input(pack, d_bx, d_by):
-        pack_load = copy_of(o.pack4, pack, 0)
-        pack_load.start()
-
-        def body(n1_tile, pack_tile):
-            right = n1_tile[...]
-            pack_tile[:width, :] = dot_tn(d_bx[...], right).astype(HALF)
-            pack_tile[width:, :] = dot_tn(d_by[...], right).astype(HALF)
-
-        pltpu.emit_pipeline(
-            body,
-            grid=(parts,),
-            in_specs=[tall],
-            out_specs=[pl.BlockSpec((2 * width, depth), lambda t: (t, 0))],
-        )(o.n1, o.grad_pack)
-        sums.tick()
         pack_load.wait()
         plane = PlaneSum(
             [
@@ -1538,14 +1546,6 @@
             pl.run_scoped(
                 lambda out_w: temporal_back(hidden, down, out_w, d_bx, d_by),
                 pltpu.VMEM(o.out4.shape, HALF),
-            )
-            pl.run_scoped(
-                lambda small32: (
-                    small_gradients(small32, gin, ga, gchan, chan, heads, bite),
-                    small.__setitem__(Ellipsis, small32[...].astype(HALF)),
-                    None,
-                )[2],
-                pltpu.VMEM(small.shape, SINGLE),
             )
             pl.run_scoped(
                 lambda pack: block_input(pack, d_bx, d_by), pltpu.VMEM(o.pack4.shape, HALF)

time: 507 us -> 506 us (level)
  no operation moved by 1% of the time
where the time goes in v8:
time: 506 us; the launch traced here: 504 us
  Pallas kernels  491 us (97%)
  local copies, waits for them, and re-layouts  11 us (2%)
    pallas_call x1, Pallas kernels, fused_layer(): pl.pallas_call(layer_kernel, out_shape=list(outs), in_specs=list(in_specs...  491 us

profile of v8, /device:TPU:0, one launch (start us, length us, event | category | flops | bytes accessed | tf_op | source)
XLA Modules:
  0.0 503.6 jit_solution(9455116548540132042)
XLA Ops:
  0.7 490.5 %layer.1 = (bf16[256,2048]{1,0:T(8,128)(2,1)}, f32[256,2048]{1,0:T(8,128)}, f32[8,128]{1,0:T(8,128)}, bf16[2048,2048]{1,0:T(8,128)(2,1)}, bf16[2048,2048]{1,0:T(...) custom-call(s32[1,3]{1,0:T(1,128)} %refs_0_.1, ...), custom_call_target="tpu_custom_call" | custom-call | flops 77309411328 | bytes 335544320 | tf_op jit(solution)/shard_map/layer/pallas_call | solution.py:1672
  491.2 0.0 copy-start.6
  491.2 0.0 copy-start.3
  491.2 0.9 constant_dynamic-slice_fusion
  492.1 0.5 slice_bitcast_fusion.4
  492.6 2.4 slice_bitcast_fusion.2
  495.0 0.0 copy-done.6
  495.0 0.7 fusion
  495.7 0.6 slice.36
  496.3 0.0 copy-done.3
  496.3 0.0 copy-start.4
  496.3 0.1 slice_bitcast_fusion.1
  496.4 0.0 copy-start
  496.4 1.3 pad_maximum_fusion
  497.8 0.0 copy-done.4
  497.8 1.0 copy.32
  498.7 0.2 copy-done
  498.9 0.0 copy-start.5
  498.9 0.0 copy-start.2
  498.9 1.3 copy.33
  500.2 0.2 copy-done.5
  500.5 0.0 copy-start.1
  500.5 0.8 copy.34
  501.3 0.0 copy-done.2
  501.3 1.1 copy.35
  502.4 0.0 copy-done.1
  502.4 1.1 copy.36
Async XLA Ops:
  491.2 3.9 copy-start.6
  491.2 5.1 %copy-start.3 = (f32[2,768,256]{2,1,0:T(8,128)S(1)}, f32[2,768,256]{2,1,0:T(8,128)}, u32[]{:S(2)}) copy-start(f32[2,768,256]{2,1,0:T(8,128)} %get-tuple-element.30) | copy-start | bytes 4718596
  496.3 1.5 copy-start.4
  496.4 2.5 copy-start
  498.9 1.5 copy-start.5
  498.9 2.4 copy-start.2
  500.5 2.0 copy-start.1
